TPU v7x, 32 devices: a whole 2x2x4 slice. The times are simulated.
32 devices in a mesh: section: 2 (over x), dp: 16 (over z, y, core).
Axes of the slice: x: 2, y: 2, z: 4, core: 2. Of those that a mesh axis runs over, the one named last changes fastest.
Arguments:
- patches: bfloat16 [16384, 768], P('dp'), may hold values from -6 to 6
- targets: bfloat16 [16384, 768], P('dp'), may hold values from -6 to 6
- code_ids: int32 [16384], P('dp'), may hold values from 0 to 3199
- codebook: bfloat16 [3200, 768], P('dp'), may hold values from -6 to 6
- norm_gains: float32 [2, 2, 768], P('section'), may hold values from 0.25 to 1.75
- norm_shifts: float32 [2, 2, 768], P('section'), may hold values from -4 to 4
- w_qkv: bfloat16 [2, 768, 2304], P('section'), may hold values from -0.21875 to 0.21875
- w_out: bfloat16 [2, 768, 768], P('section'), may hold values from -0.875 to 0.875
- out_bias: float32 [2, 768], P('section'), may hold values from -4 to 4
- w_up: bfloat16 [2, 768, 3072], P('section'), may hold values from -0.21875 to 0.21875
- up_bias: float32 [2, 3072], P('section'), may hold values from -6 to 6
- w_down: bfloat16 [2, 3072, 768], P('section'), may hold values from -0.109375 to 0.109375
- down_bias: float32 [2, 768], P('section'), may hold values from -4 to 4
Outputs:
- block_out: bfloat16 [2, 16384, 768], P('section', 'dp')
- input_grad: float32 [2, 16384, 768], P('section', 'dp')
- g_norm_gains: float32 [2, 2, 768], P('section')
- g_norm_shifts: float32 [2, 2, 768], P('section')
- g_qkv: float32 [2, 768, 2304], P('section', 'dp')
- g_out: float32 [2, 768, 768], P('section', 'dp')
- g_out_bias: float32 [2, 768], P('section')
- g_up: float32 [2, 768, 3072], P('section', 'dp')
- g_up_bias: float32 [2, 3072], P('section')
- g_down: float32 [2, 3072, 768], P('section', 'dp')
- g_down_bias: float32 [2, 768], P('section')
- histogram: int32 [3200], P('dp')
- stats: float32 [3], replicated
Inputs may be any that keep to these rules, and one draw needn't show every extreme that they name: `code_ids`: each patch's chosen codebook row.
All inputs are finite; a program needn't handle non-finite values.
Results may differ from a plain program's by a relative error of at most 0.011.
Values may be sent and summed in bfloat16 or wider, within the bound.
A program may use at most 256 MiB of HBM per device.

v0:
```python
import math

import jax
import jax.numpy as jnp
from jax import lax
from jax.sharding import PartitionSpec as P

HEADS = 12
HD = 64
SEQ = 256
MICRO = 4


COMMIT_WEIGHT = 0.25
EPSILON = 1e-06
SQRT_HALF = 0.5**0.5
INV_ROOT_TAU = (2.0 * math.pi) ** (-0.5)


def from_behind(block, axis, distance):
    devices = range(lax.axis_size(axis))
    route = [(i - distance, i) for i in devices if i - distance in devices]
    return lax.ppermute(block, axis, route)


def matmul_bf(left, right):
    return jnp.dot(left, right, preferred_element_type=jnp.float32)


def matmul_tn(left, right):
    return lax.dot_general(
        left, right, (((0,), (0,)), ((), ())), preferred_element_type=jnp.float32
    )


def matmul_nt(left, right):
    return lax.dot_general(
        left, right, (((1,), (1,)), ((), ())), preferred_element_type=jnp.float32
    )


def layer_norm(rows_in):
    average = jnp.mean(rows_in, axis=-1, keepdims=True)
    centered = rows_in - average
    inv_std = lax.rsqrt(jnp.mean(centered * centered, axis=-1, keepdims=True) + EPSILON)
    return (centered * inv_std, inv_std)


def norm_back(incoming, scaled, inv_std, gain_row):
    scaled_grad = incoming * gain_row
    return inv_std * (
        scaled_grad
        - jnp.mean(scaled_grad, axis=-1, keepdims=True)
        - scaled * jnp.mean(scaled_grad * scaled, axis=-1, keepdims=True)
    )


def gelu_pair(preact):
    curve = 1.0 + lax.erf(preact * SQRT_HALF)
    slope = 0.5 * curve + preact * jnp.exp(-0.5 * preact * preact) * INV_ROOT_TAU
    return (0.5 * preact * curve, slope)


def count_shares(counts, total_count):
    shares = counts / total_count
    nonzero_share = jnp.where(counts > 0, shares, 1.0)
    return (-jnp.sum(shares * jnp.log(nonzero_share)), jnp.sum((counts > 0).astype(jnp.float32)))


def forward(rows_in, weights):
    gain_rows, shift_rows, w_qkv, w_out, out_bias, w_up, up_bias, w_down, down_bias = weights
    row_count = rows_in.shape[0]
    head_scale = HD ** (-0.5)
    scaled_one, inv_one = layer_norm(rows_in)
    normal_a = (scaled_one * gain_rows[0] + shift_rows[0]).astype(jnp.bfloat16)
    projected = (
        matmul_bf(normal_a, w_qkv).astype(jnp.bfloat16).reshape(row_count // SEQ, SEQ, 3, HEADS, HD)
    )
    queries, key_rows, value_rows = (projected[:, :, 0], projected[:, :, 1], projected[:, :, 2])
    scores = (
        jnp.einsum("bqhd,bkhd->bhqk", queries, key_rows, preferred_element_type=jnp.float32)
        * head_scale
    )
    peak_score = jnp.max(scores, axis=-1, keepdims=True)
    exponent = jnp.exp(scores - peak_score)
    denominator = jnp.sum(exponent, axis=-1, keepdims=True)
    log_total = peak_score + jnp.log(denominator)
    weights_bf = (exponent / denominator).astype(jnp.bfloat16)
    attended = jnp.einsum(
        "bhqk,bkhd->bqhd", weights_bf, value_rows, preferred_element_type=jnp.float32
    )
    attended = attended.astype(jnp.bfloat16).reshape(row_count, HEADS * HD)
    hidden_one = rows_in + matmul_bf(attended, w_out) + out_bias
    scaled_two, inv_two = layer_norm(hidden_one)
    normal_b = (scaled_two * gain_rows[1] + shift_rows[1]).astype(jnp.bfloat16)
    preact = matmul_bf(normal_b, w_up) + up_bias
    activated = gelu_pair(preact)[0].astype(jnp.bfloat16)
    result = hidden_one + matmul_bf(activated, w_down) + down_bias
    stored = (
        scaled_one,
        inv_one,
        normal_a,
        projected,
        log_total,
        attended,
        scaled_two,
        inv_two,
        normal_b,
        preact,
        activated,
    )
    return (result, stored)


def backward(cotangent, stored, weights):
    (
        scaled_one,
        inv_one,
        normal_a,
        projected,
        log_total,
        attended,
        scaled_two,
        inv_two,
        normal_b,
        preact,
        activated,
    ) = stored
    gain_rows, shift_rows, w_qkv, w_out, out_bias, w_up, up_bias, w_down, down_bias = weights
    row_count = cotangent.shape[0]
    head_scale = HD ** (-0.5)
    grad_down_bias = jnp.sum(cotangent, axis=0)
    cot_bf = cotangent.astype(jnp.bfloat16)
    grad_down = matmul_tn(activated, cot_bf)
    grad_act = matmul_nt(cot_bf, w_down)
    grad_pre = (grad_act * gelu_pair(preact)[1]).astype(jnp.bfloat16)
    grad_up_bias = jnp.sum(grad_pre.astype(jnp.float32), axis=0)
    grad_up = matmul_tn(normal_b, grad_pre)
    grad_normb = matmul_nt(grad_pre, w_up)
    gain_two = jnp.sum(grad_normb * scaled_two, axis=0)
    shift_two = jnp.sum(grad_normb, axis=0)
    grad_hidden = cotangent + norm_back(grad_normb, scaled_two, inv_two, gain_rows[1])
    grad_out_bias = jnp.sum(grad_hidden, axis=0)
    hidden_bf = grad_hidden.astype(jnp.bfloat16)
    grad_out = matmul_tn(attended, hidden_bf)
    grad_att = (
        matmul_nt(hidden_bf, w_out).astype(jnp.bfloat16).reshape(row_count // SEQ, SEQ, HEADS, HD)
    )
    queries, key_rows, value_rows = (projected[:, :, 0], projected[:, :, 1], projected[:, :, 2])
    scores = (
        jnp.einsum("bqhd,bkhd->bhqk", queries, key_rows, preferred_element_type=jnp.float32)
        * head_scale
    )
    shares = jnp.exp(scores - log_total)
    grad_value = jnp.einsum(
        "bhqk,bqhd->bkhd", shares.astype(jnp.bfloat16), grad_att, preferred_element_type=jnp.float32
    )
    grad_shares = jnp.einsum(
        "bqhd,bkhd->bhqk", grad_att, value_rows, preferred_element_type=jnp.float32
    )
    row_dot = jnp.sum(grad_shares * shares, axis=-1, keepdims=True)
    grad_scores = (shares * (grad_shares - row_dot)).astype(jnp.bfloat16)
    grad_query = (
        jnp.einsum("bhqk,bkhd->bqhd", grad_scores, key_rows, preferred_element_type=jnp.float32)
        * head_scale
    )
    grad_key = (
        jnp.einsum("bhqk,bqhd->bkhd", grad_scores, queries, preferred_element_type=jnp.float32)
        * head_scale
    )
    grad_proj = (
        jnp.stack([grad_query, grad_key, grad_value], axis=2)
        .reshape(row_count, 3 * HEADS * HD)
        .astype(jnp.bfloat16)
    )
    grad_qkv = matmul_tn(normal_a, grad_proj)
    grad_norma = matmul_nt(grad_proj, w_qkv)
    gain_one = jnp.sum(grad_norma * scaled_one, axis=0)
    shift_one = jnp.sum(grad_norma, axis=0)
    grad_input = grad_hidden + norm_back(grad_norma, scaled_one, inv_one, gain_rows[0])
    matrices = (grad_qkv, grad_out, grad_up, grad_down)
    vectors = (
        jnp.stack([gain_one, gain_two]),
        jnp.stack([shift_one, shift_two]),
        grad_out_bias,
        grad_up_bias,
        grad_down_bias,
    )
    return (grad_input, matrices, vectors)


def on_device(
    patches,
    targets,
    code_ids,
    codebook,
    norm_gains,
    norm_shifts,
    w_qkv,
    w_out,
    out_bias,
    w_up,
    up_bias,
    w_down,
    down_bias,
):
    leading = lax.axis_index("section") == 0
    weights = tuple(
        (
            param[0]
            for param in (
                norm_gains,
                norm_shifts,
                w_qkv,
                w_out,
                out_bias,
                w_up,
                up_bias,
                w_down,
                down_bias,
            )
        )
    )
    tokens_here = patches.shape[0]
    block_rows = tokens_here // MICRO
    width = patches.shape[1]
    vocab_local = codebook.shape[0]
    vocab_all = vocab_local * lax.axis_size("dp")
    total_tokens = tokens_here * lax.axis_size("dp")
    shard_rows = lax.all_gather(codebook, "dp", axis=0, tiled=True)
    shard_len = shard_rows.shape[0]
    inside = (code_ids >= 0) & (code_ids < shard_len)
    picked = jnp.take(shard_rows, jnp.clip(code_ids, 0, shard_len - 1), axis=0).astype(jnp.float32)
    chosen = jnp.where(inside[:, None], picked, jnp.zeros((tokens_here, width), jnp.float32))
    chosen_bf = chosen.astype(jnp.bfloat16)
    vocab_iota = lax.broadcasted_iota(jnp.int32, (1, vocab_all), 1)
    counts = jnp.zeros((vocab_all,), jnp.float32)
    for block_index in range(MICRO):
        id_rows = code_ids[block_index * block_rows : (block_index + 1) * block_rows]
        counts = counts + jnp.sum((id_rows[:, None] == vocab_iota).astype(jnp.float32), axis=0)
    results = []
    stores = []
    for moment in range(MICRO + 1):
        current = min(moment, MICRO - 1)
        previous = max(moment - 1, 0)
        own_rows = patches[current * block_rows : (current + 1) * block_rows].astype(jnp.float32)
        arrived = chosen_bf[previous * block_rows : (previous + 1) * block_rows]
        inputs = jnp.where(leading, own_rows, arrived.astype(jnp.float32))
        result, stored = forward(inputs, weights)
        results.append(result)
        stores.append(stored)
    loss_part = jnp.zeros((), jnp.float32)
    for block_index in range(MICRO):
        code_rows = chosen[block_index * block_rows : (block_index + 1) * block_rows]
        target_rows = targets[block_index * block_rows : (block_index + 1) * block_rows].astype(
            jnp.float32
        )
        commit_sum = COMMIT_WEIGHT * jnp.sum((results[block_index] - code_rows) ** 2)
        recon_sum = jnp.sum((results[block_index + 1] - target_rows) ** 2)
        loss_part = loss_part + jnp.where(leading, commit_sum, recon_sum)
    gradients = []
    matrix_total = None
    vector_total = None
    outgoing_grad = jnp.zeros((block_rows, width), jnp.bfloat16)
    for moment in range(MICRO + 1):
        earlier = MICRO - moment
        enc_block = min(earlier, MICRO - 1)
        dec_block = max(earlier - 1, 0)
        produced = results[earlier]
        if moment > 0:
            arrived_grad = from_behind(outgoing_grad, "section", -1)
        else:
            arrived_grad = jnp.zeros((block_rows, width), jnp.bfloat16)
        enc_cot = arrived_grad.astype(jnp.float32) + COMMIT_WEIGHT * (
            produced - chosen[enc_block * block_rows : (enc_block + 1) * block_rows]
        )
        dec_cot = produced - targets[dec_block * block_rows : (dec_block + 1) * block_rows].astype(
            jnp.float32
        )
        cotangent = jnp.where(leading, enc_cot, dec_cot)
        grad_input, matrices, vectors = backward(cotangent, stores[earlier], weights)
        active = jnp.where(
            leading, 1.0 if moment >= 1 else 0.0, 1.0 if moment < MICRO else 0.0
        ).astype(jnp.float32)
        matrices = tuple((active * piece for piece in matrices))
        vectors = tuple((active * piece for piece in vectors))
        if matrix_total is None:
            matrix_total, vector_total = (matrices, vectors)
        else:
            matrix_total = tuple((left + right for left, right in zip(matrix_total, matrices)))
            vector_total = tuple((left + right for left, right in zip(vector_total, vectors)))
        gradients.append(grad_input)
        outgoing_grad = grad_input.astype(jnp.bfloat16)
    grad_qkv, grad_out, grad_up, grad_down = (
        lax.psum_scatter(matrix_total[0][None], "dp", scatter_dimension=1, tiled=True),
        lax.psum_scatter(matrix_total[1][None], "dp", scatter_dimension=1, tiled=True),
        lax.psum_scatter(matrix_total[2][None], "dp", scatter_dimension=1, tiled=True),
        lax.psum_scatter(matrix_total[3][None], "dp", scatter_dimension=1, tiled=True),
    )
    gain_grad, shift_grad, out_bias_grad, up_bias_grad, down_bias_grad = lax.psum(
        (vector_total[0], vector_total[1], vector_total[2], vector_total[3], vector_total[4]), "dp"
    )
    hist_local = lax.psum_scatter(counts, "dp", scatter_dimension=0, tiled=True)
    entropy_part, used_part = count_shares(hist_local, total_tokens)
    loss_all, entropy_all, used_all = lax.psum(
        (loss_part, jnp.where(leading, entropy_part, 0.0), jnp.where(leading, used_part, 0.0)),
        ("section", "dp"),
    )
    block_out = jnp.concatenate(
        [jnp.where(leading, results[index], results[index + 1]) for index in range(MICRO)], axis=0
    )
    input_grad = jnp.concatenate(
        [
            jnp.where(leading, gradients[MICRO - index], gradients[MICRO - 1 - index])
            for index in range(MICRO)
        ],
        axis=0,
    )
    stats = jnp.stack(
        [loss_all / (total_tokens * width), used_all / vocab_all, jnp.exp(entropy_all) / vocab_all]
    )
    return (
        block_out.astype(jnp.bfloat16)[None],
        input_grad[None],
        gain_grad[None],
        shift_grad[None],
        grad_qkv,
        grad_out,
        out_bias_grad[None],
        grad_up,
        up_bias_grad[None],
        grad_down,
        down_bias_grad[None],
        hist_local.astype(jnp.int32),
        stats,
    )


def solution(mesh):
    return jax.shard_map(
        on_device,
        mesh=mesh,
        in_specs=(
            P("dp", None),
            P("dp", None),
            P("dp"),
            P("dp", None),
            P("section", None, None),
            P("section", None, None),
            P("section", None, None),
            P("section", None, None),
            P("section", None),
            P("section", None, None),
            P("section", None),
            P("section", None, None),
            P("section", None),
        ),
        out_specs=(
            P("section", "dp", None),
            P("section", "dp", None),
            P("section", None, None),
            P("section", None, None),
            P("section", "dp", None),
            P("section", "dp", None),
            P("section", None),
            P("section", "dp", None),
            P("section", None),
            P("section", "dp", None),
            P("section", None),
            P("dp"),
            P(),
        ),
        check_vma=False,
    )
```

profile of v0, /device:TPU:0, one launch (start us, length us, event | category | flops | bytes accessed | tf_op | source)
XLA Modules:
  0.0 727.6 jit_solution(8166993076057065564)
XLA Ops:
  14.2 53.2 %all-gather.2.cloned.1.call-done = bf16[3200,768]{1,0:T(8,128)(2,1)} async-done(((bf16[200,768]{1,0:T(8,128)(2,1)}), bf16[3200,768]{1,0:T(8,128)(2,1)}) %all-gather.2.cloned.1.call-update) | async-done | bytes 4915216 | tf_op jit(solution)/shard_map/all_gather | solution.py:230
  67.4 8.8 %gather_fusion = bf16[1024,768]{1,0:T(8,128)(2,1)} fusion(bf16[3200,768]{1,0:T(8,128)(2,1)} %all-gather.2.cloned.1.call-done, s32[1024]{0:T(1024)} %fusion.292), kind=kCustom, calls=%fused_computation | custom fusion | bytes 3149824 | tf_op jit(solution)/shard_map/jit(_take)/gather | solution.py:233
  97.2 4.3 fusion.308
  139.0 12.9 %copy.135 = bf16[256,2304]{0,1:T(8,128)(2,1)} copy(bf16[256,2304]{1,0:T(8,128)(2,1)} %convolution_convert_fusion.2) | data formatting | bytes 2359296 | tf_op jit(solution)/shard_map/convert_element_type | solution.py:77
  180.8 3.8 multiply_convert_fusion.7
  184.6 4.3 fusion.281
  188.9 4.3 fusion.309
  230.0 4.0 multiply_convert_fusion.8
  234.1 4.3 fusion.280
  241.0 4.4 fusion.310
  268.7 4.1 fusion.279
  272.8 6.7 collective-permute-done.2
  279.6 4.4 fusion.311
  308.6 8.7 %collective-permute-done.3 = bf16[256,768]{1,0:T(8,128)(2,1)S(1)} collective-permute-done((bf16[256,768]{1,0:T(8,128)(2,1)S(1)}, bf16[256,768]{1,0:T(8,128)(2,1)S(1)}, u32[]{:S(2)}, u32[]{:S(2)}) %collective-permute-start.3) | collective-permute-done | bytes 393248 | tf_op jit(solution)/shard_map/ppermute | solution.py:23
  317.4 6.8 multiply_reduce_fusion.10
  333.7 5.8 fusion.278
  350.7 10.6 %add_bitcast_fusion.2 = f32[1,768,2304]{2,1,0:T(8,128)} fusion(f32[768,2304]{1,0:T(8,128)} %fusion.278, f32[768,2304]{1,0:T(8,128)} %fusion.279, f32[768,2304]{1,0:T(8,128)} %fusion.280, f32[768,2304]{1,0:T(8,128)S(1)} %bitcast.499, bf16[256,2304]{0,1:T(8,128)(2,1)S(1)} %bitcast.525, f32[]{:T(128)S(6)} %select_n.146, f32[]{:T(128)S(6)} %select_n.145, ...), kind=kOutput, calls=%fused_computation.3 | convolution fusion | flops 918159360 | bytes 37363720 | tf_op jit(solution)/shard_map/dot_general | solution.py:31
  361.9 7.0 fusion.306
  369.0 5.2 fusion.305
  374.3 5.3 fusion.304
  379.6 5.2 fusion.303
  384.9 17.4 %add_bitcast_fusion.1 = f32[1,768,3072]{2,1,0:T(8,128)} fusion(f32[768,3072]{1,0:T(8,128)} %fusion.303, f32[768,3072]{1,0:T(8,128)} %fusion.304, f32[768,3072]{1,0:T(8,128)} %fusion.305, f32[768,3072]{1,0:T(8,128)} %fusion.306, bf16[256,3072]{1,0:T(8,128)(2,1)S(1)} %copy-done.96, f32[]{:T(128)S(6)} %select_n.146, f32[]{:T(128)S(6)} %select_n.145, ...), kind=kOutput, calls=%fused_computation.2 | convolution fusion | flops 1223098368 | bytes 49553416 | tf_op jit(solution)/shard_map/dot_general | solution.py:31
  402.6 7.5 %fusion.275 = f32[3072,768]{1,0:T(8,128)} fusion(bf16[256,3072]{1,0:T(8,128)(2,1)} %copy-done.88, f32[256,768]{1,0:T(8,128)} %copy-done.74), kind=kOutput, calls=%fused_computation.424 | convolution fusion | flops 1208156160 | bytes 11796480 | tf_op jit(solution)/shard_map/dot_general | solution.py:31
  410.2 5.5 fusion.269
  415.7 5.2 fusion.263
  420.8 5.1 fusion.257
  425.9 19.0 %add_bitcast_fusion = f32[1,3072,768]{2,1,0:T(8,128)} fusion(f32[3072,768]{1,0:T(8,128)} %fusion.257, f32[3072,768]{1,0:T(8,128)} %fusion.263, f32[3072,768]{1,0:T(8,128)} %fusion.269, f32[3072,768]{1,0:T(8,128)} %fusion.275, f32[]{:T(128)S(6)} %select_n.146, f32[]{:T(128)S(6)} %select_n.145, f32[256,768]{1,0:T(8,128)S(1)} %copy-done.87, f32[256,3072]{1,0:T(8,128)} %fusion.55), kind=kOutput, calls=%fused_computation.1 | convolution fusion | flops 1226244096 | bytes 51118088 | tf_op jit(solution)/shard_map/dot_general | solution.py:31
  475.7 4.2 multiply_reduce_fusion.19
  481.4 60.2 %all-reduce.2 = (f32[1,2,768]{2,1,0:T(2,128)}, f32[1,2,768]{2,1,0:T(2,128)}, f32[1,768]{1,0:T(1,128)}, f32[1,3072]{1,0:T(1,128)}, f32[1,768]{1,0:T(1,128)}, /*index=5*/f32[3200]{0:T(1024)}) all-reduce(f32[1,2,768]{2,1,0:T(2,128)S(1)} %fusion.291, f32[1,2,768]{2,1,0:T(2,128)} %fusion.290, ...), channel_id=1, replica_groups=mesh['section'=2,'dp'=16] {'dp'}, use_global_device_ids=true, to_apply=%region_65.66 | all-reduce | flops 10880 | bytes 87040 | tf_op jit(solution)/shard_map/psum | solution.py:300
  547.3 38.9 %all-reduce.1 = (f32[]{:T(128)}, f32[]{:T(128)}, f32[]{:T(128)}) all-reduce(f32[]{:T(128)S(6)} %select_n.153, f32[]{:T(128)S(6)} %select_n.151, f32[]{:T(128)S(6)} %add.682), channel_id=1, replica_groups=mesh['section'=2,'dp'=16] {'section','dp'}, use_global_device_ids=true, to_apply=%region_116.117 | all-reduce | flops 3 | bytes 24 | tf_op jit(solution)/shard_map/psum | solution.py:305
  595.8 8.8 %reduce-scatter.9.cloned.1.call-done = f32[1,48,3072]{2,1,0:T(8,128)} async-done(((f32[1,768,3072]{2,1,0:T(8,128)}), f32[1,48,3072]{2,1,0:T(8,128)}) %reduce-scatter.9.cloned.1.call-update) | async-done | bytes 589840 | tf_op jit(solution)/shard_map/reduce_scatter | solution.py:297
  604.6 116.2 %reduce-scatter.11.cloned.1.call-done = f32[1,192,768]{2,1,0:T(8,128)} async-done(((f32[1,3072,768]{2,1,0:T(8,128)}), f32[1,192,768]{2,1,0:T(8,128)}) %reduce-scatter.11.cloned.1.call-update) | async-done | bytes 589840 | tf_op jit(solution)/shard_map/reduce_scatter | solution.py:298
  (714 shorter events, 240.0 us)
Async XLA Ops:
  7.2 74.9 %copy-start = (bf16[1,768,2304]{2,1,0:T(8,128)(2,1)S(1)}, bf16[1,768,2304]{2,1,0:T(8,128)(2,1)}, u32[]{:S(2)}) copy-start(bf16[1,768,2304]{2,1,0:T(8,128)(2,1)} %param.19) | copy-start | bytes 10616836
  7.2 60.2 %all-gather.2.cloned.1.call-start = ((), (), s32[]{:S(2)}) async-start(), calls=%async_computation.4 | async-start | bytes 5222400 | tf_op jit(solution)/shard_map/all_gather | solution.py:230
  7.9 587.9 %reduce-scatter.7.cloned.1.call-start = ((), (), s32[]{:S(2)}) async-start(), calls=%async_computation.6 | async-start | bytes 2506752 | tf_op jit(solution)/shard_map/reduce_scatter | solution.py:296
  94.6 12.1 %copy-start.51 = (f32[256,768]{1,0:T(8,128)}, f32[256,768]{1,0:T(8,128)S(1)}, u32[]{:S(2)}) copy-start(f32[256,768]{1,0:T(8,128)S(1)} %get-tuple-element.139) | copy-start | bytes 2359300
  94.6 12.1 %copy-start.124 = (f32[256]{0:T(256)}, f32[256]{0:T(256)S(1)}, u32[]{:S(2)}) copy-start(f32[256]{0:T(256)S(1)} %broadcast_multiply_fusion.20) | copy-start | bytes 3076
  94.9 11.9 %copy-start.146 = (f32[256]{0:T(256)}, f32[256]{0:T(256)S(1)}, u32[]{:S(2)}) copy-start(f32[256]{0:T(256)S(1)} %add_rsqrt_fusion) | copy-start | bytes 3076
  171.7 17.1 %collective-permute-start = (bf16[256,768]{1,0:T(8,128)(2,1)S(1)}, bf16[256,768]{1,0:T(8,128)(2,1)S(1)}, u32[]{:S(2)}, u32[]{:S(2)}) collective-permute-start(bf16[256,768]{1,0:T(8,128)(2,1)S(1)} %copy-done.117), channel_id=1, source_target_pairs={{16,0},{17,1},{18,2},{19,3},{20,4},{21,5},{22,6},{23,7},{24,8},{25... | collective-permute-start | bytes 1179656 | tf_op jit(solution)/shard_map/ppermute | solution.py:23
  178.6 19.7 %copy-start.58 = (f32[256,768]{1,0:T(8,128)}, f32[256,768]{1,0:T(8,128)S(1)}, u32[]{:S(2)}) copy-start(f32[256,768]{1,0:T(8,128)S(1)} %get-tuple-element.154) | copy-start | bytes 2359300
  178.6 19.7 %copy-start.129 = (f32[256]{0:T(256)}, f32[256]{0:T(256)S(1)}, u32[]{:S(2)}) copy-start(f32[256]{0:T(256)S(1)} %broadcast_multiply_fusion.22) | copy-start | bytes 3076
  178.8 19.5 %copy-start.150 = (f32[256]{0:T(256)}, f32[256]{0:T(256)S(1)}, u32[]{:S(2)}) copy-start(f32[256]{0:T(256)S(1)} %add_rsqrt_fusion.2) | copy-start | bytes 3076
  227.8 13.2 %collective-permute-start.1 = (bf16[256,768]{1,0:T(8,128)(2,1)S(1)}, bf16[256,768]{1,0:T(8,128)(2,1)S(1)}, u32[]{:S(2)}, u32[]{:S(2)}) collective-permute-start(bf16[256,768]{1,0:T(8,128)(2,1)S(1)} %get-tuple-element.111), channel_id=1, source_target_pairs={{16,0},{17,1},{18,2},{19,3},{20,4},{21,5},{22,6},{23,7},{24,8},{25... | collective-permute-start | bytes 1179656 | tf_op jit(solution)/shard_map/ppermute | solution.py:23
  266.9 12.7 %slice-start.8 = ((s8[4718592]{0:T(1024)(128)(4,1)}), s8[4194304]{0:T(1024)(128)(4,1)S(1)}, s32[]{:S(2)}) async-start(s8[4718592]{0:T(1024)(128)(4,1)} %bitcast.562), calls=%async_computation.17 | async-start | bytes 8388608
  266.9 12.7 %copy-start.61 = (f32[256,768]{1,0:T(8,128)S(1)}, f32[256,768]{1,0:T(8,128)}, u32[]{:S(2)}) copy-start(f32[256,768]{1,0:T(8,128)} %copy-done.60) | copy-start | bytes 2359300
  266.9 12.7 %copy-start.93 = (bf16[256,3072]{1,0:T(8,128)(2,1)S(1)}, bf16[256,3072]{1,0:T(8,128)(2,1)}, u32[]{:S(2)}) copy-start(bf16[256,3072]{1,0:T(8,128)(2,1)} %get-tuple-element.166) | copy-start | bytes 4718596
  266.9 12.7 %copy-start.204 = (f32[768]{0:T(1024)S(1)}, f32[768]{0:T(1024)}, u32[]{:S(2)}) copy-start(f32[768]{0:T(1024)} %reduce.35) | copy-start | bytes 9220
  266.9 12.7 %slice-start.9 = ((s8[4718592]{0:T(1024)(128)(4,1)}), s8[524288]{0:T(1024)(128)(4,1)S(1)}, s32[]{:S(2)}) async-start(s8[4718592]{0:T(1024)(128)(4,1)} %bitcast.562), calls=%async_computation.18 | async-start | bytes 1048576
  266.9 12.6 %collective-permute-start.2 = (bf16[256,768]{1,0:T(8,128)(2,1)S(1)}, bf16[256,768]{1,0:T(8,128)(2,1)S(1)}, u32[]{:S(2)}, u32[]{:S(2)}) collective-permute-start(bf16[256,768]{1,0:T(8,128)(2,1)S(1)} %get-tuple-element.109), channel_id=1, source_target_pairs={{16,0},{17,1},{18,2},{19,3},{20,4},{21,5},{22,6},{23,7},{24,8},{25... | collective-permute-start | bytes 1179656 | tf_op jit(solution)/shard_map/ppermute | solution.py:23
  300.4 16.9 %slice-start.10 = ((s8[4718592]{0:T(1024)(128)(4,1)}), s8[4194304]{0:T(1024)(128)(4,1)S(1)}, s32[]{:S(2)}) async-start(s8[4718592]{0:T(1024)(128)(4,1)} %bitcast.564), calls=%async_computation.19 | async-start | bytes 8388608
  302.3 15.0 %slice-start.11 = ((s8[4718592]{0:T(1024)(128)(4,1)}), s8[524288]{0:T(1024)(128)(4,1)S(1)}, s32[]{:S(2)}) async-start(s8[4718592]{0:T(1024)(128)(4,1)} %bitcast.564), calls=%async_computation.20 | async-start | bytes 1048576
  305.6 11.8 %copy-start.81 = (f32[256,3072]{1,0:T(8,128)S(1)}, f32[256,3072]{1,0:T(8,128)}, u32[]{:S(2)}) copy-start(f32[256,3072]{1,0:T(8,128)} %fusion.55) | copy-start | bytes 9437188
  305.6 11.8 %copy-start.105 = (f32[256,768]{1,0:T(8,128)S(1)}, f32[256,768]{1,0:T(8,128)}, u32[]{:S(2)}) copy-start(f32[256,768]{1,0:T(8,128)} %get-tuple-element.142) | copy-start | bytes 2359300
  305.6 11.8 %copy-start.106 = (f32[256,768]{1,0:T(8,128)S(1)}, f32[256,768]{1,0:T(8,128)}, u32[]{:S(2)}) copy-start(f32[256,768]{1,0:T(8,128)} %get-tuple-element.157) | copy-start | bytes 2359300
  305.6 11.8 %copy-start.107 = (f32[256,768]{1,0:T(8,128)S(1)}, f32[256,768]{1,0:T(8,128)}, u32[]{:S(2)}) copy-start(f32[256,768]{1,0:T(8,128)} %get-tuple-element.174) | copy-start | bytes 2359300
  305.6 11.8 %copy-start.108 = (f32[256,768]{1,0:T(8,128)S(1)}, f32[256,768]{1,0:T(8,128)}, u32[]{:S(2)}) copy-start(f32[256,768]{1,0:T(8,128)} %get-tuple-element.179) | copy-start | bytes 2359300
  305.6 11.8 %copy-start.205 = (f32[768]{0:T(1024)S(1)}, f32[768]{0:T(1024)}, u32[]{:S(2)}) copy-start(f32[768]{0:T(1024)} %reduce.35) | copy-start | bytes 9220
  305.6 11.7 %collective-permute-start.3 = (bf16[256,768]{1,0:T(8,128)(2,1)S(1)}, bf16[256,768]{1,0:T(8,128)(2,1)S(1)}, u32[]{:S(2)}, u32[]{:S(2)}) collective-permute-start(bf16[256,768]{1,0:T(8,128)(2,1)S(1)} %get-tuple-element.107), channel_id=1, source_target_pairs={{16,0},{17,1},{18,2},{19,3},{20,4},{21,5},{22,6},{23,7},{24,8},{25... | collective-permute-start | bytes 1179656 | tf_op jit(solution)/shard_map/ppermute | solution.py:23
  307.6 19.6 %slice-start.20 = ((s8[4718592]{0:T(1024)(128)(4,1)}), s8[4194304]{0:T(1024)(128)(4,1)S(1)}, s32[]{:S(2)}) async-start(s8[4718592]{0:T(1024)(128)(4,1)} %bitcast.574), calls=%async_computation.29 | async-start | bytes 8388608
  333.6 262.2 %reduce-scatter.5.cloned.1.call-start = ((), (), s32[]{:S(2)}) async-start(), calls=%async_computation.5 | async-start | bytes 7520256 | tf_op jit(solution)/shard_map/reduce_scatter | solution.py:295
  361.2 243.3 %reduce-scatter.9.cloned.1.call-start = ((), (), s32[]{:S(2)}) async-start(), calls=%async_computation.7 | async-start | bytes 10027008 | tf_op jit(solution)/shard_map/reduce_scatter | solution.py:297
  402.3 318.4 %reduce-scatter.11.cloned.1.call-start = ((), (), s32[]{:S(2)}) async-start(), calls=%async_computation.8 | async-start | bytes 10027008 | tf_op jit(solution)/shard_map/reduce_scatter | solution.py:298
  444.9 28.6 %copy-start.144 = (f32[768]{0:T(1024)S(1)}, f32[768]{0:T(1024)}, u32[]{:S(2)}) copy-start(f32[768]{0:T(1024)} %get-tuple-element.97) | copy-start | bytes 9220
  444.9 28.6 %copy-start.145 = (f32[768]{0:T(1024)S(1)}, f32[768]{0:T(1024)}, u32[]{:S(2)}) copy-start(f32[768]{0:T(1024)} %get-tuple-element.99) | copy-start | bytes 9220
  (222 other events, 813.7 us)
Sparse Core Ops, SparseCore 0:
  10.2 57.1 all-gather.1
  333.7 60.5 reduce-scatter.6
  399.5 89.0 reduce-scatter.4
  493.1 111.4 reduce-scatter.8
  609.7 111.0 reduce-scatter.10
where the time goes:
time: 732 us; the launch traced here: 728 us
  matrix products  270 us (37%)
  waiting for transfers between devices  197 us (27%)
  blocking collectives  99.1 us (14%)
  local copies, waits for them, and re-layouts  80.3 us (11%)
  other arithmetic  48.8 us (7%)
  between operations  25.2 us (3%)
    dot_general x20, matrix products, matmul_tn(): lax.dot_general(left, right, (((0,), (0,)), ((), ())), preferred_element_...  119 us
    reduce_scatter x1, waiting for transfers between devices, on_device(): lax.psum_scatter(matrix_total[3][None], 'dp', scatter_dimension=1, tiled=...  116 us
    psum x1, blocking collectives, on_device(): lax.psum((vector_total[0], vector_total[1], vector_total[2], vector_total...  60.2 us
    dot_general x20, matrix products, matmul_bf(): return jnp.dot(left, right, preferred_element_type=jnp.float32)  55.2 us
    all_gather x1, waiting for transfers between devices, on_device(): shard_rows = lax.all_gather(codebook, 'dp', axis=0, tiled=True)  53.2 us
    dot_general x20, matrix products, matmul_nt(): lax.dot_general(left, right, (((1,), (1,)), ((), ())), preferred_element_...  46.3 us
    psum x1, blocking collectives, on_device(): lax.psum((loss_part, jnp.where(leading, entropy_part, 0.0), jnp.where(lea...  38.9 us
    convert_element_type x5, local copies, waits for them, and re-layouts, forward(): matmul_bf(normal_a, w_qkv).astype(jnp.bfloat16)  22.4 us
  transfers between devices with their start and end apart: 9, of which 6 were waited for; matrix products, arithmetic and copies ran while one was open for 26% of the time, Pallas kernels for 0%

commit v1 on v0

v1 whole, which is shorter than its diff:
```python
import functools

import jax
import jax.numpy as jnp
from jax import lax
from jax.experimental import pallas as pl
from jax.experimental.pallas import tpu as pltpu
from jax.sharding import PartitionSpec as P

SEQ = 256
D = 768
HD = 64
HEADS = 12
FF = 3072
FF_PIECE = 768
QKV = 3 * D
L_O, L_A, L_M, L_ALL = D, 2 * D, 3 * D, 3 * D + FF
D_GH, D_QKV, D_GB, D_ALL = FF, FF + D, FF + D + QKV, FF + D + QKV + D
V_COUNT, V_LOSS, V_ROWS = 10, 15, 16
COUNT_ROWS = V_LOSS - V_COUNT

COMMIT_WEIGHT = 0.25
EPSILON = 1e-06
SQRT_HALF = 0.5**0.5
INV_ROOT_TAU = 0.3989422804014327
HEAD_SCALE = HD**-0.5
MESH = pl.DeviceIdType.MESH
BF, F32 = jnp.bfloat16, jnp.float32
VMEM_BYTES = 60 << 20


def matmul_nn(left, right):
    return jnp.dot(left, right, preferred_element_type=F32)


def matmul_nt(left, right):
    return lax.dot_general(left, right, (((1,), (1,)), ((), ())), preferred_element_type=F32)


def matmul_tn(left, right):
    return lax.dot_general(left, right, (((0,), (0,)), ((), ())), preferred_element_type=F32)


def layer_norm(rows_in):
    centered = rows_in - jnp.mean(rows_in, axis=-1, keepdims=True)
    inv_std = lax.rsqrt(jnp.mean(centered * centered, axis=-1, keepdims=True) + EPSILON)
    return centered * inv_std, inv_std


def norm_back(incoming, scaled, inv_std, gain_row):
    x = incoming * gain_row
    return inv_std * (
        x
        - jnp.mean(x, axis=-1, keepdims=True)
        - scaled * jnp.mean(x * scaled, axis=-1, keepdims=True)
    )


def column_sum(x):
    return jnp.sum(x, axis=0, keepdims=True)


def head_masks():
    low = lax.broadcasted_iota(jnp.int32, (SEQ, 2 * HD), 1) < HD
    return (lambda t: jnp.where(low, t, 0)), (lambda t: jnp.where(low, 0, t))


def forward_image(x_ref, weights, l_ref, qkv_ref, pt_ref, slope_ref, h1_ref, out_ref, outb_ref, vt_ref, ot_ref):
    gains, shifts, w_qkv, w_out, out_bias, w_up, up_bias, w_down, down_bias = weights
    h = x_ref[...].astype(F32)
    s1, _ = layer_norm(h)
    a = (s1 * gains[0:1, :] + shifts[0:1, :]).astype(BF)
    l_ref[:, L_A:L_M] = a
    for j in range(3):
        qkv_ref[:, j * D : (j + 1) * D] = matmul_nn(a, w_qkv[:, j * D : (j + 1) * D]).astype(BF)
    vt_ref[...] = qkv_ref[:, 2 * D : 3 * D].T
    masks = head_masks()
    for pair in range(HEADS // 2):
        q = qkv_ref[:, pair * 128 : (pair + 1) * 128]
        k = qkv_ref[:, D + pair * 128 : D + (pair + 1) * 128]
        for half in range(2):
            head = 2 * pair + half
            st = matmul_nt(masks[half](k), q)
            e = jnp.exp((st - jnp.max(st, axis=0, keepdims=True)) * HEAD_SCALE)
            pt = (e * (1.0 / column_sum(e))).astype(BF)
            pt_ref[head] = pt
            span = slice(head * HD, (head + 1) * HD)
            ot_ref[span, :] = matmul_nn(vt_ref[span, :], pt).astype(BF)
    o = ot_ref[...].T
    l_ref[:, L_O:L_A] = o
    h1 = h + matmul_nn(o, w_out[...]) + out_bias[...]
    h1_ref[...] = h1
    s2, _ = layer_norm(h1)
    b = (s2 * gains[1:2, :] + shifts[1:2, :]).astype(BF)
    l_ref[:, 0:L_O] = b
    result = h1 + down_bias[...]
    for j in range(FF // FF_PIECE):
        span = slice(j * FF_PIECE, (j + 1) * FF_PIECE)
        u = matmul_nn(b, w_up[:, span]) + up_bias[:, span]
        half_curve = 0.5 + 0.5 * lax.erf(u * SQRT_HALF)
        m = (u * half_curve).astype(BF)
        l_ref[:, L_M + j * FF_PIECE : L_M + (j + 1) * FF_PIECE] = m
        slope = half_curve + u * jnp.exp(-0.5 * u * u) * INV_ROOT_TAU
        slope_ref[:, span] = slope.astype(slope_ref.dtype)
        result = result + matmul_nn(m, w_down[span, :])
    out_ref[...] = result
    outb_ref[...] = result.astype(BF)


def backward_image(
    scale, out_ref, other_ref, arrived_ref, x_ref, weights, qkv_ref, pt_ref, slope_ref, h1_ref,
    d_ref, vec_ref, dh_ref, dhb_ref, kt_ref, qt_ref,
):
    gains, shifts, w_qkv, w_out, out_bias, w_up, up_bias, w_down, down_bias = weights
    diff = out_ref[...] - other_ref[...].astype(F32)
    vec_ref[V_LOSS : V_LOSS + 1, :] = column_sum(diff * diff) * scale
    vec_ref[V_COUNT:V_LOSS, :] = jnp.zeros((COUNT_ROWS, D), F32)
    g = diff * scale + arrived_ref[...].astype(F32)
    gb = g.astype(BF)
    d_ref[:, D_GB:D_ALL] = gb
    vec_ref[9:10, :] = column_sum(g)
    db = jnp.zeros((SEQ, D), F32)
    for j in range(FF // FF_PIECE):
        span = slice(j * FF_PIECE, (j + 1) * FF_PIECE)
        du = (matmul_nt(gb, w_down[span, :]) * slope_ref[:, span].astype(F32)).astype(BF)
        d_ref[:, span] = du
        vec_ref[5 + j : 6 + j, :] = column_sum(du.astype(F32))
        db = db + matmul_nt(du, w_up[:, span])
    s2, inv2 = layer_norm(h1_ref[...])
    vec_ref[1:2, :] = column_sum(db * s2)
    vec_ref[3:4, :] = column_sum(db)
    dh1 = g + norm_back(db, s2, inv2, gains[1:2, :])
    vec_ref[4:5, :] = column_sum(dh1)
    gh = dh1.astype(BF)
    d_ref[:, D_GH:D_QKV] = gh
    do = matmul_nt(gh, w_out[...]).astype(BF)
    kt_ref[...] = qkv_ref[:, D : 2 * D].T
    masks = head_masks()
    for pair in range(HEADS // 2):
        lanes = slice(pair * 128, (pair + 1) * 128)
        q = qkv_ref[:, lanes]
        v = qkv_ref[:, 2 * D + pair * 128 : 2 * D + (pair + 1) * 128]
        do_pair = do[:, lanes]
        dk = dv = 0.0
        for half in range(2):
            head = 2 * pair + half
            pt = pt_ref[head]
            ptf = pt.astype(F32)
            dv = dv + matmul_nn(pt, masks[half](do_pair))
            dpt = matmul_nt(masks[half](v), do_pair)
            dst = (ptf * (dpt - column_sum(dpt * ptf))).astype(BF)
            dk = dk + matmul_nn(dst, masks[half](q))
            span = slice(head * HD, (head + 1) * HD)
            qt_ref[span, :] = (matmul_nn(kt_ref[span, :], dst) * HEAD_SCALE).astype(BF)
        base = D_QKV + D + pair * 128
        d_ref[:, base : base + 128] = (dk * HEAD_SCALE).astype(BF)
        d_ref[:, base + D : base + D + 128] = dv.astype(BF)
    d_ref[:, D_QKV : D_QKV + D] = qt_ref[...].T
    da = matmul_nt(d_ref[:, D_QKV:D_GB], w_qkv[...])
    s1, inv1 = layer_norm(x_ref[...].astype(F32))
    vec_ref[0:1, :] = column_sum(da * s1)
    vec_ref[2:3, :] = column_sum(da)
    dh = dh1 + norm_back(da, s1, inv1, gains[0:1, :])
    dh_ref[...] = dh
    dhb_ref[...] = dh.astype(BF)


WEIGHT_SHAPES = ((2, D), (2, D), (D, QKV), (D, D), (1, D), (D, FF), (1, FF), (FF, D), (1, D))


def weight_specs():
    def whole(shape):
        return pl.BlockSpec(shape, lambda *_: (0, 0), pipeline_mode=pl.Buffered(1))

    return [whole(shape) for shape in WEIGHT_SHAPES]


def block_forward(x, weights):
    rows = x.shape[0]
    images = rows // SEQ

    def row_block(width):
        return pl.BlockSpec((SEQ, width), lambda i: (i, 0))

    def body(x_ref, *refs):
        forward_image(x_ref, refs[:9], *refs[9:])

    def shape(width, dtype):
        return jax.ShapeDtypeStruct((rows, width), dtype)

    return pl.pallas_call(
        body,
        grid=(images,),
        in_specs=[row_block(D)] + weight_specs(),
        out_specs=[
            row_block(L_ALL),
            row_block(QKV),
            pl.BlockSpec((HEADS, SEQ, SEQ), lambda i: (i, 0, 0)),
            row_block(FF),
            row_block(D),
            row_block(D),
            row_block(D),
        ],
        out_shape=[
            shape(L_ALL, BF),
            shape(QKV, BF),
            jax.ShapeDtypeStruct((images * HEADS, SEQ, SEQ), BF),
            shape(FF, BF),
            shape(D, F32),
            shape(D, F32),
            shape(D, BF),
        ],
        scratch_shapes=[pltpu.VMEM((D, SEQ), BF), pltpu.VMEM((D, SEQ), BF)],
        compiler_params=pltpu.CompilerParams(vmem_limit_bytes=VMEM_BYTES),
        name="block_forward",
    )(x, *weights)


def block_backward(which, flags, result, other, arrived, x, weights, qkv, pt, slope, h1, vec, d, dh):
    rows = x.shape[0]

    def row_block(width):
        return pl.BlockSpec((SEQ, width), lambda i, which_ref: (which_ref[0], 0))

    def whole(height, width):
        return pl.BlockSpec((height, width), lambda i, which_ref: (0, 0))

    def body(which_ref, flags_ref, out_ref, other_ref, arrived_ref, x_ref, *refs):
        weight_refs = refs[:9]
        qkv_ref, pt_ref, slope_ref, h1_ref, vec_in = refs[9:14]
        d_ref, dh_ref, vec_out, dhb_ref, kt_ref, qt_ref = refs[-6:]
        backward_image(
            flags_ref[0], out_ref, other_ref, arrived_ref, x_ref, weight_refs, qkv_ref, pt_ref,
            slope_ref, h1_ref, d_ref, vec_out, dh_ref, dhb_ref, kt_ref, qt_ref,
        )
        vec_out[...] = vec_in[...] + vec_out[...] * flags_ref[1]

    keep = [] if d is None else [d, dh]
    first_kept = 2 + 4 + 9 + 5
    return pl.pallas_call(
        body,
        grid_spec=pltpu.PrefetchScalarGridSpec(
            num_scalar_prefetch=1,
            grid=(1,),
            in_specs=[pl.BlockSpec(memory_space=pltpu.SMEM), row_block(D), row_block(D), whole(SEQ, D), row_block(D)]
            + weight_specs()
            + [
                row_block(QKV),
                pl.BlockSpec((HEADS, SEQ, SEQ), lambda i, which_ref: (which_ref[0], 0, 0)),
                row_block(FF),
                row_block(D),
                whole(V_ROWS, D),
            ]
            + [pl.BlockSpec(memory_space=pl.ANY)] * len(keep),
            out_specs=[row_block(D_ALL), row_block(D), whole(V_ROWS, D), whole(SEQ, D)],
            scratch_shapes=[pltpu.VMEM((D, SEQ), BF), pltpu.VMEM((D, SEQ), BF)],
        ),
        out_shape=[
            jax.ShapeDtypeStruct((rows, D_ALL), BF),
            jax.ShapeDtypeStruct((rows, D), F32),
            jax.ShapeDtypeStruct((V_ROWS, D), F32),
            jax.ShapeDtypeStruct((SEQ, D), BF),
        ],
        input_output_aliases={first_kept: 0, first_kept + 1: 1} if keep else {},
        compiler_params=pltpu.CompilerParams(vmem_limit_bytes=VMEM_BYTES),
        name="block_backward",
    )(which, flags, result, other, arrived, x, *weights, qkv, pt, slope, h1, vec, *keep)


UNITS = 36
PART = D // 16
COLS = 256
LAG_Y, LAG_Z, LAG_OUT = 1, 3, 5
PIECE = 384


def reduce_kernel(
    l_ref, d_ref, vec_ref, qkv_out, out_out, up_out, down_out, vec_out, side_out,
    lt, lbuf, dbuf, acc_y, acc_z, acc_o, tx_c, rx_c, tx_y, rx_y, tx_z, rx_z, vec_tx, vec_c, vec_y, vec_z,
    lsem, dsem, sc, rc, sy, ry, sz, rz, sv, rv,
):
    sec, dp = lax.axis_index("section"), lax.axis_index("dp")
    core, y, z = dp % 2, (dp // 2) % 2, dp // 4
    across = (sec, dp + 1 - 2 * core)
    along_y = (sec, dp + 2 - 4 * y)
    along_z = [(sec, (z + k) % 4 * 4 + y * 2 + core) for k in (1, 2, 3)]
    beside = (1 - sec, dp)
    barrier = pltpu.get_barrier_semaphore()
    for target in [across, along_y, beside] + along_z:
        pl.semaphore_signal(barrier, inc=1, device_id=target, device_id_type=MESH)
    pl.semaphore_wait(barrier, 6)

    def remote(src, dst, send, recv, target):
        return pltpu.make_async_remote_copy(src, dst, send, recv, device_id=target, device_id_type=MESH)

    def spot(g):
        return ((g % 2 + core) % 2) * 8 + (((g // 2) % 2 + y) % 2) * 4 + (g // 4 - z + 4) % 4

    def aligned(x, n):
        return pl.multiple_of(x, n)

    def load_left(i):
        return pltpu.make_async_copy(l_ref.at[:, pl.ds(aligned(i * PIECE, PIECE), PIECE)], lbuf.at[i % 2], lsem.at[i % 2])

    def load_right(u):
        d = jnp.where(u < 24, u, 24 + u % 3)
        return pltpu.make_async_copy(d_ref.at[:, pl.ds(aligned(d * COLS, COLS), COLS)], dbuf.at[u % 2], dsem.at[u % 2])

    def prepare(i):
        load_left(i).wait()

        @pl.when(i < 13)
        def _():
            load_left(i + 1).start()

        turned = lbuf[i % 2].T

        @pl.when(i < 6)
        def _():
            for k in range(8):
                place = spot((i % 2) * 8 + k) * PART
                lt[i // 2, pl.ds(aligned(place, PART), PART), :] = turned[k * PART : (k + 1) * PART]

        @pl.when(i >= 6)
        def _():
            for k in range(8):
                place = spot((i - 6) * 2 + k // 4) * PART
                lt[3 + k % 4, pl.ds(aligned(place, PART), PART), :] = turned[k * PART : (k + 1) * PART]

    def send_core(u):
        return remote(tx_c.at[u], rx_c.at[u], sc.at[u], rc.at[u], across)

    def send_y(u):
        return remote(tx_y.at[u], rx_y.at[u], sy.at[u], ry.at[u], along_y)

    def send_z(u, k):
        return remote(tx_z.at[u, k], rx_z.at[u, k], sz.at[u, k], rz.at[u, k], along_z[k])

    vec_core = remote(vec_ref, vec_c, sv.at[0], rv.at[0], across)
    vec_along_y = remote(vec_tx, vec_y, sv.at[1], rv.at[1], along_y)
    vec_along_z = [remote(vec_z.at[z], vec_z.at[z], sv.at[2 + k], rv.at[2 + k], along_z[k]) for k in range(3)]
    vec_beside = remote(vec_out.at[8:16], side_out, sv.at[5], rv.at[5], beside)

    load_left(0).start()
    load_right(0).start()
    prepare(0)
    prepare(1)
    vec_core.start()

    def step(i, carry):
        @pl.when(i < UNITS)
        def _():
            u = i

            @pl.when(u + 1 < UNITS)
            def _():
                load_right(u + 1).start()

            load_right(u).wait()
            l = jnp.where(u < 12, 0, jnp.where(u < 15, 1, jnp.where(u < 24, 2, 3 + (u - 24) // 3)))
            product = matmul_nn(lt[l], dbuf[u % 2])
            acc_y[u % 2] = product[: 8 * PART]
            tx_c[u] = product[8 * PART :].astype(BF)
            send_core(u).start()

        @pl.when((i >= LAG_Y) & (i < UNITS + LAG_Y))
        def _():
            u = i - LAG_Y
            send_core(u).wait()
            t = acc_y[u % 2] + rx_c[u].astype(F32)
            acc_z[u % 4] = t[: 4 * PART]
            tx_y[u] = t[4 * PART :].astype(BF)
            send_y(u).start()

        @pl.when((i >= LAG_Z) & (i < UNITS + LAG_Z))
        def _():
            u = i - LAG_Z
            send_y(u).wait()
            t = acc_z[u % 4] + rx_y[u].astype(F32)
            acc_o[u % 4] = t[:PART]
            for k in range(3):
                tx_z[u, k] = t[PART * (k + 1) : PART * (k + 2)].astype(BF)
                send_z(u, k).start()

        @pl.when(i >= LAG_OUT)
        def _():
            u = i - LAG_OUT
            t = acc_o[u % 4]
            for k in range(3):
                send_z(u, k).wait()
                t = t + rx_z[u, k].astype(F32)

            def lanes(n):
                return pl.ds(aligned(n * COLS, COLS), COLS)

            @pl.when(u < 12)
            def _():
                up_out[:, lanes(u)] = t

            @pl.when((u >= 12) & (u < 15))
            def _():
                out_out[:, lanes(u - 12)] = t

            @pl.when((u >= 15) & (u < 24))
            def _():
                qkv_out[:, lanes(u - 15)] = t

            @pl.when(u >= 24)
            def _():
                down_out[pl.ds(aligned((u - 24) // 3 * PART, PART), PART), lanes(u % 3)] = t

        @pl.when(i < 12)
        def _():
            prepare(i + 2)

        @pl.when(i == 3)
        def _():
            vec_core.wait()
            vec_tx[...] = vec_ref[...] + vec_c[...]
            vec_along_y.start()

        @pl.when(i == 8)
        def _():
            vec_along_y.wait()
            vec_z[z] = vec_tx[...] + vec_y[...]
            for copy in vec_along_z:
                copy.start()

        @pl.when(i == 14)
        def _():
            for copy in vec_along_z:
                copy.wait()
            vec_out[...] = (vec_z[0] + vec_z[1]) + (vec_z[2] + vec_z[3])
            vec_beside.start()

        return carry

    lax.fori_loop(0, UNITS + LAG_OUT, step, 0)
    vec_beside.wait()


def reduce_weights(l, d, vec):
    dma = pltpu.SemaphoreType.DMA
    vm = pltpu.VMEM
    return pl.pallas_call(
        reduce_kernel,
        out_shape=[
            jax.ShapeDtypeStruct((PART, QKV), F32),
            jax.ShapeDtypeStruct((PART, D), F32),
            jax.ShapeDtypeStruct((PART, FF), F32),
            jax.ShapeDtypeStruct((4 * PART, D), F32),
            jax.ShapeDtypeStruct((V_ROWS, D), F32),
            jax.ShapeDtypeStruct((8, D), F32),
        ],
        in_specs=[pl.BlockSpec(memory_space=pl.ANY)] * 2 + [pl.BlockSpec(memory_space=pltpu.VMEM)],
        out_specs=[pl.BlockSpec(memory_space=pltpu.VMEM)] * 6,
        scratch_shapes=[
            vm((7, D, 4 * SEQ), BF), vm((2, 4 * SEQ, PIECE), BF), vm((2, 4 * SEQ, COLS), BF),
            vm((2, 8 * PART, COLS), F32), vm((4, 4 * PART, COLS), F32), vm((4, PART, COLS), F32),
            vm((UNITS, 8 * PART, COLS), BF), vm((UNITS, 8 * PART, COLS), BF),
            vm((UNITS, 4 * PART, COLS), BF), vm((UNITS, 4 * PART, COLS), BF),
            vm((UNITS, 3, PART, COLS), BF), vm((UNITS, 3, PART, COLS), BF),
            vm((V_ROWS, D), F32), vm((V_ROWS, D), F32), vm((V_ROWS, D), F32), vm((4, V_ROWS, D), F32),
            dma((2,)), dma((2,)), dma((UNITS,)), dma((UNITS,)), dma((UNITS,)), dma((UNITS,)),
            dma((UNITS, 3)), dma((UNITS, 3)), dma((6,)), dma((6,)),
        ],
        compiler_params=pltpu.CompilerParams(collective_id=1, has_side_effects=True, vmem_limit_bytes=VMEM_BYTES),
        name="weight_grad_reduce",
    )(l, d, vec)


def count_shares(counts, total_count):
    shares = counts / total_count
    nonzero_share = jnp.where(counts > 0, shares, 1.0)
    return -jnp.sum(shares * jnp.log(nonzero_share)), jnp.sum((counts > 0).astype(F32))


def on_device(
    patches, targets, code_ids, codebook, norm_gains, norm_shifts, w_qkv, w_out, out_bias, w_up, up_bias, w_down, down_bias
):
    section = lax.axis_index("section")
    leading = section == 0
    dp_size = lax.axis_size("dp")
    dp = lax.axis_index("dp")
    weights = (
        norm_gains[0], norm_shifts[0], w_qkv[0], w_out[0], out_bias, w_up[0], up_bias, w_down[0], down_bias
    )
    rows, width = patches.shape
    images = rows // SEQ
    vocab_local = codebook.shape[0]
    vocab_all = vocab_local * dp_size
    total_tokens = rows * dp_size

    shard_rows = lax.all_gather(codebook, "dp", axis=0, tiled=True)
    chosen = jnp.take(shard_rows, jnp.clip(code_ids, 0, vocab_all - 1), axis=0)

    l, qkv, pt, slope, h1, result, result_bf = block_forward(jnp.where(leading, patches, chosen), weights)

    other = jnp.where(leading, chosen, targets)
    d = dh = None
    vec = jnp.zeros((V_ROWS, D), F32)
    arrived = jnp.zeros((SEQ, D), BF)
    x = jnp.where(leading, patches, chosen)
    for moment in range(images + 1):
        which = jnp.clip(moment - 1 + section, 0, images - 1).astype(jnp.int32)[None]
        active = jnp.where(leading, moment >= 1, moment < images).astype(F32)
        flags = jnp.stack([jnp.where(leading, COMMIT_WEIGHT, 1.0).astype(F32), active])
        d, dh, vec, outgoing = block_backward(
            which, flags, result, other, arrived, x, weights, qkv, pt, slope, h1, vec, d, dh
        )
        if moment < images:
            arrived = lax.ppermute(outgoing, "section", [(1, 0)])

    vocab_iota = lax.broadcasted_iota(jnp.int32, (1, vocab_all), 1)
    counts = jnp.sum((code_ids[:, None] == vocab_iota).astype(F32), axis=0)
    small = dp_size == 16 and vocab_all <= COUNT_ROWS * D and rows == 4 * SEQ
    if small:
        spread = jnp.pad(counts, (0, COUNT_ROWS * D - vocab_all)).reshape(COUNT_ROWS, D)
        vec = lax.dynamic_update_slice(vec, spread, (V_COUNT, 0))
        g_qkv, g_out, g_up, g_down, vec, side = reduce_weights(l, d, vec)
        counts = vec[V_COUNT:V_LOSS].reshape(-1)[:vocab_all]
        loss_all = jnp.sum(vec[V_LOSS]) + jnp.sum(side[V_LOSS - 8])
        entropy_all, used_all = count_shares(counts, total_tokens)
        hist_local = lax.dynamic_slice(counts, (dp * vocab_local,), (vocab_local,))
    else:
        pairs = (
            (l[:, L_A:L_M], d[:, D_QKV:D_GB]),
            (l[:, L_O:L_A], d[:, D_GH:D_QKV]),
            (l[:, :L_O], d[:, :D_GH]),
            (l[:, L_M:], d[:, D_GB:]),
        )
        g_qkv, g_out, g_up, g_down = (
            lax.psum_scatter(matmul_tn(left, right), "dp", scatter_dimension=0, tiled=True) for left, right in pairs
        )
        hist_local = lax.psum_scatter(counts, "dp", scatter_dimension=0, tiled=True)
        entropy_part, used_part = count_shares(hist_local, total_tokens)
        vec = lax.psum(vec, "dp")
        entropy_all, used_all = lax.psum((entropy_part, used_part), "dp")
        loss_all = lax.psum(jnp.sum(vec[V_LOSS]), "section")
    stats = jnp.stack([loss_all / (total_tokens * width), used_all / vocab_all, jnp.exp(entropy_all) / vocab_all])
    return (
        result_bf[None],
        dh[None],
        vec[None, 0:2],
        vec[None, 2:4],
        g_qkv[None],
        g_out[None],
        vec[None, 4],
        g_up[None],
        vec[5:9].reshape(1, FF),
        g_down[None],
        vec[None, 9],
        hist_local.astype(jnp.int32),
        stats,
    )


def solution(mesh):
    return jax.shard_map(
        on_device,
        mesh=mesh,
        in_specs=(
            P("dp", None),
            P("dp", None),
            P("dp"),
            P("dp", None),
            P("section", None, None),
            P("section", None, None),
            P("section", None, None),
            P("section", None, None),
            P("section", None),
            P("section", None, None),
            P("section", None),
            P("section", None, None),
            P("section", None),
        ),
        out_specs=(
            P("section", "dp", None),
            P("section", "dp", None),
            P("section", None, None),
            P("section", None, None),
            P("section", "dp", None),
            P("section", "dp", None),
            P("section", None),
            P("section", "dp", None),
            P("section", None),
            P("section", "dp", None),
            P("section", None),
            P("dp"),
            P(),
        ),
        check_vma=False,
    )
```

time: 732 us -> 393 us (0.54)
  matrix products: 270 us -> 0 us
  Pallas kernels: 0 us -> 228 us
  waiting for transfers between devices: 197 us -> 97.1 us
  blocking collectives: 99.1 us -> 0 us
  local copies, waits for them, and re-layouts: 80.3 us -> 24.4 us
  other arithmetic: 48.8 us -> 12.3 us
  between operations: 25.2 us -> 17.4 us
    dot_general x90 -> x0, matrix products: 270 us -> none  [the longest x20 119 us: matmul_tn(): lax.dot_general(left, right, (((0,), (0,)), ((), ())), preferred_element_...]
    pallas_call x0 -> x7, Pallas kernels: none -> 228 us  [the longest x1 100 us: reduce_weights(): pl.pallas_call(reduce_kernel, out_shape=[jax.ShapeDtypeStruct((PART, QKV)...]
    reduce_scatter x4 -> x0, waiting for transfers between devices: 125 us -> none  [the longest x1 116 us: on_device(): lax.psum_scatter(matrix_total[3][None], 'dp', scatter_dimension=1, tiled=...]
    psum x2 -> x0, blocking collectives: 99.1 us -> none  [the longest x1 60.2 us: on_device(): lax.psum((vector_total[0], vector_total[1], vector_total[2], vector_total...]
    convert_element_type x10 -> x0, local copies, waits for them, and re-layouts: 31.9 us -> none  [the longest x5 22.4 us: forward(): matmul_bf(normal_a, w_qkv).astype(jnp.bfloat16)]
    another operation x20 -> x0, local copies, waits for them, and re-layouts: 21 us -> none  [the longest x10 10.8 us: backward(): jnp.stack([gain_one, gain_two])]
    ppermute x4, waiting for transfers between devices: 18.1 us -> 39 us  [on_device(): arrived = lax.ppermute(outgoing, 'section', [(1, 0)])]
    convert_element_type x14 -> x1, other arithmetic: 9.91 us -> 0.64 us  [on_device(): hist_local.astype(jnp.int32)]
  transfers between devices with their start and end apart: 9 -> 5, of which waited for: 6 -> 5; matrix products, arithmetic and copies ran while one was open for 26% -> 1% of each run, Pallas kernels for 0% -> 0%
where the time goes in v1:
time: 393 us; the launch traced here: 386 us
  Pallas kernels  228 us (58%)
  waiting for transfers between devices  97.1 us (25%)
  local copies, waits for them, and re-layouts  24.4 us (6%)
  between operations  17.4 us (4%)
  other arithmetic  12.3 us (3%)
  starting transfers between devices  6.09 us (2%)
    pallas_call x1, Pallas kernels, reduce_weights(): pl.pallas_call(reduce_kernel, out_shape=[jax.ShapeDtypeStruct((PART, QKV)...  100 us
    pallas_call x5, Pallas kernels, block_backward(): pl.pallas_call(body, grid_spec=pltpu.PrefetchScalarGridSpec(num_scalar_pr...  83.5 us
    all_gather x1, waiting for transfers between devices, on_device(): shard_rows = lax.all_gather(codebook, 'dp', axis=0, tiled=True)  57.5 us
    pallas_call x1, Pallas kernels, block_forward(): pl.pallas_call(body, grid=(images,), in_specs=[row_block(D)] + weight_spe...  44.6 us
    ppermute x4, waiting for transfers between devices, on_device(): arrived = lax.ppermute(outgoing, 'section', [(1, 0)])  39 us
    unnamed x18, local copies, waits for them, and re-layouts  11.6 us
  transfers between devices with their start and end apart: 5, of which 5 were waited for; matrix products, arithmetic and copies ran while one was open for 1% of the time, Pallas kernels for 0%

profile of v1, /device:TPU:0, one launch (start us, length us, event | category | flops | bytes accessed | tf_op | source)
XLA Modules:
  0.0 385.6 jit_solution(6557057244304714282)
XLA Ops:
  9.9 57.5 %all-gather.2.cloned.1.call-done = bf16[3200,768]{1,0:T(8,128)(2,1)} async-done(((bf16[200,768]{1,0:T(8,128)(2,1)}), bf16[3200,768]{1,0:T(8,128)(2,1)}) %all-gather.2.cloned.1.call-update) | async-done | bytes 4915216 | tf_op jit(solution)/shard_map/all_gather | solution.py:494
  67.4 7.5 %gather_fusion = bf16[1024,768]{1,0:T(8,128)(2,1)S(1)} fusion(bf16[3200,768]{1,0:T(8,128)(2,1)} %all-gather.2.cloned.1.call-done, s32[1024]{0:T(1024)S(1)} %fusion), kind=kCustom, calls=%fused_computation | custom fusion | bytes 3149824 | tf_op jit(solution)/shard_map/jit(_take)/gather | solution.py:495
  74.9 3.4 broadcast_select_fusion.1
  78.3 44.6 %block_forward.1 = (bf16[1024,5376]{1,0:T(8,128)(2,1)}, bf16[1024,2304]{1,0:T(8,128)(2,1)}, bf16[48,256,256]{2,1,0:T(8,128)(2,1)}, bf16[1024,3072]{1,0:T(8,128)(...) custom-call(bf16[1024,768]{1,0:T(8,128)(2,1)} %get-tuple-element.80.x_ref, ...), custom_call_target="tpu_custom_call" | custom-call | tf_op jit(solution)/shard_map/block_forward/pallas_call | solution.py:191
  122.8 0.8 broadcast_in_dim.71.arrived_ref
  124.2 16.7 %block_backward.5 = (bf16[1024,6912]{1,0:T(8,128)(2,1)}, f32[1024,768]{1,0:T(8,128)}, f32[16,768]{1,0:T(8,128)}, bf16[256,768]{1,0:T(8,128)(2,1)}) custom-call(s32[1]{0:T(128)} %bitcast.13.which_ref, f32[2]{0:T(128)} %pad_maximum_fusion.2.flags_ref, f32[1024,768]{1,0:T(8,128)} %get-tuple-element.46.out_ref, bf16[1024,768]{1,0:T(8,128)(2,1)} %get-tuple-element.79.other_ref, ...), custom_call_target="tpu_custom_call" | custom-call | tf_op jit(solution)/shard_map/block_backward/pallas_call | solution.py:240
  141.0 1.5 collective-permute-start
  143.0 11.3 %collective-permute-done.arrived_ref = bf16[256,768]{1,0:T(8,128)(2,1)S(1)} collective-permute-done((bf16[256,768]{1,0:T(8,128)(2,1)}, bf16[256,768]{1,0:T(8,128)(2,1)S(1)}, u32[]{:S(2)}, u32[]{:S(2)}) %collective-permute-start) | collective-permute-done | bytes 393248 | tf_op jit(solution)/shard_map/ppermute | solution.py:512
  154.4 0.7 copy-done.4
  155.1 16.7 %block_backward.6 = (bf16[1024,6912]{1,0:T(8,128)(2,1)}, f32[1024,768]{1,0:T(8,128)}, f32[16,768]{1,0:T(8,128)}, bf16[256,768]{1,0:T(8,128)(2,1)}) custom-call(s32[1]{0:T(128)} %bitcast.12.which_ref, f32[2]{0:T(128)} %pad_maximum_fusion.1.flags_ref, f32[1024,768]{1,0:T(8,128)} %get-tuple-element.46.out_ref, ...), custom_call_target="tpu_custom_call", output_to_operand_aliasing={{0}: (20, {}), {1}: (21, {})} | custom-call | tf_op jit(solution)/shard_map/block_backward/pallas_call | solution.py:240
  171.8 1.5 collective-permute-start.1
  173.3 11.1 %collective-permute-done.1.arrived_ref = bf16[256,768]{1,0:T(8,128)(2,1)S(1)} collective-permute-done((bf16[256,768]{1,0:T(8,128)(2,1)}, bf16[256,768]{1,0:T(8,128)(2,1)S(1)}, u32[]{:S(2)}, u32[]{:S(2)}) %collective-permute-start.1) | collective-permute-done | bytes 393248 | tf_op jit(solution)/shard_map/ppermute | solution.py:512
  184.4 0.7 copy-done.3
  185.1 16.7 %block_backward.7 = (bf16[1024,6912]{1,0:T(8,128)(2,1)}, f32[1024,768]{1,0:T(8,128)}, f32[16,768]{1,0:T(8,128)}, bf16[256,768]{1,0:T(8,128)(2,1)}) custom-call(s32[1]{0:T(128)} %bitcast.11.which_ref, f32[2]{0:T(128)} %pad_maximum_fusion.1.flags_ref, f32[1024,768]{1,0:T(8,128)} %get-tuple-element.46.out_ref, ...), custom_call_target="tpu_custom_call", output_to_operand_aliasing={{0}: (20, {}), {1}: (21, {})} | custom-call | tf_op jit(solution)/shard_map/block_backward/pallas_call | solution.py:240
  201.8 1.5 collective-permute-start.2
  203.3 10.1 %collective-permute-done.2.arrived_ref = bf16[256,768]{1,0:T(8,128)(2,1)S(1)} collective-permute-done((bf16[256,768]{1,0:T(8,128)(2,1)}, bf16[256,768]{1,0:T(8,128)(2,1)S(1)}, u32[]{:S(2)}, u32[]{:S(2)}) %collective-permute-start.2) | collective-permute-done | bytes 393248 | tf_op jit(solution)/shard_map/ppermute | solution.py:512
  213.4 0.7 copy-done.2
  214.2 16.7 %block_backward.8 = (bf16[1024,6912]{1,0:T(8,128)(2,1)}, f32[1024,768]{1,0:T(8,128)}, f32[16,768]{1,0:T(8,128)}, bf16[256,768]{1,0:T(8,128)(2,1)}) custom-call(s32[1]{0:T(128)} %bitcast.10.which_ref, f32[2]{0:T(128)} %pad_maximum_fusion.1.flags_ref, f32[1024,768]{1,0:T(8,128)} %get-tuple-element.46.out_ref, ...), custom_call_target="tpu_custom_call", output_to_operand_aliasing={{0}: (20, {}), {1}: (21, {})} | custom-call | tf_op jit(solution)/shard_map/block_backward/pallas_call | solution.py:240
  230.9 1.6 collective-permute-start.3
  232.5 2.0 convert_reduce_fusion
  235.1 6.5 %collective-permute-done.3.arrived_ref = bf16[256,768]{1,0:T(8,128)(2,1)S(1)} collective-permute-done((bf16[256,768]{1,0:T(8,128)(2,1)}, bf16[256,768]{1,0:T(8,128)(2,1)S(1)}, u32[]{:S(2)}, u32[]{:S(2)}) %collective-permute-start.3) | collective-permute-done | bytes 393248 | tf_op jit(solution)/shard_map/ppermute | solution.py:512
  241.6 0.7 copy-done.1
  242.4 16.7 %block_backward.9 = (bf16[1024,6912]{1,0:T(8,128)(2,1)}, f32[1024,768]{1,0:T(8,128)}, f32[16,768]{1,0:T(8,128)}, bf16[256,768]{1,0:T(8,128)(2,1)}) custom-call(s32[1]{0:T(128)} %bitcast.7.which_ref, f32[2]{0:T(128)} %pad_maximum_fusion.flags_ref, f32[1024,768]{1,0:T(8,128)} %get-tuple-element.46.out_ref, ...), custom_call_target="tpu_custom_call", output_to_operand_aliasing={{0}: (20, {}), {1}: (21, {})} | custom-call | tf_op jit(solution)/shard_map/block_backward/pallas_call | solution.py:240
  259.1 1.7 dynamic_update_slice.3.vec_ref
  260.7 100.1 %weight_grad_reduce.1 = (f32[48,2304]{1,0:T(8,128)}, f32[48,768]{1,0:T(8,128)}, f32[48,3072]{1,0:T(8,128)}, f32[192,768]{1,0:T(8,128)}, f32[16,768]{1,0:T(8,128)}, /*index=5*/f32[8,768]{1,0:T(8,128)}) custom-call(bf16[1024,5376]{1,0:T(8,128)(2,1)} %get-tuple-element.68.l_ref, bf16[1024,6912]{1,0:T(8,128)(2,1)} %get-tuple-element.69.d_ref, ...), custom_call_target="tpu_custom_call" | custom-call | tf_op jit(solution)/shard_map/weight_grad_reduce/pallas_call | solution.py:445
  361.6 0.8 slice_bitcast_fusion
  362.4 1.4 slice_bitcast_fusion.1
  363.8 2.0 slice_reduce_fusion.1
  370.9 1.8 copy.48
  372.7 1.6 copy.49
  374.3 1.9 copy.50
  376.2 1.9 copy.51
  (24 shorter events, 7.7 us)
Async XLA Ops:
  7.2 60.2 %all-gather.2.cloned.1.call-start = ((), (), s32[]{:S(2)}) async-start(), calls=%async_computation | async-start | bytes 5222400 | tf_op jit(solution)/shard_map/all_gather | solution.py:494
  9.9 65.0 %copy-start = (bf16[1024,768]{1,0:T(8,128)(2,1)S(1)}, bf16[1024,768]{1,0:T(8,128)(2,1)}, u32[]{:S(2)}) copy-start(bf16[1024,768]{1,0:T(8,128)(2,1)} %param.14) | copy-start | bytes 4718596
  141.0 13.4 %collective-permute-start = (bf16[256,768]{1,0:T(8,128)(2,1)}, bf16[256,768]{1,0:T(8,128)(2,1)S(1)}, u32[]{:S(2)}, u32[]{:S(2)}) collective-permute-start(bf16[256,768]{1,0:T(8,128)(2,1)} %get-tuple-element.51), channel_id=1, source_target_pairs={{16,0},{17,1},{18,2},{19,3},{20,4},{21,5},{22,6},{23,7},{24,8},{25... | collective-permute-start | bytes 1179656 | tf_op jit(solution)/shard_map/ppermute | solution.py:512
  154.3 0.7 copy-start.4
  171.8 12.6 %collective-permute-start.1 = (bf16[256,768]{1,0:T(8,128)(2,1)}, bf16[256,768]{1,0:T(8,128)(2,1)S(1)}, u32[]{:S(2)}, u32[]{:S(2)}) collective-permute-start(bf16[256,768]{1,0:T(8,128)(2,1)} %get-tuple-element.55), channel_id=1, source_target_pairs={{16,0},{17,1},{18,2},{19,3},{20,4},{21,5},{22,6},{23,7},{24,8},{25... | collective-permute-start | bytes 1179656 | tf_op jit(solution)/shard_map/ppermute | solution.py:512
  184.4 0.7 copy-start.3
  201.8 11.6 %collective-permute-start.2 = (bf16[256,768]{1,0:T(8,128)(2,1)}, bf16[256,768]{1,0:T(8,128)(2,1)S(1)}, u32[]{:S(2)}, u32[]{:S(2)}) collective-permute-start(bf16[256,768]{1,0:T(8,128)(2,1)} %get-tuple-element.59), channel_id=1, source_target_pairs={{16,0},{17,1},{18,2},{19,3},{20,4},{21,5},{22,6},{23,7},{24,8},{25... | collective-permute-start | bytes 1179656 | tf_op jit(solution)/shard_map/ppermute | solution.py:512
  213.4 0.7 copy-start.2
  214.2 18.3 %copy-start.5 = (s32[1024]{0:T(1024)S(1)}, s32[1024]{0:T(1024)}, u32[]{:S(2)}) copy-start(s32[1024]{0:T(1024)} %param.15) | copy-start | bytes 12292
  230.9 10.7 %collective-permute-start.3 = (bf16[256,768]{1,0:T(8,128)(2,1)}, bf16[256,768]{1,0:T(8,128)(2,1)S(1)}, u32[]{:S(2)}, u32[]{:S(2)}) collective-permute-start(bf16[256,768]{1,0:T(8,128)(2,1)} %get-tuple-element.63), channel_id=1, source_target_pairs={{16,0},{17,1},{18,2},{19,3},{20,4},{21,5},{22,6},{23,7},{24,8},{25... | collective-permute-start | bytes 1179656 | tf_op jit(solution)/shard_map/ppermute | solution.py:512
  241.6 0.7 copy-start.1
Sparse Core Ops, SparseCore 0:
  10.2 57.1 all-gather.1

commit v2 on v1

--- a/solution.py
+++ b/solution.py
@@ -16,13 +16,13 @@
 QKV = 3 * D
 L_O, L_A, L_M, L_ALL = D, 2 * D, 3 * D, 3 * D + FF
 D_GH, D_QKV, D_GB, D_ALL = FF, FF + D, FF + D + QKV, FF + D + QKV + D
-V_COUNT, V_LOSS, V_ROWS = 10, 15, 16
-COUNT_ROWS = V_LOSS - V_COUNT
+V_LOSS, V_ROWS, V_COLS = 15, 16, D + 256
 
 COMMIT_WEIGHT = 0.25
 EPSILON = 1e-06
 SQRT_HALF = 0.5**0.5
 INV_ROOT_TAU = 0.3989422804014327
+LOG2_E = 1.4426950408889634
 HEAD_SCALE = HD**-0.5
 MESH = pl.DeviceIdType.MESH
 BF, F32 = jnp.bfloat16, jnp.float32
@@ -61,8 +61,13 @@
 
 
 def head_masks():
-    low = lax.broadcasted_iota(jnp.int32, (SEQ, 2 * HD), 1) < HD
-    return (lambda t: jnp.where(low, t, 0)), (lambda t: jnp.where(low, 0, t))
+    low = lax.broadcasted_iota(jnp.int32, (1, 2 * HD), 1) < HD
+    ones = low.astype(F32)
+    return ones.astype(BF), (1.0 - ones).astype(BF)
+
+
+def head_pair(ref, base, head):
+    return ref[:, base + head // 2 * 128 : base + (head // 2 + 1) * 128]
 
 
 def forward_image(x_ref, weights, l_ref, qkv_ref, pt_ref, slope_ref, h1_ref, out_ref, outb_ref, vt_ref, ot_ref):
@@ -75,17 +80,16 @@
         qkv_ref[:, j * D : (j + 1) * D] = matmul_nn(a, w_qkv[:, j * D : (j + 1) * D]).astype(BF)
     vt_ref[...] = qkv_ref[:, 2 * D : 3 * D].T
     masks = head_masks()
-    for pair in range(HEADS // 2):
-        q = qkv_ref[:, pair * 128 : (pair + 1) * 128]
-        k = qkv_ref[:, D + pair * 128 : D + (pair + 1) * 128]
-        for half in range(2):
-            head = 2 * pair + half
-            st = matmul_nt(masks[half](k), q)
-            e = jnp.exp((st - jnp.max(st, axis=0, keepdims=True)) * HEAD_SCALE)
-            pt = (e * (1.0 / column_sum(e))).astype(BF)
-            pt_ref[head] = pt
-            span = slice(head * HD, (head + 1) * HD)
-            ot_ref[span, :] = matmul_nn(vt_ref[span, :], pt).astype(BF)
+    scores = [
+        matmul_nt(head_pair(qkv_ref, D, head) * masks[head % 2], head_pair(qkv_ref, 0, head)) for head in range(HEADS)
+    ]
+    for head in range(HEADS):
+        st = scores[head]
+        e = jnp.exp2((st - jnp.max(st, axis=0, keepdims=True)) * (HEAD_SCALE * LOG2_E))
+        pt_ref[head] = (e * (1.0 / column_sum(e))).astype(BF)
+    for head in range(HEADS):
+        span = slice(head * HD, (head + 1) * HD)
+        ot_ref[span, :] = matmul_nn(vt_ref[span, :], pt_ref[head]).astype(BF)
     o = ot_ref[...].T
     l_ref[:, L_O:L_A] = o
     h1 = h + matmul_nn(o, w_out[...]) + out_bias[...]
@@ -113,53 +117,63 @@
 ):
     gains, shifts, w_qkv, w_out, out_bias, w_up, up_bias, w_down, down_bias = weights
     diff = out_ref[...] - other_ref[...].astype(F32)
-    vec_ref[V_LOSS : V_LOSS + 1, :] = column_sum(diff * diff) * scale
-    vec_ref[V_COUNT:V_LOSS, :] = jnp.zeros((COUNT_ROWS, D), F32)
+
+    def add(row, value):
+        vec_ref[row : row + 1, :D] += column_sum(value)
+
+    add(V_LOSS, diff * diff * scale)
     g = diff * scale + arrived_ref[...].astype(F32)
     gb = g.astype(BF)
     d_ref[:, D_GB:D_ALL] = gb
-    vec_ref[9:10, :] = column_sum(g)
+    add(9, g)
     db = jnp.zeros((SEQ, D), F32)
     for j in range(FF // FF_PIECE):
         span = slice(j * FF_PIECE, (j + 1) * FF_PIECE)
         du = (matmul_nt(gb, w_down[span, :]) * slope_ref[:, span].astype(F32)).astype(BF)
         d_ref[:, span] = du
-        vec_ref[5 + j : 6 + j, :] = column_sum(du.astype(F32))
+        add(5 + j, du.astype(F32))
         db = db + matmul_nt(du, w_up[:, span])
     s2, inv2 = layer_norm(h1_ref[...])
-    vec_ref[1:2, :] = column_sum(db * s2)
-    vec_ref[3:4, :] = column_sum(db)
+    add(1, db * s2)
+    add(3, db)
     dh1 = g + norm_back(db, s2, inv2, gains[1:2, :])
-    vec_ref[4:5, :] = column_sum(dh1)
+    add(4, dh1)
     gh = dh1.astype(BF)
     d_ref[:, D_GH:D_QKV] = gh
     do = matmul_nt(gh, w_out[...]).astype(BF)
     kt_ref[...] = qkv_ref[:, D : 2 * D].T
     masks = head_masks()
+
+    def do_pair(head):
+        return do[:, head // 2 * 128 : (head // 2 + 1) * 128]
+
+    dpts = [matmul_nt(head_pair(qkv_ref, 2 * D, head) * masks[head % 2], do_pair(head)) for head in range(HEADS)]
+
+    def both(parts, pair, make):
+        return matmul_nn(
+            jnp.concatenate(parts[2 * pair : 2 * pair + 2], axis=1),
+            jnp.concatenate([make(2 * pair) * masks[0], make(2 * pair) * masks[1]], axis=0),
+        )
+
+    base = D_QKV + D
     for pair in range(HEADS // 2):
-        lanes = slice(pair * 128, (pair + 1) * 128)
-        q = qkv_ref[:, lanes]
-        v = qkv_ref[:, 2 * D + pair * 128 : 2 * D + (pair + 1) * 128]
-        do_pair = do[:, lanes]
-        dk = dv = 0.0
-        for half in range(2):
-            head = 2 * pair + half
-            pt = pt_ref[head]
-            ptf = pt.astype(F32)
-            dv = dv + matmul_nn(pt, masks[half](do_pair))
-            dpt = matmul_nt(masks[half](v), do_pair)
-            dst = (ptf * (dpt - column_sum(dpt * ptf))).astype(BF)
-            dk = dk + matmul_nn(dst, masks[half](q))
-            span = slice(head * HD, (head + 1) * HD)
-            qt_ref[span, :] = (matmul_nn(kt_ref[span, :], dst) * HEAD_SCALE).astype(BF)
-        base = D_QKV + D + pair * 128
-        d_ref[:, base : base + 128] = (dk * HEAD_SCALE).astype(BF)
-        d_ref[:, base + D : base + D + 128] = dv.astype(BF)
+        dv = both([pt_ref[head] for head in range(HEADS)], pair, do_pair)
+        d_ref[:, base + D + pair * 128 : base + D + (pair + 1) * 128] = dv.astype(BF)
+    dsts = []
+    for head in range(HEADS):
+        ptf = pt_ref[head].astype(F32)
+        dsts.append((ptf * (dpts[head] - column_sum(dpts[head] * ptf))).astype(BF))
+    for pair in range(HEADS // 2):
+        dk = both(dsts, pair, lambda head: head_pair(qkv_ref, 0, head))
+        d_ref[:, base + pair * 128 : base + (pair + 1) * 128] = (dk * HEAD_SCALE).astype(BF)
+    for head in range(HEADS):
+        span = slice(head * HD, (head + 1) * HD)
+        qt_ref[span, :] = (matmul_nn(kt_ref[span, :], dsts[head]) * HEAD_SCALE).astype(BF)
     d_ref[:, D_QKV : D_QKV + D] = qt_ref[...].T
     da = matmul_nt(d_ref[:, D_QKV:D_GB], w_qkv[...])
     s1, inv1 = layer_norm(x_ref[...].astype(F32))
-    vec_ref[0:1, :] = column_sum(da * s1)
-    vec_ref[2:3, :] = column_sum(da)
+    add(0, da * s1)
+    add(2, da)
     dh = dh1 + norm_back(da, s1, inv1, gains[0:1, :])
     dh_ref[...] = dh
     dhb_ref[...] = dh.astype(BF)
@@ -229,6 +243,7 @@
         weight_refs = refs[:9]
         qkv_ref, pt_ref, slope_ref, h1_ref, vec_in = refs[9:14]
         d_ref, dh_ref, vec_out, dhb_ref, kt_ref, qt_ref = refs[-6:]
+        vec_out[...] = jnp.zeros_like(vec_out)
         backward_image(
             flags_ref[0], out_ref, other_ref, arrived_ref, x_ref, weight_refs, qkv_ref, pt_ref,
             slope_ref, h1_ref, d_ref, vec_out, dh_ref, dhb_ref, kt_ref, qt_ref,
@@ -249,16 +264,16 @@
                 pl.BlockSpec((HEADS, SEQ, SEQ), lambda i, which_ref: (which_ref[0], 0, 0)),
                 row_block(FF),
                 row_block(D),
-                whole(V_ROWS, D),
+                whole(V_ROWS, V_COLS),
             ]
             + [pl.BlockSpec(memory_space=pl.ANY)] * len(keep),
-            out_specs=[row_block(D_ALL), row_block(D), whole(V_ROWS, D), whole(SEQ, D)],
+            out_specs=[row_block(D_ALL), row_block(D), whole(V_ROWS, V_COLS), whole(SEQ, D)],
             scratch_shapes=[pltpu.VMEM((D, SEQ), BF), pltpu.VMEM((D, SEQ), BF)],
         ),
         out_shape=[
             jax.ShapeDtypeStruct((rows, D_ALL), BF),
             jax.ShapeDtypeStruct((rows, D), F32),
-            jax.ShapeDtypeStruct((V_ROWS, D), F32),
+            jax.ShapeDtypeStruct((V_ROWS, V_COLS), F32),
             jax.ShapeDtypeStruct((SEQ, D), BF),
         ],
         input_output_aliases={first_kept: 0, first_kept + 1: 1} if keep else {},
@@ -267,6 +282,244 @@
     )(which, flags, result, other, arrived, x, *weights, qkv, pt, slope, h1, vec, *keep)
 
 
+IMAGES = 4
+SHARD = 208
+
+
+def blocks_kernel(
+    patches_ref, targets_ref, ids_ref, codebook_ref, gains, shifts, w_qkv_ref, w_out_ref, out_bias, w_up_ref, up_bias,
+    w_down_ref, down_bias, result_ref, dh_ref, l_ref, d_ref, vec_ref,
+    w_qkv, w_out, w_up, w_down, shards, ids_col, x_buf, other_buf, arrived, outgoing,
+    qkv, pt, slope, h1, result, l_buf, d_buf, result_buf, dh_buf, vt, ot,
+    w_sem, in_sem, out_sem, sz, rz, sy, ry, sc, rc, sx, rx,
+):
+    section, dp = lax.axis_index("section"), lax.axis_index("dp")
+    core, y, z = dp % 2, (dp // 2) % 2, dp // 4
+    across = (section, dp + 1 - 2 * core)
+    along_y = (section, dp + 2 - 4 * y)
+    along_z = [(section, (z + k) % 4 * 4 + y * 2 + core) for k in (1, 2, 3)]
+    beside = (1 - section, dp)
+
+    big = ((w_qkv_ref, w_qkv), (w_out_ref, w_out), (w_up_ref, w_up), (w_down_ref, w_down))
+    loads = [pltpu.make_async_copy(src, dst, w_sem.at[i]) for i, (src, dst) in enumerate(big)]
+    for load in loads:
+        load.start()
+    patch_load = pltpu.make_async_copy(patches_ref, x_buf, in_sem)
+    target_load = pltpu.make_async_copy(targets_ref, other_buf, in_sem)
+
+    @pl.when(section == 0)
+    def _():
+        patch_load.start()
+
+    @pl.when(section == 1)
+    def _():
+        target_load.start()
+        arrived[...] = jnp.zeros_like(arrived)
+
+    rows_here = codebook_ref.shape[0]
+    shards[dp] = jnp.zeros((SHARD, D), BF)
+    shards[dp, :rows_here] = codebook_ref[...]
+
+    barrier = pltpu.get_barrier_semaphore()
+    for target in [across, along_y, beside] + along_z:
+        pl.semaphore_signal(barrier, inc=1, device_id=target, device_id_type=MESH)
+    pl.semaphore_wait(barrier, 6)
+
+    def move(place, send, recv, target):
+        return pltpu.make_async_remote_copy(
+            shards.at[place], shards.at[place], send, recv, device_id=target, device_id_type=MESH
+        )
+
+    near = [(z - k + 4) % 4 * 4 + y * 2 + core for k in range(4)]
+    far = [(z - k + 4) % 4 * 4 + (1 - y) * 2 + core for k in range(4)]
+
+    def send_z(k):
+        return move(dp, sz.at[k - 1], rz.at[k - 1], along_z[k - 1])
+
+    def got_z(k):
+        return move(near[k], sz.at[k - 1], rz.at[k - 1], along_z[k - 1])
+
+    def send_y(k):
+        return move(near[k], sy.at[k], ry.at[k], along_y)
+
+    def got_y(k):
+        return move(far[k], sy.at[k], ry.at[k], along_y)
+
+    def send_core(k):
+        return move(near[k] if k < 4 else far[k - 4], sc.at[k], rc.at[k], across)
+
+    def got_core(k):
+        place = near[k] if k < 4 else far[k - 4]
+        return move(place + 1 - 2 * core, sc.at[k], rc.at[k], across)
+
+    send_z(1).start()
+    send_y(0).start()
+    send_z(2).start()
+    send_z(3).start()
+    send_core(0).start()
+
+    vec_ref[...] = jnp.zeros_like(vec_ref)
+    ids_col[...] = jnp.broadcast_to(ids_ref[...], (128, IMAGES * SEQ)).T
+    lane = lax.broadcasted_iota(jnp.int32, (IMAGES * SEQ, 128), 1)
+
+    def pick(place, dest, first):
+        rel = ids_col[...] - place * rows_here
+        low = (rel == lane).astype(F32)
+        high = ((rel - 128 == lane) & (lane < rows_here - 128)).astype(F32)
+        one_hot = jnp.concatenate([low, high], axis=1)
+        vec_ref[pl.ds(place, 1), D:] = column_sum(one_hot)
+        one_hot = one_hot[:, :SHARD].astype(BF)
+        for i in range(IMAGES):
+            rows = matmul_nn(one_hot[i * SEQ : (i + 1) * SEQ], shards[place]).astype(BF)
+            dest[i] = rows if first else dest[i] + rows
+
+    def gather(dest):
+        pick(dp, dest, True)
+        for step in ("c0", "z1", "c1", "y0", "c4", "z2", "c2", "y1", "c5", "z3", "c3", "y2", "c6", "y3", "c7"):
+            k = int(step[1])
+            if step[0] == "z":
+                got_z(k).wait_recv()
+                send_y(k).start()
+                send_core(k).start()
+                place = near[k]
+            elif step[0] == "y":
+                got_y(k).wait_recv()
+                send_core(4 + k).start()
+                place = far[k]
+            else:
+                got_core(k).wait_recv()
+                place = (near[k] if k < 4 else far[k - 4]) + 1 - 2 * core
+            pick(place, dest, False)
+
+    @pl.when(section == 0)
+    def _():
+        gather(other_buf)
+        patch_load.wait()
+
+    @pl.when(section == 1)
+    def _():
+        gather(x_buf)
+        target_load.wait()
+
+    for k in range(1, 4):
+        send_z(k).wait_send()
+    for k in range(4):
+        send_y(k).wait_send()
+    for k in range(8):
+        send_core(k).wait_send()
+    for load in loads:
+        load.wait()
+
+    weights = (gains, shifts, w_qkv, w_out, out_bias, w_up, up_bias, w_down, down_bias)
+    scale = jnp.where(section == 0, COMMIT_WEIGHT, 1.0)
+
+    def rows_of(ref, image):
+        return ref.at[pl.ds(pl.multiple_of(image * SEQ, SEQ), SEQ)]
+
+    def stores(image, forward):
+        pairs = ((l_buf, l_ref), (result_buf, result_ref)) if forward else ((d_buf, d_ref), (dh_buf, dh_ref))
+        first = 0 if forward else 2
+        return [
+            pltpu.make_async_copy(src, rows_of(dst, image), out_sem.at[first + i]) for i, (src, dst) in enumerate(pairs)
+        ]
+
+    def cross(image):
+        return pltpu.make_async_remote_copy(
+            outgoing.at[image], arrived.at[image], sx.at[image], rx.at[image], device_id=beside, device_id_type=MESH
+        )
+
+    def step(i, carry):
+        even = i % 2 == 0
+        ahead = jnp.where(section == 1, even, (i == 0) | ((i % 2 == 1) & (i < 7)))
+
+        @pl.when(ahead)
+        def _():
+            image = (i + 1) // 2
+            slot = image % 2
+
+            @pl.when(image > 0)
+            def _():
+                for copy in stores(image - 1, True):
+                    copy.wait()
+
+            forward_image(
+                x_buf.at[image], weights, l_buf, qkv.at[slot], pt.at[slot], slope.at[slot], h1.at[slot],
+                result.at[slot], result_buf, vt, ot,
+            )
+            for copy in stores(image, True):
+                copy.start()
+
+        @pl.when(jnp.logical_not(ahead))
+        def _():
+            image = (i - 1) // 2
+            slot = image % 2
+
+            @pl.when(image > 0)
+            def _():
+                for copy in stores(image - 1, False):
+                    copy.wait()
+
+            @pl.when(section == 0)
+            def _():
+                cross(image).wait_recv()
+
+            backward_image(
+                scale, result.at[slot], other_buf.at[image], arrived.at[image], x_buf.at[image], weights,
+                qkv.at[slot], pt.at[slot], slope.at[slot], h1.at[slot], d_buf, vec_ref, dh_buf, outgoing.at[image], vt, ot,
+            )
+
+            @pl.when(section == 1)
+            def _():
+                cross(image).start()
+
+            for copy in stores(image, False):
+                copy.start()
+
+        return carry
+
+    lax.fori_loop(0, 2 * IMAGES, step, 0)
+    for forward in (True, False):
+        for copy in stores(IMAGES - 1, forward):
+            copy.wait()
+
+    @pl.when(section == 1)
+    def _():
+        for image in range(IMAGES):
+            cross(image).wait_send()
+
+
+def run_blocks(patches, targets, ids, codebook, weights):
+    dma = pltpu.SemaphoreType.DMA
+    vm = pltpu.VMEM
+    rows = IMAGES * SEQ
+    inside, outside = pl.BlockSpec(memory_space=pltpu.VMEM), pl.BlockSpec(memory_space=pl.ANY)
+    weight_places = [inside, inside, outside, outside, inside, outside, inside, outside, inside]
+    return pl.pallas_call(
+        blocks_kernel,
+        out_shape=[
+            jax.ShapeDtypeStruct((rows, D), BF),
+            jax.ShapeDtypeStruct((rows, D), F32),
+            jax.ShapeDtypeStruct((rows, L_ALL), BF),
+            jax.ShapeDtypeStruct((rows, D_ALL), BF),
+            jax.ShapeDtypeStruct((V_ROWS, V_COLS), F32),
+        ],
+        in_specs=[outside, outside, inside, inside] + weight_places,
+        out_specs=[outside] * 4 + [inside],
+        scratch_shapes=[
+            vm((D, QKV), BF), vm((D, D), BF), vm((D, FF), BF), vm((FF, D), BF),
+            vm((16, SHARD, D), BF), vm((rows, 128), jnp.int32),
+            vm((IMAGES, SEQ, D), BF), vm((IMAGES, SEQ, D), BF), vm((IMAGES, SEQ, D), BF), vm((IMAGES, SEQ, D), BF),
+            vm((2, SEQ, QKV), BF), vm((2, HEADS, SEQ, SEQ), BF), vm((2, SEQ, FF), BF), vm((2, SEQ, D), F32),
+            vm((2, SEQ, D), F32), vm((SEQ, L_ALL), BF), vm((SEQ, D_ALL), BF), vm((SEQ, D), BF), vm((SEQ, D), F32),
+            vm((D, SEQ), BF), vm((D, SEQ), BF),
+            dma((4,)), dma(()), dma((4,)), dma((3,)), dma((3,)), dma((4,)), dma((4,)), dma((8,)), dma((8,)),
+            dma((IMAGES,)), dma((IMAGES,)),
+        ],
+        compiler_params=pltpu.CompilerParams(collective_id=2, has_side_effects=True, vmem_limit_bytes=VMEM_BYTES),
+        name="blocks",
+    )(patches.reshape(IMAGES, SEQ, D), targets.reshape(IMAGES, SEQ, D), ids.reshape(1, rows), codebook, *weights)
+
+
 UNITS = 36
 PART = D // 16
 COLS = 256
@@ -275,8 +528,8 @@
 
 
 def reduce_kernel(
-    l_ref, d_ref, vec_ref, qkv_out, out_out, up_out, down_out, vec_out, side_out,
-    lt, lbuf, dbuf, acc_y, acc_z, acc_o, tx_c, rx_c, tx_y, rx_y, tx_z, rx_z, vec_tx, vec_c, vec_y, vec_z,
+    vocab, l_ref, d_ref, vec_ref, qkv_out, out_out, up_out, down_out, vec_out, hist_out, stats_out,
+    lt, lbuf, dbuf, acc_y, acc_z, acc_o, tx_c, rx_c, tx_y, rx_y, tx_z, rx_z, vec_tx, vec_c, vec_y, vec_z, side,
     lsem, dsem, sc, rc, sy, ry, sz, rz, sv, rv,
 ):
     sec, dp = lax.axis_index("section"), lax.axis_index("dp")
@@ -339,7 +592,7 @@
     vec_core = remote(vec_ref, vec_c, sv.at[0], rv.at[0], across)
     vec_along_y = remote(vec_tx, vec_y, sv.at[1], rv.at[1], along_y)
     vec_along_z = [remote(vec_z.at[z], vec_z.at[z], sv.at[2 + k], rv.at[2 + k], along_z[k]) for k in range(3)]
-    vec_beside = remote(vec_out.at[8:16], side_out, sv.at[5], rv.at[5], beside)
+    vec_beside = remote(vec_out.at[8:16], side, sv.at[5], rv.at[5], beside)
 
     load_left(0).start()
     load_right(0).start()
@@ -438,29 +691,45 @@
     lax.fori_loop(0, UNITS + LAG_OUT, step, 0)
     vec_beside.wait()
 
-
-def reduce_weights(l, d, vec):
+    def total(value):
+        return jnp.sum(jnp.sum(value, axis=1, keepdims=True), axis=0, keepdims=True)
+
+    tokens = 16 * l_ref.shape[0]
+    counts = vec_out[:, D:]
+    shares = counts * (1.0 / tokens)
+    entropy = -total(shares * jnp.log(jnp.where(counts > 0, shares, 1.0)))
+    used = total((counts > 0).astype(F32))
+    loss = total(vec_out[V_LOSS : V_LOSS + 1, :D]) + total(side[V_LOSS - 8 : V_LOSS - 7, :D])
+    lane = lax.broadcasted_iota(jnp.int32, (8, 128), 1)
+    last = jnp.where(lane == 1, used / vocab, jnp.exp(entropy) / vocab)
+    stats_out[...] = jnp.where(lane == 0, loss / (tokens * D), last)
+    hist_out[...] = vec_out[pl.ds(dp, 1), D:].astype(jnp.int32)
+
+
+def reduce_weights(l, d, vec, vocab):
     dma = pltpu.SemaphoreType.DMA
     vm = pltpu.VMEM
     return pl.pallas_call(
-        reduce_kernel,
+        functools.partial(reduce_kernel, vocab),
         out_shape=[
             jax.ShapeDtypeStruct((PART, QKV), F32),
             jax.ShapeDtypeStruct((PART, D), F32),
             jax.ShapeDtypeStruct((PART, FF), F32),
             jax.ShapeDtypeStruct((4 * PART, D), F32),
-            jax.ShapeDtypeStruct((V_ROWS, D), F32),
-            jax.ShapeDtypeStruct((8, D), F32),
+            jax.ShapeDtypeStruct((V_ROWS, V_COLS), F32),
+            jax.ShapeDtypeStruct((1, V_COLS - D), jnp.int32),
+            jax.ShapeDtypeStruct((8, 128), F32),
         ],
         in_specs=[pl.BlockSpec(memory_space=pl.ANY)] * 2 + [pl.BlockSpec(memory_space=pltpu.VMEM)],
-        out_specs=[pl.BlockSpec(memory_space=pltpu.VMEM)] * 6,
+        out_specs=[pl.BlockSpec(memory_space=pltpu.VMEM)] * 7,
         scratch_shapes=[
             vm((7, D, 4 * SEQ), BF), vm((2, 4 * SEQ, PIECE), BF), vm((2, 4 * SEQ, COLS), BF),
             vm((2, 8 * PART, COLS), F32), vm((4, 4 * PART, COLS), F32), vm((4, PART, COLS), F32),
             vm((UNITS, 8 * PART, COLS), BF), vm((UNITS, 8 * PART, COLS), BF),
             vm((UNITS, 4 * PART, COLS), BF), vm((UNITS, 4 * PART, COLS), BF),
             vm((UNITS, 3, PART, COLS), BF), vm((UNITS, 3, PART, COLS), BF),
-            vm((V_ROWS, D), F32), vm((V_ROWS, D), F32), vm((V_ROWS, D), F32), vm((4, V_ROWS, D), F32),
+            vm((V_ROWS, V_COLS), F32), vm((V_ROWS, V_COLS), F32), vm((V_ROWS, V_COLS), F32), vm((4, V_ROWS, V_COLS), F32),
+            vm((8, V_COLS), F32),
             dma((2,)), dma((2,)), dma((UNITS,)), dma((UNITS,)), dma((UNITS,)), dma((UNITS,)),
             dma((UNITS, 3)), dma((UNITS, 3)), dma((6,)), dma((6,)),
         ],
@@ -491,38 +760,30 @@
     vocab_all = vocab_local * dp_size
     total_tokens = rows * dp_size
 
-    shard_rows = lax.all_gather(codebook, "dp", axis=0, tiled=True)
-    chosen = jnp.take(shard_rows, jnp.clip(code_ids, 0, vocab_all - 1), axis=0)
-
-    l, qkv, pt, slope, h1, result, result_bf = block_forward(jnp.where(leading, patches, chosen), weights)
-
-    other = jnp.where(leading, chosen, targets)
-    d = dh = None
-    vec = jnp.zeros((V_ROWS, D), F32)
-    arrived = jnp.zeros((SEQ, D), BF)
-    x = jnp.where(leading, patches, chosen)
-    for moment in range(images + 1):
-        which = jnp.clip(moment - 1 + section, 0, images - 1).astype(jnp.int32)[None]
-        active = jnp.where(leading, moment >= 1, moment < images).astype(F32)
-        flags = jnp.stack([jnp.where(leading, COMMIT_WEIGHT, 1.0).astype(F32), active])
-        d, dh, vec, outgoing = block_backward(
-            which, flags, result, other, arrived, x, weights, qkv, pt, slope, h1, vec, d, dh
-        )
-        if moment < images:
-            arrived = lax.ppermute(outgoing, "section", [(1, 0)])
-
-    vocab_iota = lax.broadcasted_iota(jnp.int32, (1, vocab_all), 1)
-    counts = jnp.sum((code_ids[:, None] == vocab_iota).astype(F32), axis=0)
-    small = dp_size == 16 and vocab_all <= COUNT_ROWS * D and rows == 4 * SEQ
+    small = dp_size == 16 and vocab_local <= SHARD and rows == IMAGES * SEQ
     if small:
-        spread = jnp.pad(counts, (0, COUNT_ROWS * D - vocab_all)).reshape(COUNT_ROWS, D)
-        vec = lax.dynamic_update_slice(vec, spread, (V_COUNT, 0))
-        g_qkv, g_out, g_up, g_down, vec, side = reduce_weights(l, d, vec)
-        counts = vec[V_COUNT:V_LOSS].reshape(-1)[:vocab_all]
-        loss_all = jnp.sum(vec[V_LOSS]) + jnp.sum(side[V_LOSS - 8])
-        entropy_all, used_all = count_shares(counts, total_tokens)
-        hist_local = lax.dynamic_slice(counts, (dp * vocab_local,), (vocab_local,))
+        result_bf, dh, l, d, vec = run_blocks(patches, targets, code_ids, codebook, weights)
+        g_qkv, g_out, g_up, g_down, vec, hist, stats = reduce_weights(l, d, vec, vocab_all)
+        hist_local = hist[0, :vocab_local]
+        stats = stats[0, :3]
     else:
+        shard_rows = lax.all_gather(codebook, "dp", axis=0, tiled=True)
+        chosen = jnp.take(shard_rows, jnp.clip(code_ids, 0, vocab_all - 1), axis=0)
+        x = jnp.where(leading, patches, chosen)
+        l, qkv, pt, slope, h1, result, result_bf = block_forward(x, weights)
+        other = jnp.where(leading, chosen, targets)
+        d = dh = None
+        vec = jnp.zeros((V_ROWS, V_COLS), F32)
+        arrived = jnp.zeros((SEQ, D), BF)
+        for moment in range(images + 1):
+            which = jnp.clip(moment - 1 + section, 0, images - 1).astype(jnp.int32)[None]
+            active = jnp.where(leading, moment >= 1, moment < images).astype(F32)
+            flags = jnp.stack([jnp.where(leading, COMMIT_WEIGHT, 1.0).astype(F32), active])
+            d, dh, vec, outgoing = block_backward(
+                which, flags, result, other, arrived, x, weights, qkv, pt, slope, h1, vec, d, dh
+            )
+            if moment < images:
+                arrived = lax.ppermute(outgoing, "section", [(1, 0)])
         pairs = (
             (l[:, L_A:L_M], d[:, D_QKV:D_GB]),
             (l[:, L_O:L_A], d[:, D_GH:D_QKV]),
@@ -532,25 +793,30 @@
         g_qkv, g_out, g_up, g_down = (
             lax.psum_scatter(matmul_tn(left, right), "dp", scatter_dimension=0, tiled=True) for left, right in pairs
         )
+        vocab_iota = lax.broadcasted_iota(jnp.int32, (1, vocab_all), 1)
+        counts = jnp.sum((code_ids[:, None] == vocab_iota).astype(F32), axis=0)
         hist_local = lax.psum_scatter(counts, "dp", scatter_dimension=0, tiled=True)
         entropy_part, used_part = count_shares(hist_local, total_tokens)
+        hist_local = hist_local.astype(jnp.int32)
         vec = lax.psum(vec, "dp")
         entropy_all, used_all = lax.psum((entropy_part, used_part), "dp")
-        loss_all = lax.psum(jnp.sum(vec[V_LOSS]), "section")
-    stats = jnp.stack([loss_all / (total_tokens * width), used_all / vocab_all, jnp.exp(entropy_all) / vocab_all])
+        loss_all = lax.psum(jnp.sum(vec[V_LOSS, :D]), "section")
+        stats = jnp.stack(
+            [loss_all / (total_tokens * width), used_all / vocab_all, jnp.exp(entropy_all) / vocab_all]
+        )
     return (
         result_bf[None],
         dh[None],
-        vec[None, 0:2],
-        vec[None, 2:4],
+        vec[None, 0:2, :D],
+        vec[None, 2:4, :D],
         g_qkv[None],
         g_out[None],
-        vec[None, 4],
+        vec[None, 4, :D],
         g_up[None],
-        vec[5:9].reshape(1, FF),
+        vec[5:9, :D].reshape(1, FF),
         g_down[None],
-        vec[None, 9],
-        hist_local.astype(jnp.int32),
+        vec[None, 9, :D],
+        hist_local,
         stats,
     )
 

time: 393 us -> 242 us (0.62); the launches traced: 386 us -> 241 us
  waiting for transfers between devices: 97.1 us -> 0 us
  between operations: 17.4 us -> 0.7 us
  local copies, waits for them, and re-layouts: 24.4 us -> 11.9 us
  other arithmetic: 12.3 us -> 0 us
  starting transfers between devices: 6.09 us -> 0 us
    all_gather x1 -> x0, waiting for transfers between devices: 57.5 us -> none  [on_device(): shard_rows = lax.all_gather(codebook, 'dp', axis=0, tiled=True)]
    ppermute x4 -> x0, waiting for transfers between devices: 39 us -> none  [on_device(): arrived = lax.ppermute(outgoing, 'section', [(1, 0)])]
    gather x1 -> x0, local copies, waits for them, and re-layouts: 7.5 us -> none  [on_device(): chosen = jnp.take(shard_rows, jnp.clip(code_ids, 0, vocab_all - 1), axis=0)]
    ppermute x4 -> x0, starting transfers between devices: 6.05 us -> none  [on_device(): arrived = lax.ppermute(outgoing, 'section', [(1, 0)])]
    reduce_sum x3 -> x0, other arithmetic: 4.6 us -> none  [the longest x1 2.01 us: on_device(): loss_all = jnp.sum(vec[V_LOSS]) + jnp.sum(side[V_LOSS - 8])]
    unnamed x18 -> x23, local copies, waits for them, and re-layouts: 11.6 us -> 7.87 us
    pallas_call x7 -> x2, Pallas kernels: 228 us -> 229 us  [the longest x1 120 us: run_blocks(): pl.pallas_call(blocks_kernel, out_shape=[jax.ShapeDtypeStruct((rows, D),...]
  transfers between devices with their start and end apart: 5 -> 0, of which waited for: 5 -> 0; matrix products, arithmetic and copies ran while one was open for 1% -> 0% of each run, Pallas kernels for 0% -> 0%
where the time goes in v2:
time: 242 us; the launch traced here: 241 us
  Pallas kernels  229 us (95%)
  local copies, waits for them, and re-layouts  11.9 us (5%)
    pallas_call x1, Pallas kernels, run_blocks(): pl.pallas_call(blocks_kernel, out_shape=[jax.ShapeDtypeStruct((rows, D),...  120 us
    pallas_call x1, Pallas kernels, reduce_weights(): pl.pallas_call(functools.partial(reduce_kernel, vocab), out_shape=[jax.Sh...  109 us
    unnamed x23, local copies, waits for them, and re-layouts  7.87 us

profile of v2, /device:TPU:0, one launch (start us, length us, event | category | flops | bytes accessed | tf_op | source)
XLA Modules:
  0.0 241.4 jit_solution(16355747122270163634)
XLA Ops:
  0.6 120.2 %blocks.1 = (bf16[1024,768]{1,0:T(8,128)(2,1)}, f32[1024,768]{1,0:T(8,128)}, bf16[1024,5376]{1,0:T(8,128)(2,1)}, bf16[1024,6912]{1,0:T(8,128)(2,1)}, f32[16,1024]{1,0:T(8,128)}) custom-call(bf16[4,256,768]{2,1,0:T(8,128)(2,1)} %bitcast.31, bf16[4,256,768]{2,1,0:T(8,128)(2,1)} %bitcast.32, s32[1,1024]{1,0:T(1,128)} %bitcast.42, ...), custom_call_target="tpu_custom_call" | custom-call | tf_op jit(solution)/shard_map/blocks/pallas_call | solution.py:497
  120.8 0.0 copy-start.1
  120.8 108.6 %weight_grad_reduce.1 = (f32[48,2304]{1,0:T(8,128)}, f32[48,768]{1,0:T(8,128)}, f32[48,3072]{1,0:T(8,128)}, f32[192,768]{1,0:T(8,128)}, f32[16,1024]{1,0:T(8,128)}, /*index=5*/s32[1,256]{1,0:T(1,128)}, f32[8,128]{1,0:T(8,128)}) custom-call(bf16[1024,5376]{1,0:T(8,128)(2,1)} %get-tuple-element.27.l_ref, bf16[1024,6912]{1,0:T(8,128)(2,1)} %get-tuple-element.28.d_ref, ...), custom_call_target="tpu_custom_call" | custom-call | tf_op jit(solution)/shard_map/weight_grad_reduce/pallas_call | solution.py:712
  229.5 0.0 copy-start
  229.5 1.5 slice_bitcast_fusion.1
  231.0 1.3 fusion
  232.3 0.8 slice_bitcast_fusion
  233.1 0.6 copy.26
  233.7 1.2 slice_bitcast_fusion.3
  234.9 0.0 copy-done.1
  234.9 1.1 copy.34
  236.1 0.0 copy-done
  236.1 0.0 copy-start.4
  236.1 0.0 copy-start.5
  236.1 0.0 copy-start.3
  236.1 0.0 copy-start.2
  236.1 1.7 copy.35
  237.8 0.0 copy-done.4
  237.8 0.0 copy-start.6
  237.8 0.8 copy.36
  238.5 0.0 copy-done.5
  238.5 0.7 copy.37
  239.2 0.0 copy-done.3
  239.2 0.8 copy.38
  240.0 0.0 copy-done.2
  240.0 0.8 copy.39
  240.8 0.0 copy-done.6
  240.8 0.6 copy.40
Async XLA Ops:
  120.8 114.1 %copy-start.1 = (bf16[1024,768]{1,0:T(8,128)(2,1)S(1)}, bf16[1024,768]{1,0:T(8,128)(2,1)}, u32[]{:S(2)}) copy-start(bf16[1024,768]{1,0:T(8,128)(2,1)} %get-tuple-element.25) | copy-start | bytes 4718596
  229.5 6.6 %copy-start = (f32[1024,768]{1,0:T(8,128)S(1)}, f32[1024,768]{1,0:T(8,128)}, u32[]{:S(2)}) copy-start(f32[1024,768]{1,0:T(8,128)} %get-tuple-element.26) | copy-start | bytes 9437188
  236.1 1.7 copy-start.4
  236.1 2.5 %copy-start.5 = (f32[48,768]{1,0:T(8,128)S(1)}, f32[48,768]{1,0:T(8,128)}, u32[]{:S(2)}) copy-start(f32[48,768]{1,0:T(8,128)} %get-tuple-element.32) | copy-start | bytes 442372
  236.1 3.1 %copy-start.3 = (f32[48,3072]{1,0:T(8,128)S(1)}, f32[48,3072]{1,0:T(8,128)}, u32[]{:S(2)}) copy-start(f32[48,3072]{1,0:T(8,128)} %get-tuple-element.33) | copy-start | bytes 1769476
  236.1 3.9 %copy-start.2 = (f32[192,768]{1,0:T(8,128)S(1)}, f32[192,768]{1,0:T(8,128)}, u32[]{:S(2)}) copy-start(f32[192,768]{1,0:T(8,128)} %get-tuple-element.34) | copy-start | bytes 1769476
  237.8 3.1 %copy-start.6 = (s32[1,256]{1,0:T(1,128)S(1)}, s32[1,256]{1,0:T(1,128)}, u32[]{:S(2)}) copy-start(s32[1,256]{1,0:T(1,128)} %get-tuple-element.35) | copy-start | bytes 3076

commit v3 on v2

--- a/solution.py
+++ b/solution.py
@@ -16,7 +16,7 @@
 QKV = 3 * D
 L_O, L_A, L_M, L_ALL = D, 2 * D, 3 * D, 3 * D + FF
 D_GH, D_QKV, D_GB, D_ALL = FF, FF + D, FF + D + QKV, FF + D + QKV + D
-V_LOSS, V_ROWS, V_COLS = 15, 16, D + 256
+V_SIDE, V_LOSS, V_ROWS, V_COLS = 14, 15, 16, D + 256
 
 COMMIT_WEIGHT = 0.25
 EPSILON = 1e-06
@@ -112,7 +112,7 @@
 
 
 def backward_image(
-    scale, out_ref, other_ref, arrived_ref, x_ref, weights, qkv_ref, pt_ref, slope_ref, h1_ref,
+    scale, receives, out_ref, other_ref, arrived_ref, x_ref, weights, qkv_ref, pt_ref, slope_ref, h1_ref,
     d_ref, vec_ref, dh_ref, dhb_ref, kt_ref, qt_ref,
 ):
     gains, shifts, w_qkv, w_out, out_bias, w_up, up_bias, w_down, down_bias = weights
@@ -121,8 +121,7 @@
     def add(row, value):
         vec_ref[row : row + 1, :D] += column_sum(value)
 
-    add(V_LOSS, diff * diff * scale)
-    g = diff * scale + arrived_ref[...].astype(F32)
+    g = diff * scale + jnp.where(receives, arrived_ref[...].astype(F32), 0.0)
     gb = g.astype(BF)
     d_ref[:, D_GB:D_ALL] = gb
     add(9, g)
@@ -245,9 +244,11 @@
         d_ref, dh_ref, vec_out, dhb_ref, kt_ref, qt_ref = refs[-6:]
         vec_out[...] = jnp.zeros_like(vec_out)
         backward_image(
-            flags_ref[0], out_ref, other_ref, arrived_ref, x_ref, weight_refs, qkv_ref, pt_ref,
+            flags_ref[0], flags_ref[2] > 0, out_ref, other_ref, arrived_ref, x_ref, weight_refs, qkv_ref, pt_ref,
             slope_ref, h1_ref, d_ref, vec_out, dh_ref, dhb_ref, kt_ref, qt_ref,
         )
+        diff = out_ref[...] - other_ref[...].astype(F32)
+        vec_out[V_LOSS : V_LOSS + 1, :D] = column_sum(diff * diff * flags_ref[0])
         vec_out[...] = vec_in[...] + vec_out[...] * flags_ref[1]
 
     keep = [] if d is None else [d, dh]
@@ -284,14 +285,16 @@
 
 IMAGES = 4
 SHARD = 208
+SLICES = 3
+SLICE = D // SLICES
 
 
 def blocks_kernel(
     patches_ref, targets_ref, ids_ref, codebook_ref, gains, shifts, w_qkv_ref, w_out_ref, out_bias, w_up_ref, up_bias,
     w_down_ref, down_bias, result_ref, dh_ref, l_ref, d_ref, vec_ref,
-    w_qkv, w_out, w_up, w_down, shards, ids_col, x_buf, other_buf, arrived, outgoing,
+    w_qkv, w_out, w_up, w_down, shards, ids_col, rows_buf, crossing, loss_buf, loss_side,
     qkv, pt, slope, h1, result, l_buf, d_buf, result_buf, dh_buf, vt, ot,
-    w_sem, in_sem, out_sem, sz, rz, sy, ry, sc, rc, sx, rx,
+    w_sem, in_sem, out_sem, r_in, s_z, s_y, s_x, s_c, r_c, s_loss, r_loss, sx, rx,
 ):
     section, dp = lax.axis_index("section"), lax.axis_index("dp")
     core, y, z = dp % 2, (dp // 2) % 2, dp // 4
@@ -304,8 +307,8 @@
     loads = [pltpu.make_async_copy(src, dst, w_sem.at[i]) for i, (src, dst) in enumerate(big)]
     for load in loads:
         load.start()
-    patch_load = pltpu.make_async_copy(patches_ref, x_buf, in_sem)
-    target_load = pltpu.make_async_copy(targets_ref, other_buf, in_sem)
+    patch_load = pltpu.make_async_copy(patches_ref, rows_buf.at[0], in_sem)
+    target_load = pltpu.make_async_copy(targets_ref, rows_buf.at[1], in_sem)
 
     @pl.when(section == 0)
     def _():
@@ -314,55 +317,76 @@
     @pl.when(section == 1)
     def _():
         target_load.start()
-        arrived[...] = jnp.zeros_like(arrived)
 
     rows_here = codebook_ref.shape[0]
-    shards[dp] = jnp.zeros((SHARD, D), BF)
-    shards[dp, :rows_here] = codebook_ref[...]
+    for p in range(SLICES):
+        shards[dp, p] = jnp.zeros((SHARD, SLICE), BF)
+        shards[dp, p, :rows_here] = codebook_ref[:, p * SLICE : (p + 1) * SLICE]
 
     barrier = pltpu.get_barrier_semaphore()
     for target in [across, along_y, beside] + along_z:
         pl.semaphore_signal(barrier, inc=1, device_id=target, device_id_type=MESH)
     pl.semaphore_wait(barrier, 6)
 
-    def move(place, send, recv, target):
-        return pltpu.make_async_remote_copy(
-            shards.at[place], shards.at[place], send, recv, device_id=target, device_id_type=MESH
-        )
-
-    near = [(z - k + 4) % 4 * 4 + y * 2 + core for k in range(4)]
-    far = [(z - k + 4) % 4 * 4 + (1 - y) * 2 + core for k in range(4)]
-
-    def send_z(k):
-        return move(dp, sz.at[k - 1], rz.at[k - 1], along_z[k - 1])
-
-    def got_z(k):
-        return move(near[k], sz.at[k - 1], rz.at[k - 1], along_z[k - 1])
-
-    def send_y(k):
-        return move(near[k], sy.at[k], ry.at[k], along_y)
-
-    def got_y(k):
-        return move(far[k], sy.at[k], ry.at[k], along_y)
-
-    def send_core(k):
-        return move(near[k] if k < 4 else far[k - 4], sc.at[k], rc.at[k], across)
-
-    def got_core(k):
-        place = near[k] if k < 4 else far[k - 4]
-        return move(place + 1 - 2 * core, sc.at[k], rc.at[k], across)
-
-    send_z(1).start()
-    send_y(0).start()
-    send_z(2).start()
-    send_z(3).start()
-    send_core(0).start()
+    home = section == core
+    corner = (z == 0) | (z == 3)
+    near_1 = jnp.where(z == 0, 3, 1)
+    near_2 = jnp.where(corner, 2, 3)
+    near_3 = jnp.where(z == 0, 1, jnp.where(z == 3, 3, 2))
+    def place_of(number):
+        return (z - number % 4 + 4) % 4 * 4 + (y + number // 4) % 2 * 2 + core
+
+    def move(place, p, send, recv, target):
+        part = shards.at[place, p]
+        return pltpu.make_async_remote_copy(part, part, send.at[p], recv.at[p], device_id=target, device_id_type=MESH)
+
+    def send_z(order, place, up, p):
+        towards = jnp.where(up, z + 1, z - 1)
+        number = (towards - place // 4 + 4) % 4
+        return move(place, p, s_z.at[order], r_in.at[number], (section, towards * 4 + y * 2 + core))
+
+    def pass_on(e, p):
+        up = (e == 1) | ((e == 5) & (z == 2))
+        return send_z((e + 3) // 2, place_of(number_at(e)), up, p)
+
+    def send_y(order, number, p):
+        return move(place_of(number), p, s_y.at[order], r_in.at[4 + number], along_y)
+
+    def send_x(order, number, p):
+        return move(place_of(number), p, s_x.at[order], r_in.at[number], beside)
+
+    def send_core(order, number, p):
+        return move(place_of(number), p, s_c.at[order], r_c.at[order], across)
+
+    pieces = range(SLICES)
+
+    def number_at(e):
+        pairs = ((1, near_1), (2, 4), (3, near_2), (4, 4 + near_1), (5, near_3), (6, 4 + near_2), (7, 4 + near_3))
+        number = 0
+        for at, value in pairs:
+            number = jnp.where(e == at, value, number)
+        return number
+
+    for p in pieces:
+
+        @pl.when(z < 3)
+        def _():
+            send_z(0, dp, True, p).start()
+
+        @pl.when(z > 0)
+        def _():
+            send_z(1, dp, False, p).start()
+
+        send_y(0, 0, p).start()
+        send_core(0, 0, p).start()
 
     vec_ref[...] = jnp.zeros_like(vec_ref)
+    loss_buf[...] = jnp.zeros_like(loss_buf)
     ids_col[...] = jnp.broadcast_to(ids_ref[...], (128, IMAGES * SEQ)).T
     lane = lax.broadcasted_iota(jnp.int32, (IMAGES * SEQ, 128), 1)
-
-    def pick(place, dest, first):
+    dest = 1 - section
+
+    def pick(place, first=False):
         rel = ids_col[...] - place * rows_here
         low = (rel == lane).astype(F32)
         high = ((rel - 128 == lane) & (lane < rows_here - 128)).astype(F32)
@@ -370,45 +394,83 @@
         vec_ref[pl.ds(place, 1), D:] = column_sum(one_hot)
         one_hot = one_hot[:, :SHARD].astype(BF)
         for i in range(IMAGES):
-            rows = matmul_nn(one_hot[i * SEQ : (i + 1) * SEQ], shards[place]).astype(BF)
-            dest[i] = rows if first else dest[i] + rows
-
-    def gather(dest):
-        pick(dp, dest, True)
-        for step in ("c0", "z1", "c1", "y0", "c4", "z2", "c2", "y1", "c5", "z3", "c3", "y2", "c6", "y3", "c7"):
-            k = int(step[1])
-            if step[0] == "z":
-                got_z(k).wait_recv()
-                send_y(k).start()
-                send_core(k).start()
-                place = near[k]
-            elif step[0] == "y":
-                got_y(k).wait_recv()
-                send_core(4 + k).start()
-                place = far[k]
-            else:
-                got_core(k).wait_recv()
-                place = (near[k] if k < 4 else far[k - 4]) + 1 - 2 * core
-            pick(place, dest, False)
+            for p in pieces:
+                rows = matmul_nn(one_hot[i * SEQ : (i + 1) * SEQ], shards[place, p]).astype(BF)
+                cols = slice(p * SLICE, (p + 1) * SLICE)
+                rows_buf[dest, i, :, cols] = rows if first else rows_buf[dest, i, :, cols] + rows
+
+    def pick_core(e):
+        for p in pieces:
+            send_core(e, number_at(e), p).wait_recv()
+        pick(place_of(number_at(e)) + 1 - 2 * core)
+
+    def event(e, carry):
+        number = number_at(e)
+        near = (e == 1) | (e == 3) | (e == 5)
+        for p in pieces:
+            move(place_of(number), p, s_c.at[e], r_in.at[number], across).wait_recv()
+
+            @pl.when(home & near & jnp.logical_not(corner))
+            def _():
+                pass_on(e, p).start()
+
+            @pl.when(home & near)
+            def _():
+                send_y((e + 1) // 2, number, p).start()
+
+            @pl.when(home & ((e >= 4) | ((e == 3) & corner)))
+            def _():
+                send_x(e - 3, number, p).start()
+
+            send_core(e, number, p).start()
+        pick(place_of(number))
+        pick_core(e - 1)
+        return carry
+
+    pick(dp, True)
+    lax.fori_loop(1, 8, event, 0)
+    pick_core(7)
+
+    for p in pieces:
+
+        @pl.when(z < 3)
+        def _():
+            send_z(0, dp, True, p).wait_send()
+
+        @pl.when(z > 0)
+        def _():
+            send_z(1, dp, False, p).wait_send()
+
+        send_y(0, 0, p).wait_send()
+
+        @pl.when(home)
+        def _():
+            for order in (1, 2, 3):
+                send_y(order, number_at(2 * order - 1), p).wait_send()
+            for e in (4, 5, 6, 7):
+                send_x(e - 3, number_at(e), p).wait_send()
+
+        @pl.when(home & jnp.logical_not(corner))
+        def _():
+            for e in (1, 3, 5):
+                pass_on(e, p).wait_send()
+
+        @pl.when(home & corner)
+        def _():
+            send_x(0, number_at(3), p).wait_send()
+
+        for e in range(8):
+            send_core(e, number_at(e), p).wait_send()
+    for load in loads:
+        load.wait()
 
     @pl.when(section == 0)
     def _():
-        gather(other_buf)
         patch_load.wait()
 
     @pl.when(section == 1)
     def _():
-        gather(x_buf)
         target_load.wait()
-
-    for k in range(1, 4):
-        send_z(k).wait_send()
-    for k in range(4):
-        send_y(k).wait_send()
-    for k in range(8):
-        send_core(k).wait_send()
-    for load in loads:
-        load.wait()
 
     weights = (gains, shifts, w_qkv, w_out, out_bias, w_up, up_bias, w_down, down_bias)
     scale = jnp.where(section == 0, COMMIT_WEIGHT, 1.0)
@@ -425,8 +487,10 @@
 
     def cross(image):
         return pltpu.make_async_remote_copy(
-            outgoing.at[image], arrived.at[image], sx.at[image], rx.at[image], device_id=beside, device_id_type=MESH
+            crossing.at[image], crossing.at[image], sx.at[image], rx.at[image], device_id=beside, device_id_type=MESH
         )
+
+    trade = pltpu.make_async_remote_copy(loss_buf, loss_side, s_loss, r_loss, device_id=beside, device_id_type=MESH)
 
     def step(i, carry):
         even = i % 2 == 0
@@ -443,12 +507,18 @@
                     copy.wait()
 
             forward_image(
-                x_buf.at[image], weights, l_buf, qkv.at[slot], pt.at[slot], slope.at[slot], h1.at[slot],
+                rows_buf.at[0, image], weights, l_buf, qkv.at[slot], pt.at[slot], slope.at[slot], h1.at[slot],
                 result.at[slot], result_buf, vt, ot,
             )
+            diff = result[slot] - rows_buf[1, image].astype(F32)
+            loss_buf[0:1, :] += column_sum(diff * diff * scale)
             for copy in stores(image, True):
                 copy.start()
 
+            @pl.when(image == IMAGES - 1)
+            def _():
+                trade.start()
+
         @pl.when(jnp.logical_not(ahead))
         def _():
             image = (i - 1) // 2
@@ -464,8 +534,9 @@
                 cross(image).wait_recv()
 
             backward_image(
-                scale, result.at[slot], other_buf.at[image], arrived.at[image], x_buf.at[image], weights,
-                qkv.at[slot], pt.at[slot], slope.at[slot], h1.at[slot], d_buf, vec_ref, dh_buf, outgoing.at[image], vt, ot,
+                scale, section == 0, result.at[slot], rows_buf.at[1, image], crossing.at[image], rows_buf.at[0, image], weights,
+                qkv.at[slot], pt.at[slot], slope.at[slot], h1.at[slot], d_buf, vec_ref, dh_buf, crossing.at[image],
+                vt, ot,
             )
 
             @pl.when(section == 1)
@@ -486,6 +557,10 @@
     def _():
         for image in range(IMAGES):
             cross(image).wait_send()
+
+    trade.wait()
+    vec_ref[V_LOSS : V_LOSS + 1, :D] = loss_buf[0:1, :]
+    vec_ref[V_SIDE : V_SIDE + 1, :D] = loss_side[0:1, :]
 
 
 def run_blocks(patches, targets, ids, codebook, weights):
@@ -507,12 +582,13 @@
         out_specs=[outside] * 4 + [inside],
         scratch_shapes=[
             vm((D, QKV), BF), vm((D, D), BF), vm((D, FF), BF), vm((FF, D), BF),
-            vm((16, SHARD, D), BF), vm((rows, 128), jnp.int32),
-            vm((IMAGES, SEQ, D), BF), vm((IMAGES, SEQ, D), BF), vm((IMAGES, SEQ, D), BF), vm((IMAGES, SEQ, D), BF),
+            vm((16, SLICES, SHARD, SLICE), BF), vm((rows, 128), jnp.int32),
+            vm((2, IMAGES, SEQ, D), BF), vm((IMAGES, SEQ, D), BF), vm((8, D), F32), vm((8, D), F32),
             vm((2, SEQ, QKV), BF), vm((2, HEADS, SEQ, SEQ), BF), vm((2, SEQ, FF), BF), vm((2, SEQ, D), F32),
             vm((2, SEQ, D), F32), vm((SEQ, L_ALL), BF), vm((SEQ, D_ALL), BF), vm((SEQ, D), BF), vm((SEQ, D), F32),
             vm((D, SEQ), BF), vm((D, SEQ), BF),
-            dma((4,)), dma(()), dma((4,)), dma((3,)), dma((3,)), dma((4,)), dma((4,)), dma((8,)), dma((8,)),
+            dma((4,)), dma(()), dma((4,)), dma((8, SLICES)), dma((5, SLICES)),
+            dma((4, SLICES)), dma((5, SLICES)), dma((8, SLICES)), dma((8, SLICES)), dma(()), dma(()),
             dma((IMAGES,)), dma((IMAGES,)),
         ],
         compiler_params=pltpu.CompilerParams(collective_id=2, has_side_effects=True, vmem_limit_bytes=VMEM_BYTES),
@@ -523,148 +599,273 @@
 UNITS = 36
 PART = D // 16
 COLS = 256
-LAG_Y, LAG_Z, LAG_OUT = 1, 3, 5
-PIECE = 384
+LAG_Y, LAG_Z, HOP = 1, 4, 3
+LAG_OUT = LAG_Z + 3 * HOP
+BLOCKS = D_ALL // COLS
+FIRST_DOWN = 24
+EVERY, EARLY = 6, UNITS // 6
+LAG_LAST = 3
+RING = 16
 
 
 def reduce_kernel(
     vocab, l_ref, d_ref, vec_ref, qkv_out, out_out, up_out, down_out, vec_out, hist_out, stats_out,
-    lt, lbuf, dbuf, acc_y, acc_z, acc_o, tx_c, rx_c, tx_y, rx_y, tx_z, rx_z, vec_tx, vec_c, vec_y, vec_z, side,
-    lsem, dsem, sc, rc, sy, ry, sz, rz, sv, rv,
+    left, right, product, acc_y, acc_z, tx_c, rx_c, tx_y, rx_y, tx_up, rx_up, tx_dn, rx_dn,
+    acc_e, tx_eu, rx_eu, tx_ed, rx_ed, acc_l, tx_l, rx_l, vec_tx, vec_c, vec_y, vec_z,
+    lsem, dsem, sc, rc, sy, ry, s_up, r_up, s_dn, r_dn,
+    s_eu, r_eu, s_ed, r_ed, s_l, r_l, sv, rv,
 ):
     sec, dp = lax.axis_index("section"), lax.axis_index("dp")
     core, y, z = dp % 2, (dp // 2) % 2, dp // 4
     across = (sec, dp + 1 - 2 * core)
     along_y = (sec, dp + 2 - 4 * y)
     along_z = [(sec, (z + k) % 4 * 4 + y * 2 + core) for k in (1, 2, 3)]
-    beside = (1 - sec, dp)
+    above, below = (sec, jnp.minimum(dp + 4, 12 + dp % 4)), (sec, jnp.maximum(dp - 4, dp % 4))
+
+    lefts = [pltpu.make_async_copy(l_ref.at[:, i * D : (i + 1) * D], left.at[i], lsem.at[i]) for i in range(7)]
+
+    def load_right(n):
+        cols = pl.ds(pl.multiple_of(n * COLS, COLS), COLS)
+        return pltpu.make_async_copy(d_ref.at[:, cols], right.at[n % 2], dsem.at[n % 2])
+
+    lefts[0].start()
+    load_right(0).start()
+
     barrier = pltpu.get_barrier_semaphore()
-    for target in [across, along_y, beside] + along_z:
+    for target in [across, along_y] + along_z:
         pl.semaphore_signal(barrier, inc=1, device_id=target, device_id_type=MESH)
-    pl.semaphore_wait(barrier, 6)
+    pl.semaphore_wait(barrier, 5)
 
     def remote(src, dst, send, recv, target):
         return pltpu.make_async_remote_copy(src, dst, send, recv, device_id=target, device_id_type=MESH)
 
-    def spot(g):
-        return ((g % 2 + core) % 2) * 8 + (((g // 2) % 2 + y) % 2) * 4 + (g // 4 - z + 4) % 4
-
-    def aligned(x, n):
-        return pl.multiple_of(x, n)
-
-    def load_left(i):
-        return pltpu.make_async_copy(l_ref.at[:, pl.ds(aligned(i * PIECE, PIECE), PIECE)], lbuf.at[i % 2], lsem.at[i % 2])
-
-    def load_right(u):
-        d = jnp.where(u < 24, u, 24 + u % 3)
-        return pltpu.make_async_copy(d_ref.at[:, pl.ds(aligned(d * COLS, COLS), COLS)], dbuf.at[u % 2], dsem.at[u % 2])
-
-    def prepare(i):
-        load_left(i).wait()
-
-        @pl.when(i < 13)
-        def _():
-            load_left(i + 1).start()
-
-        turned = lbuf[i % 2].T
-
-        @pl.when(i < 6)
-        def _():
-            for k in range(8):
-                place = spot((i % 2) * 8 + k) * PART
-                lt[i // 2, pl.ds(aligned(place, PART), PART), :] = turned[k * PART : (k + 1) * PART]
-
-        @pl.when(i >= 6)
-        def _():
-            for k in range(8):
-                place = spot((i - 6) * 2 + k // 4) * PART
-                lt[3 + k % 4, pl.ds(aligned(place, PART), PART), :] = turned[k * PART : (k + 1) * PART]
-
     def send_core(u):
-        return remote(tx_c.at[u], rx_c.at[u], sc.at[u], rc.at[u], across)
+        return remote(tx_c.at[u % 2], rx_c.at[u], sc.at[u % 2], rc.at[u], across)
 
     def send_y(u):
-        return remote(tx_y.at[u], rx_y.at[u], sy.at[u], ry.at[u], along_y)
-
-    def send_z(u, k):
-        return remote(tx_z.at[u, k], rx_z.at[u, k], sz.at[u, k], rz.at[u, k], along_z[k])
+        return remote(tx_y.at[u % RING], rx_y.at[u], sy.at[u % RING], ry.at[u], along_y)
+
+    def send_up(u, d):
+        return remote(tx_up.at[u % RING, d], rx_up.at[u, d], s_up.at[u % RING, d], r_up.at[u, d], above)
+
+    def send_dn(u, d):
+        return remote(tx_dn.at[u % RING, d], rx_dn.at[u, d], s_dn.at[u % RING, d], r_dn.at[u, d], below)
+
+    def early_up(u, h, d):
+        return remote(tx_eu.at[u, h, d], rx_eu.at[u, h, d], s_eu.at[u, h, d], r_eu.at[u, h, d], above)
+
+    def early_dn(u, h, d):
+        return remote(tx_ed.at[u, h, d], rx_ed.at[u, h, d], s_ed.at[u, h, d], r_ed.at[u, h, d], below)
+
+    def send_last(u):
+        return remote(tx_l.at[u], rx_l.at[u], s_l.at[u], r_l.at[u], along_y)
+
+    def is_early(u):
+        return u % EVERY == 2
+
+    def valid(u):
+        return (u >= 0) & (u < UNITS)
+
+    def climb(quarter, tx, rx, send):
+        for d in range(3):
+
+            @pl.when((z > 0) & (d + 1 >= z))
+            def _():
+                send(d).wait_recv()
+
+            @pl.when(d + 1 > z)
+            def _():
+                got = jnp.where(z > 0, rx[d].astype(F32), 0.0)
+                tx[d] = (quarter(d + 1) + got).astype(BF)
+                send(d).start()
+
+    def sink(quarter, tx, rx, send):
+        for d in range(3):
+
+            @pl.when((z < 3) & (d <= z))
+            def _():
+                send(d).wait_recv()
+
+            @pl.when(d < z)
+            def _():
+                got = jnp.where(z < 3, rx[d].astype(F32), 0.0)
+                tx[d] = (quarter(d) + got).astype(BF)
+                send(d).start()
+
+    def settle(quarter_own, rx_above, rx_below, up, dn):
+        for d in range(3):
+
+            @pl.when(d + 1 > z)
+            def _():
+                up(d).wait_send()
+
+            @pl.when(d < z)
+            def _():
+                dn(d).wait_send()
+
+        from_below = jnp.where(z > 0, rx_above[jnp.maximum(z - 1, 0)].astype(F32), 0.0)
+        from_above = jnp.where(z < 3, rx_below[jnp.minimum(z, 2)].astype(F32), 0.0)
+        return quarter_own + from_below + from_above
 
     vec_core = remote(vec_ref, vec_c, sv.at[0], rv.at[0], across)
     vec_along_y = remote(vec_tx, vec_y, sv.at[1], rv.at[1], along_y)
     vec_along_z = [remote(vec_z.at[z], vec_z.at[z], sv.at[2 + k], rv.at[2 + k], along_z[k]) for k in range(3)]
-    vec_beside = remote(vec_out.at[8:16], side, sv.at[5], rv.at[5], beside)
-
-    load_left(0).start()
-    load_right(0).start()
-    prepare(0)
-    prepare(1)
     vec_core.start()
+
+    def multiply(u):
+        down = u >= FIRST_DOWN
+        n = jnp.where(down, FIRST_DOWN + (u - FIRST_DOWN) // 4, u)
+        fresh = jnp.logical_not(down) | (u % 4 == 0)
+
+        @pl.when(fresh & (n + 1 < BLOCKS))
+        def _():
+            load_right(n + 1).start()
+
+        @pl.when(fresh)
+        def _():
+            load_right(n).wait()
+
+        @pl.when(u == 1)
+        def _():
+            for load in lefts[1:]:
+                load.start()
+
+        for i, first in enumerate((0, 12, 15, FIRST_DOWN)):
+
+            @pl.when(u == first)
+            def _():
+                for load in lefts[i : i + 1] if i < 3 else lefts[3:]:
+                    load.wait()
+
+        @pl.when(jnp.logical_not(down))
+        def _():
+            which = jnp.where(u < 12, 0, jnp.where(u < 15, 1, 2))
+            product[:D] = matmul_tn(left[which], right[n % 2])
+
+        @pl.when(down & fresh)
+        def _():
+            for i in range(4):
+                product[i * D : (i + 1) * D] = matmul_tn(left[3 + i], right[n % 2])
+
+        def rows_for(place):
+            owner = place % 4 * 4 + (y + place // 4 % 2) % 2 * 2 + (core + place // 8) % 2
+            row = jnp.where(down, owner * (4 * PART) + u % 4 * PART, owner * PART)
+            return product[pl.ds(pl.multiple_of(row, PART), PART), :]
+
+        for place in range(8):
+            tx_c[u % 2, place * PART : (place + 1) * PART] = rows_for(8 + place).astype(BF)
+        send_core(u).start()
+        for place in range(8):
+            acc_y[u % 2, place * PART : (place + 1) * PART] = rows_for(place)
 
     def step(i, carry):
         @pl.when(i < UNITS)
         def _():
-            u = i
-
-            @pl.when(u + 1 < UNITS)
-            def _():
-                load_right(u + 1).start()
-
-            load_right(u).wait()
-            l = jnp.where(u < 12, 0, jnp.where(u < 15, 1, jnp.where(u < 24, 2, 3 + (u - 24) // 3)))
-            product = matmul_nn(lt[l], dbuf[u % 2])
-            acc_y[u % 2] = product[: 8 * PART]
-            tx_c[u] = product[8 * PART :].astype(BF)
-            send_core(u).start()
+            multiply(i)
 
         @pl.when((i >= LAG_Y) & (i < UNITS + LAG_Y))
         def _():
             u = i - LAG_Y
             send_core(u).wait()
-            t = acc_y[u % 2] + rx_c[u].astype(F32)
-            acc_z[u % 4] = t[: 4 * PART]
-            tx_y[u] = t[4 * PART :].astype(BF)
-            send_y(u).start()
-
-        @pl.when((i >= LAG_Z) & (i < UNITS + LAG_Z))
+
+            @pl.when(is_early(u))
+            def _():
+                acc_e[u // EVERY] = acc_y[u % 2] + rx_c[u].astype(F32)
+
+            @pl.when(jnp.logical_not(is_early(u)))
+            def _():
+                tx_y[u % RING] = (acc_y[u % 2, 4 * PART :] + rx_c[u, 4 * PART :].astype(F32)).astype(BF)
+                send_y(u).start()
+                acc_z[u % RING] = acc_y[u % 2, : 4 * PART] + rx_c[u, : 4 * PART].astype(F32)
+
+        @pl.when(valid(i - LAG_Z) & jnp.logical_not(is_early(i - LAG_Z)))
         def _():
             u = i - LAG_Z
             send_y(u).wait()
-            t = acc_z[u % 4] + rx_y[u].astype(F32)
-            acc_o[u % 4] = t[:PART]
-            for k in range(3):
-                tx_z[u, k] = t[PART * (k + 1) : PART * (k + 2)].astype(BF)
-                send_z(u, k).start()
-
-        @pl.when(i >= LAG_OUT)
+            acc_z[u % RING] = acc_z[u % RING] + rx_y[u].astype(F32)
+
+        def quarter(u):
+            return lambda d: acc_z[u % RING, d * PART : (d + 1) * PART]
+
+        def early_quarter(u, h):
+            return lambda d: acc_e[u, (4 * h + d) * PART : (4 * h + d + 1) * PART]
+
+        u_up = i - LAG_Z - z * HOP
+
+        @pl.when(valid(u_up) & jnp.logical_not(is_early(u_up)))
+        def _():
+            climb(quarter(u_up), tx_up.at[u_up % RING], rx_up.at[u_up], functools.partial(send_up, u_up))
+
+        @pl.when(valid(u_up) & is_early(u_up))
+        def _():
+            e = u_up // EVERY
+            for h in range(2):
+                climb(early_quarter(e, h), tx_eu.at[e, h], rx_eu.at[e, h], functools.partial(early_up, e, h))
+
+        u_dn = i - LAG_Z - (3 - z) * HOP
+
+        @pl.when(valid(u_dn) & jnp.logical_not(is_early(u_dn)))
+        def _():
+            sink(quarter(u_dn), tx_dn.at[u_dn % RING], rx_dn.at[u_dn], functools.partial(send_dn, u_dn))
+
+        @pl.when(valid(u_dn) & is_early(u_dn))
+        def _():
+            e = u_dn // EVERY
+            for h in range(2):
+                sink(early_quarter(e, h), tx_ed.at[e, h], rx_ed.at[e, h], functools.partial(early_dn, e, h))
+
+        own = pl.ds(pl.multiple_of(z * PART, PART), PART)
+
+        def put(u, t):
+            def lanes(n):
+                return pl.ds(pl.multiple_of(n * COLS, COLS), COLS)
+
+            @pl.when(u < 12)
+            def _():
+                up_out[:, lanes(u)] = t
+
+            @pl.when((u >= 12) & (u < 15))
+            def _():
+                out_out[:, lanes(u - 12)] = t
+
+            @pl.when((u >= 15) & (u < FIRST_DOWN))
+            def _():
+                qkv_out[:, lanes(u - 15)] = t
+
+            @pl.when(u >= FIRST_DOWN)
+            def _():
+                rows = pl.ds(pl.multiple_of(u % 4 * PART, PART), PART)
+                down_out[rows, lanes((u - FIRST_DOWN) // 4)] = t
+
+        @pl.when(valid(i - LAG_OUT) & is_early(i - LAG_OUT))
+        def _():
+            e = (i - LAG_OUT) // EVERY
+            for h in range(2):
+                rows = pl.ds(pl.multiple_of((4 * h + z) * PART, PART), PART)
+                t = settle(
+                    acc_e[e, rows, :], rx_eu.at[e, h], rx_ed.at[e, h],
+                    functools.partial(early_up, e, h), functools.partial(early_dn, e, h),
+                )
+                if h == 0:
+                    acc_l[e] = t
+                else:
+                    tx_l[e] = t.astype(BF)
+                    send_last(e).start()
+
+        @pl.when(valid(i - LAG_OUT - LAG_LAST) & is_early(i - LAG_OUT - LAG_LAST))
+        def _():
+            u = i - LAG_OUT - LAG_LAST
+            e = u // EVERY
+            send_last(e).wait()
+            put(u, acc_l[e] + rx_l[e].astype(F32))
+
+        @pl.when(valid(i - LAG_OUT) & jnp.logical_not(is_early(i - LAG_OUT)))
         def _():
             u = i - LAG_OUT
-            t = acc_o[u % 4]
-            for k in range(3):
-                send_z(u, k).wait()
-                t = t + rx_z[u, k].astype(F32)
-
-            def lanes(n):
-                return pl.ds(aligned(n * COLS, COLS), COLS)
-
-            @pl.when(u < 12)
-            def _():
-                up_out[:, lanes(u)] = t
-
-            @pl.when((u >= 12) & (u < 15))
-            def _():
-                out_out[:, lanes(u - 12)] = t
-
-            @pl.when((u >= 15) & (u < 24))
-            def _():
-                qkv_out[:, lanes(u - 15)] = t
-
-            @pl.when(u >= 24)
-            def _():
-                down_out[pl.ds(aligned((u - 24) // 3 * PART, PART), PART), lanes(u % 3)] = t
-
-        @pl.when(i < 12)
-        def _():
-            prepare(i + 2)
+            put(u, settle(
+                acc_z[u % RING, own, :], rx_up.at[u], rx_dn.at[u],
+                functools.partial(send_up, u), functools.partial(send_dn, u),
+            ))
 
         @pl.when(i == 3)
         def _():
@@ -684,12 +885,10 @@
             for copy in vec_along_z:
                 copy.wait()
             vec_out[...] = (vec_z[0] + vec_z[1]) + (vec_z[2] + vec_z[3])
-            vec_beside.start()
 
         return carry
 
     lax.fori_loop(0, UNITS + LAG_OUT, step, 0)
-    vec_beside.wait()
 
     def total(value):
         return jnp.sum(jnp.sum(value, axis=1, keepdims=True), axis=0, keepdims=True)
@@ -699,7 +898,7 @@
     shares = counts * (1.0 / tokens)
     entropy = -total(shares * jnp.log(jnp.where(counts > 0, shares, 1.0)))
     used = total((counts > 0).astype(F32))
-    loss = total(vec_out[V_LOSS : V_LOSS + 1, :D]) + total(side[V_LOSS - 8 : V_LOSS - 7, :D])
+    loss = total(vec_out[V_LOSS : V_LOSS + 1, :D]) + total(vec_out[V_SIDE : V_SIDE + 1, :D])
     lane = lax.broadcasted_iota(jnp.int32, (8, 128), 1)
     last = jnp.where(lane == 1, used / vocab, jnp.exp(entropy) / vocab)
     stats_out[...] = jnp.where(lane == 0, loss / (tokens * D), last)
@@ -709,6 +908,8 @@
 def reduce_weights(l, d, vec, vocab):
     dma = pltpu.SemaphoreType.DMA
     vm = pltpu.VMEM
+    rows = l.shape[0]
+    sums = (V_ROWS, V_COLS)
     return pl.pallas_call(
         functools.partial(reduce_kernel, vocab),
         out_shape=[
@@ -716,26 +917,88 @@
             jax.ShapeDtypeStruct((PART, D), F32),
             jax.ShapeDtypeStruct((PART, FF), F32),
             jax.ShapeDtypeStruct((4 * PART, D), F32),
-            jax.ShapeDtypeStruct((V_ROWS, V_COLS), F32),
+            jax.ShapeDtypeStruct(sums, F32),
             jax.ShapeDtypeStruct((1, V_COLS - D), jnp.int32),
             jax.ShapeDtypeStruct((8, 128), F32),
         ],
         in_specs=[pl.BlockSpec(memory_space=pl.ANY)] * 2 + [pl.BlockSpec(memory_space=pltpu.VMEM)],
         out_specs=[pl.BlockSpec(memory_space=pltpu.VMEM)] * 7,
         scratch_shapes=[
-            vm((7, D, 4 * SEQ), BF), vm((2, 4 * SEQ, PIECE), BF), vm((2, 4 * SEQ, COLS), BF),
-            vm((2, 8 * PART, COLS), F32), vm((4, 4 * PART, COLS), F32), vm((4, PART, COLS), F32),
-            vm((UNITS, 8 * PART, COLS), BF), vm((UNITS, 8 * PART, COLS), BF),
-            vm((UNITS, 4 * PART, COLS), BF), vm((UNITS, 4 * PART, COLS), BF),
-            vm((UNITS, 3, PART, COLS), BF), vm((UNITS, 3, PART, COLS), BF),
-            vm((V_ROWS, V_COLS), F32), vm((V_ROWS, V_COLS), F32), vm((V_ROWS, V_COLS), F32), vm((4, V_ROWS, V_COLS), F32),
-            vm((8, V_COLS), F32),
-            dma((2,)), dma((2,)), dma((UNITS,)), dma((UNITS,)), dma((UNITS,)), dma((UNITS,)),
-            dma((UNITS, 3)), dma((UNITS, 3)), dma((6,)), dma((6,)),
+            vm((7, rows, D), BF), vm((2, rows, COLS), BF), vm((4 * D, COLS), F32),
+            vm((2, 8 * PART, COLS), F32), vm((RING, 4 * PART, COLS), F32),
+            vm((2, 8 * PART, COLS), BF), vm((UNITS, 8 * PART, COLS), BF),
+            vm((RING, 4 * PART, COLS), BF), vm((UNITS, 4 * PART, COLS), BF),
+            vm((RING, 3, PART, COLS), BF), vm((UNITS, 3, PART, COLS), BF),
+            vm((RING, 3, PART, COLS), BF), vm((UNITS, 3, PART, COLS), BF),
+            vm((EARLY, 8 * PART, COLS), F32), vm((EARLY, 2, 3, PART, COLS), BF), vm((EARLY, 2, 3, PART, COLS), BF),
+            vm((EARLY, 2, 3, PART, COLS), BF), vm((EARLY, 2, 3, PART, COLS), BF),
+            vm((EARLY, PART, COLS), F32), vm((EARLY, PART, COLS), BF), vm((EARLY, PART, COLS), BF),
+            vm(sums, F32), vm(sums, F32), vm(sums, F32), vm((4,) + sums, F32),
+            dma((7,)), dma((2,)), dma((2,)), dma((UNITS,)), dma((RING,)), dma((UNITS,)),
+            dma((RING, 3)), dma((UNITS, 3)), dma((RING, 3)), dma((UNITS, 3)),
+            dma((EARLY, 2, 3)), dma((EARLY, 2, 3)), dma((EARLY, 2, 3)), dma((EARLY, 2, 3)), dma((EARLY,)), dma((EARLY,)),
+            dma((5,)), dma((5,)),
         ],
         compiler_params=pltpu.CompilerParams(collective_id=1, has_side_effects=True, vmem_limit_bytes=VMEM_BYTES),
         name="weight_grad_reduce",
     )(l, d, vec)
+
+
+def finish(result, dh, g_qkv, g_out, g_up, g_down, vec):
+    rows = result.shape[0]
+    pieces = 4
+
+    def body(result_ref, dh_ref, qkv_ref, out_ref, up_ref, down_ref, vec_ref,
+             result_to, dh_to, gains_to, shifts_to, qkv_to, out_to, out_bias_to, up_to, up_bias_to, down_to, down_bias_to, *scratch):
+        *bufs, into, outof = scratch
+        copies = []
+        for src, dst in ((dh_ref, dh_to), (result_ref, result_to)):
+            for i in range(pieces):
+                part = pl.ds(i * rows // pieces, rows // pieces)
+                copies.append((src.at[part], dst.at[0, part]))
+        copies += [(qkv_ref, qkv_to.at[0]), (out_ref, out_to.at[0]), (up_ref, up_to.at[0]), (down_ref, down_to.at[0])]
+        loads, saves = [], []
+        for i, (src, dst) in enumerate(copies):
+            buf = bufs[i // pieces].at[i % pieces] if i < 2 * pieces else bufs[i - 2 * pieces + 2]
+            loads.append(pltpu.make_async_copy(src, buf, into.at[i]))
+            saves.append(pltpu.make_async_copy(buf, dst, outof.at[i]))
+        for load in loads:
+            load.start()
+        for load, save in zip(loads, saves):
+            load.wait()
+            save.start()
+        gains_to[0] = vec_ref[0:2, :D]
+        shifts_to[0] = vec_ref[2:4, :D]
+        out_bias_to[...] = vec_ref[4:5, :D]
+        for j in range(FF // D):
+            up_bias_to[:, j * D : (j + 1) * D] = vec_ref[5 + j : 6 + j, :D]
+        down_bias_to[...] = vec_ref[9:10, :D]
+        for save in saves:
+            save.wait()
+
+    inside, outside = pl.BlockSpec(memory_space=pltpu.VMEM), pl.BlockSpec(memory_space=pl.ANY)
+
+    def shape(*dims, dtype=F32):
+        return jax.ShapeDtypeStruct((1,) + dims, dtype)
+
+    out = pl.pallas_call(
+        body,
+        out_shape=[
+            shape(rows, D, dtype=BF), shape(rows, D), shape(2, D), shape(2, D), shape(PART, QKV), shape(PART, D),
+            shape(D), shape(PART, FF), shape(FF), shape(4 * PART, D), shape(D),
+        ],
+        in_specs=[outside] * 6 + [inside],
+        out_specs=[outside, outside, inside, inside, outside, outside, inside, outside, inside, outside, inside],
+        scratch_shapes=[
+            pltpu.VMEM((pieces, rows // pieces, D), F32), pltpu.VMEM((pieces, rows // pieces, D), BF),
+            pltpu.VMEM((PART, QKV), F32), pltpu.VMEM((PART, D), F32), pltpu.VMEM((PART, FF), F32),
+            pltpu.VMEM((4 * PART, D), F32),
+            pltpu.SemaphoreType.DMA((2 * pieces + 4,)), pltpu.SemaphoreType.DMA((2 * pieces + 4,)),
+        ],
+        compiler_params=pltpu.CompilerParams(vmem_limit_bytes=VMEM_BYTES),
+        name="place_outputs",
+    )(result, dh, g_qkv, g_out, g_up, g_down, vec)
+    return tuple(out)
 
 
 def count_shares(counts, total_count):
@@ -764,8 +1027,7 @@
     if small:
         result_bf, dh, l, d, vec = run_blocks(patches, targets, code_ids, codebook, weights)
         g_qkv, g_out, g_up, g_down, vec, hist, stats = reduce_weights(l, d, vec, vocab_all)
-        hist_local = hist[0, :vocab_local]
-        stats = stats[0, :3]
+        return finish(result_bf, dh, g_qkv, g_out, g_up, g_down, vec) + (hist[0, :vocab_local], stats[0, :3])
     else:
         shard_rows = lax.all_gather(codebook, "dp", axis=0, tiled=True)
         chosen = jnp.take(shard_rows, jnp.clip(code_ids, 0, vocab_all - 1), axis=0)
@@ -778,7 +1040,9 @@
         for moment in range(images + 1):
             which = jnp.clip(moment - 1 + section, 0, images - 1).astype(jnp.int32)[None]
             active = jnp.where(leading, moment >= 1, moment < images).astype(F32)
-            flags = jnp.stack([jnp.where(leading, COMMIT_WEIGHT, 1.0).astype(F32), active])
+            flags = jnp.stack(
+                [jnp.where(leading, COMMIT_WEIGHT, 1.0).astype(F32), active, jnp.where(leading, 1.0, 0.0).astype(F32)]
+            )
             d, dh, vec, outgoing = block_backward(
                 which, flags, result, other, arrived, x, weights, qkv, pt, slope, h1, vec, d, dh
             )

time: 242 us -> 224 us (0.926)
  local copies, waits for them, and re-layouts: 11.9 us -> 1.75 us
  Pallas kernels: 229 us -> 221 us
    pallas_call x1, Pallas kernels: 109 us -> 95.2 us  [reduce_weights(): pl.pallas_call(functools.partial(reduce_kernel, vocab), out_shape=[jax.Sh...]
    unnamed x23 -> x3, local copies, waits for them, and re-layouts: 7.87 us -> 0.57 us
    pallas_call x0 -> x1, Pallas kernels: none -> 7.19 us  [finish(): pl.pallas_call(body, out_shape=[shape(rows, D, dtype=BF), shape(rows, D),...]
where the time goes in v3:
time: 224 us; the launch traced here: 223 us
  Pallas kernels  221 us (99%)
    pallas_call x1, Pallas kernels, run_blocks(): pl.pallas_call(blocks_kernel, out_shape=[jax.ShapeDtypeStruct((rows, D),...  118 us
    pallas_call x1, Pallas kernels, reduce_weights(): pl.pallas_call(functools.partial(reduce_kernel, vocab), out_shape=[jax.Sh...  95.2 us
    pallas_call x1, Pallas kernels, finish(): pl.pallas_call(body, out_shape=[shape(rows, D, dtype=BF), shape(rows, D),...  7.19 us

profile of v3, /device:TPU:0, one launch (start us, length us, event | category | flops | bytes accessed | tf_op | source)
XLA Modules:
  0.0 223.3 jit_solution(13655448064682566441)
XLA Ops:
  0.7 118.4 %blocks.1 = (bf16[1024,768]{1,0:T(8,128)(2,1)}, f32[1024,768]{1,0:T(8,128)}, bf16[1024,5376]{1,0:T(8,128)(2,1)}, bf16[1024,6912]{1,0:T(8,128)(2,1)}, f32[16,1024]{1,0:T(8,128)}) custom-call(bf16[4,256,768]{2,1,0:T(8,128)(2,1)} %bitcast.16, bf16[4,256,768]{2,1,0:T(8,128)(2,1)} %bitcast.17, s32[1,1024]{1,0:T(1,128)} %bitcast.21, ...), custom_call_target="tpu_custom_call" | custom-call | tf_op jit(solution)/shard_map/blocks/pallas_call | solution.py:572
  119.1 95.2 %weight_grad_reduce.1 = (f32[48,2304]{1,0:T(8,128)}, f32[48,768]{1,0:T(8,128)}, f32[48,3072]{1,0:T(8,128)}, f32[192,768]{1,0:T(8,128)}, f32[16,1024]{1,0:T(8,128)}, /*index=5*/s32[1,256]{1,0:T(1,128)}, f32[8,128]{1,0:T(8,128)}) custom-call(bf16[1024,5376]{1,0:T(8,128)(2,1)} %get-tuple-element.38.l_ref, bf16[1024,6912]{1,0:T(8,128)(2,1)} %get-tuple-element.39.d_ref, ...), custom_call_target="tpu_custom_call" | custom-call | tf_op jit(solution)/shard_map/weight_grad_reduce/pallas_call | solution.py:913
  214.3 0.0 copy-start
  214.3 7.2 %place_outputs.1 = (bf16[1,1024,768]{2,1,0:T(8,128)(2,1)}, f32[1,1024,768]{2,1,0:T(8,128)}, f32[1,2,768]{2,1,0:T(2,128)}, f32[1,2,768]{2,1,0:T(2,128)}, f32[1,48...) custom-call(bf16[1024,768]{1,0:T(8,128)(2,1)} %get-tuple-element.36., ...), custom_call_target="tpu_custom_call" | custom-call | tf_op jit(solution)/shard_map/place_outputs/pallas_call | solution.py:984
  221.5 1.2 slice_bitcast_fusion
  222.7 0.0 copy-done
  222.7 0.6 copy.27
Async XLA Ops:
  214.3 8.4 %copy-start = (s32[1,256]{1,0:T(1,128)S(1)}, s32[1,256]{1,0:T(1,128)}, u32[]{:S(2)}) copy-start(s32[1,256]{1,0:T(1,128)} %get-tuple-element.57) | copy-start | bytes 3076

commit v4 on v3

--- a/solution.py
+++ b/solution.py
@@ -86,10 +86,10 @@
     for head in range(HEADS):
         st = scores[head]
         e = jnp.exp2((st - jnp.max(st, axis=0, keepdims=True)) * (HEAD_SCALE * LOG2_E))
-        pt_ref[head] = (e * (1.0 / column_sum(e))).astype(BF)
+        pt_ref[head] = e * (1.0 / column_sum(e))
     for head in range(HEADS):
         span = slice(head * HD, (head + 1) * HD)
-        ot_ref[span, :] = matmul_nn(vt_ref[span, :], pt_ref[head]).astype(BF)
+        ot_ref[span, :] = matmul_nn(vt_ref[span, :], pt_ref[head].astype(BF)).astype(BF)
     o = ot_ref[...].T
     l_ref[:, L_O:L_A] = o
     h1 = h + matmul_nn(o, w_out[...]) + out_bias[...]
@@ -105,7 +105,7 @@
         m = (u * half_curve).astype(BF)
         l_ref[:, L_M + j * FF_PIECE : L_M + (j + 1) * FF_PIECE] = m
         slope = half_curve + u * jnp.exp(-0.5 * u * u) * INV_ROOT_TAU
-        slope_ref[:, span] = slope.astype(slope_ref.dtype)
+        slope_ref[:, span] = slope
         result = result + matmul_nn(m, w_down[span, :])
     out_ref[...] = result
     outb_ref[...] = result.astype(BF)
@@ -128,7 +128,7 @@
     db = jnp.zeros((SEQ, D), F32)
     for j in range(FF // FF_PIECE):
         span = slice(j * FF_PIECE, (j + 1) * FF_PIECE)
-        du = (matmul_nt(gb, w_down[span, :]) * slope_ref[:, span].astype(F32)).astype(BF)
+        du = (matmul_nt(gb, w_down[span, :]) * slope_ref[:, span]).astype(BF)
         d_ref[:, span] = du
         add(5 + j, du.astype(F32))
         db = db + matmul_nt(du, w_up[:, span])
@@ -156,11 +156,11 @@
 
     base = D_QKV + D
     for pair in range(HEADS // 2):
-        dv = both([pt_ref[head] for head in range(HEADS)], pair, do_pair)
+        dv = both([pt_ref[head].astype(BF) for head in range(HEADS)], pair, do_pair)
         d_ref[:, base + D + pair * 128 : base + D + (pair + 1) * 128] = dv.astype(BF)
     dsts = []
     for head in range(HEADS):
-        ptf = pt_ref[head].astype(F32)
+        ptf = pt_ref[head]
         dsts.append((ptf * (dpts[head] - column_sum(dpts[head] * ptf))).astype(BF))
     for pair in range(HEADS // 2):
         dk = both(dsts, pair, lambda head: head_pair(qkv_ref, 0, head))
@@ -217,8 +217,8 @@
         out_shape=[
             shape(L_ALL, BF),
             shape(QKV, BF),
-            jax.ShapeDtypeStruct((images * HEADS, SEQ, SEQ), BF),
-            shape(FF, BF),
+            jax.ShapeDtypeStruct((images * HEADS, SEQ, SEQ), F32),
+            shape(FF, F32),
             shape(D, F32),
             shape(D, F32),
             shape(D, BF),
@@ -584,7 +584,7 @@
             vm((D, QKV), BF), vm((D, D), BF), vm((D, FF), BF), vm((FF, D), BF),
             vm((16, SLICES, SHARD, SLICE), BF), vm((rows, 128), jnp.int32),
             vm((2, IMAGES, SEQ, D), BF), vm((IMAGES, SEQ, D), BF), vm((8, D), F32), vm((8, D), F32),
-            vm((2, SEQ, QKV), BF), vm((2, HEADS, SEQ, SEQ), BF), vm((2, SEQ, FF), BF), vm((2, SEQ, D), F32),
+            vm((2, SEQ, QKV), BF), vm((2, HEADS, SEQ, SEQ), F32), vm((2, SEQ, FF), F32), vm((2, SEQ, D), F32),
             vm((2, SEQ, D), F32), vm((SEQ, L_ALL), BF), vm((SEQ, D_ALL), BF), vm((SEQ, D), BF), vm((SEQ, D), F32),
             vm((D, SEQ), BF), vm((D, SEQ), BF),
             dma((4,)), dma(()), dma((4,)), dma((8, SLICES)), dma((5, SLICES)),
@@ -599,19 +599,19 @@
 UNITS = 36
 PART = D // 16
 COLS = 256
-LAG_Y, LAG_Z, HOP = 1, 4, 3
+LAG_Y, LAG_Z, HOP = 1, 4, 4
 LAG_OUT = LAG_Z + 3 * HOP
 BLOCKS = D_ALL // COLS
 FIRST_DOWN = 24
-EVERY, EARLY = 6, UNITS // 6
+EVERY, EARLY = 9, UNITS // 9
 LAG_LAST = 3
-RING = 16
+RING = 20
 
 
 def reduce_kernel(
     vocab, l_ref, d_ref, vec_ref, qkv_out, out_out, up_out, down_out, vec_out, hist_out, stats_out,
     left, right, product, acc_y, acc_z, tx_c, rx_c, tx_y, rx_y, tx_up, rx_up, tx_dn, rx_dn,
-    acc_e, tx_eu, rx_eu, tx_ed, rx_ed, acc_l, tx_l, rx_l, vec_tx, vec_c, vec_y, vec_z,
+    acc_e, tx_eu, rx_eu, tx_ed, rx_ed, tx_l, rx_l, vec_tx, vec_c, vec_y, vec_z,
     lsem, dsem, sc, rc, sy, ry, s_up, r_up, s_dn, r_dn,
     s_eu, r_eu, s_ed, r_ed, s_l, r_l, sv, rv,
 ):
@@ -645,17 +645,13 @@
     def send_y(u):
         return remote(tx_y.at[u % RING], rx_y.at[u], sy.at[u % RING], ry.at[u], along_y)
 
-    def send_up(u, d):
-        return remote(tx_up.at[u % RING, d], rx_up.at[u, d], s_up.at[u % RING, d], r_up.at[u, d], above)
-
-    def send_dn(u, d):
-        return remote(tx_dn.at[u % RING, d], rx_dn.at[u, d], s_dn.at[u % RING, d], r_dn.at[u, d], below)
-
-    def early_up(u, h, d):
-        return remote(tx_eu.at[u, h, d], rx_eu.at[u, h, d], s_eu.at[u, h, d], r_eu.at[u, h, d], above)
-
-    def early_dn(u, h, d):
-        return remote(tx_ed.at[u, h, d], rx_ed.at[u, h, d], s_ed.at[u, h, d], r_ed.at[u, h, d], below)
+    def up_link(at, high, tx, rx, send, recv):
+        rows = slice(at * high, 3 * high)
+        return remote(tx.at[rows], rx.at[rows], send, recv, above)
+
+    def dn_link(at, high, tx, rx, send, recv):
+        rows = slice(0, at * high)
+        return remote(tx.at[rows], rx.at[rows], send, recv, below)
 
     def send_last(u):
         return remote(tx_l.at[u], rx_l.at[u], s_l.at[u], r_l.at[u], along_y)
@@ -666,46 +662,59 @@
     def valid(u):
         return (u >= 0) & (u < UNITS)
 
-    def climb(quarter, tx, rx, send):
-        for d in range(3):
-
-            @pl.when((z > 0) & (d + 1 >= z))
-            def _():
-                send(d).wait_recv()
-
-            @pl.when(d + 1 > z)
-            def _():
-                got = jnp.where(z > 0, rx[d].astype(F32), 0.0)
-                tx[d] = (quarter(d + 1) + got).astype(BF)
-                send(d).start()
-
-    def sink(quarter, tx, rx, send):
-        for d in range(3):
-
-            @pl.when((z < 3) & (d <= z))
-            def _():
-                send(d).wait_recv()
-
-            @pl.when(d < z)
-            def _():
-                got = jnp.where(z < 3, rx[d].astype(F32), 0.0)
-                tx[d] = (quarter(d) + got).astype(BF)
-                send(d).start()
-
-    def settle(quarter_own, rx_above, rx_below, up, dn):
-        for d in range(3):
-
-            @pl.when(d + 1 > z)
-            def _():
-                up(d).wait_send()
-
-            @pl.when(d < z)
-            def _():
-                dn(d).wait_send()
-
-        from_below = jnp.where(z > 0, rx_above[jnp.maximum(z - 1, 0)].astype(F32), 0.0)
-        from_above = jnp.where(z < 3, rx_below[jnp.minimum(z, 2)].astype(F32), 0.0)
-        return quarter_own + from_below + from_above
+    def climb(high, acc, tx, rx, send, recv):
+        for at in range(4):
+
+            @pl.when(z == at)
+            def _():
+                if at > 0:
+                    up_link(at - 1, high, tx, rx, send, recv).wait_recv()
+                if at < 3:
+                    t = acc[(at + 1) * high : 4 * high]
+                    if at > 0:
+                        t = t + rx[at * high : 3 * high].astype(F32)
+                    tx[at * high : 3 * high] = t.astype(BF)
+                    up_link(at, high, tx, rx, send, recv).start()
+
+    def sink(high, acc, tx, rx, send, recv):
+        for at in range(4):
+
+            @pl.when(z == at)
+            def _():
+                if at < 3:
+                    dn_link(at + 1, high, tx, rx, send, recv).wait_recv()
+                if at > 0:
+                    t = acc[: at * high]
+                    if at < 3:
+                        t = t + rx[: at * high].astype(F32)
+                    tx[: at * high] = t.astype(BF)
+                    dn_link(at, high, tx, rx, send, recv).start()
+
+    def settle(high, acc, up, dn):
+        for at in range(4):
+
+            @pl.when(z == at)
+            def _():
+                t = acc[at * high : (at + 1) * high]
+                if at < 3:
+                    up_link(at, high, *up).wait_send()
+                    t = t + dn[1][at * high : (at + 1) * high].astype(F32)
+                if at > 0:
+                    dn_link(at, high, *dn).wait_send()
+                    t = t + up[1][(at - 1) * high : at * high].astype(F32)
+                acc[at * high : (at + 1) * high] = t
+
+    def up_args(u):
+        return tx_up.at[u % RING], rx_up.at[u], s_up.at[u % RING], r_up.at[u]
+
+    def dn_args(u):
+        return tx_dn.at[u % RING], rx_dn.at[u], s_dn.at[u % RING], r_dn.at[u]
+
+    def early_up(e):
+        return tx_eu.at[e], rx_eu.at[e], s_eu.at[e], r_eu.at[e]
+
+    def early_dn(e):
+        return tx_ed.at[e], rx_ed.at[e], s_ed.at[e], r_ed.at[e]
 
     vec_core = remote(vec_ref, vec_c, sv.at[0], rv.at[0], across)
     vec_along_y = remote(vec_tx, vec_y, sv.at[1], rv.at[1], along_y)
@@ -770,7 +779,10 @@
 
             @pl.when(is_early(u))
             def _():
-                acc_e[u // EVERY] = acc_y[u % 2] + rx_c[u].astype(F32)
+                t = acc_y[u % 2] + rx_c[u].astype(F32)
+                for place in range(8):
+                    to = (2 * (place % 4) + place // 4) * PART
+                    acc_e[u // EVERY, to : to + PART] = t[place * PART : (place + 1) * PART]
 
             @pl.when(jnp.logical_not(is_early(u)))
             def _():
@@ -784,37 +796,25 @@
             send_y(u).wait()
             acc_z[u % RING] = acc_z[u % RING] + rx_y[u].astype(F32)
 
-        def quarter(u):
-            return lambda d: acc_z[u % RING, d * PART : (d + 1) * PART]
-
-        def early_quarter(u, h):
-            return lambda d: acc_e[u, (4 * h + d) * PART : (4 * h + d + 1) * PART]
-
         u_up = i - LAG_Z - z * HOP
 
         @pl.when(valid(u_up) & jnp.logical_not(is_early(u_up)))
         def _():
-            climb(quarter(u_up), tx_up.at[u_up % RING], rx_up.at[u_up], functools.partial(send_up, u_up))
+            climb(PART, acc_z.at[u_up % RING], *up_args(u_up))
 
         @pl.when(valid(u_up) & is_early(u_up))
         def _():
-            e = u_up // EVERY
-            for h in range(2):
-                climb(early_quarter(e, h), tx_eu.at[e, h], rx_eu.at[e, h], functools.partial(early_up, e, h))
+            climb(2 * PART, acc_e.at[u_up // EVERY], *early_up(u_up // EVERY))
 
         u_dn = i - LAG_Z - (3 - z) * HOP
 
         @pl.when(valid(u_dn) & jnp.logical_not(is_early(u_dn)))
         def _():
-            sink(quarter(u_dn), tx_dn.at[u_dn % RING], rx_dn.at[u_dn], functools.partial(send_dn, u_dn))
+            sink(PART, acc_z.at[u_dn % RING], *dn_args(u_dn))
 
         @pl.when(valid(u_dn) & is_early(u_dn))
         def _():
-            e = u_dn // EVERY
-            for h in range(2):
-                sink(early_quarter(e, h), tx_ed.at[e, h], rx_ed.at[e, h], functools.partial(early_dn, e, h))
-
-        own = pl.ds(pl.multiple_of(z * PART, PART), PART)
+            sink(2 * PART, acc_e.at[u_dn // EVERY], *early_dn(u_dn // EVERY))
 
         def put(u, t):
             def lanes(n):
@@ -840,32 +840,24 @@
         @pl.when(valid(i - LAG_OUT) & is_early(i - LAG_OUT))
         def _():
             e = (i - LAG_OUT) // EVERY
-            for h in range(2):
-                rows = pl.ds(pl.multiple_of((4 * h + z) * PART, PART), PART)
-                t = settle(
-                    acc_e[e, rows, :], rx_eu.at[e, h], rx_ed.at[e, h],
-                    functools.partial(early_up, e, h), functools.partial(early_dn, e, h),
-                )
-                if h == 0:
-                    acc_l[e] = t
-                else:
-                    tx_l[e] = t.astype(BF)
-                    send_last(e).start()
+            settle(2 * PART, acc_e.at[e], early_up(e), early_dn(e))
+            rows = pl.ds(pl.multiple_of((2 * z + 1) * PART, PART), PART)
+            tx_l[e] = acc_e[e, rows, :].astype(BF)
+            send_last(e).start()
 
         @pl.when(valid(i - LAG_OUT - LAG_LAST) & is_early(i - LAG_OUT - LAG_LAST))
         def _():
             u = i - LAG_OUT - LAG_LAST
             e = u // EVERY
             send_last(e).wait()
-            put(u, acc_l[e] + rx_l[e].astype(F32))
+            rows = pl.ds(pl.multiple_of(2 * z * PART, PART), PART)
+            put(u, acc_e[e, rows, :] + rx_l[e].astype(F32))
 
         @pl.when(valid(i - LAG_OUT) & jnp.logical_not(is_early(i - LAG_OUT)))
         def _():
             u = i - LAG_OUT
-            put(u, settle(
-                acc_z[u % RING, own, :], rx_up.at[u], rx_dn.at[u],
-                functools.partial(send_up, u), functools.partial(send_dn, u),
-            ))
+            settle(PART, acc_z.at[u % RING], up_args(u), dn_args(u))
+            put(u, acc_z[u % RING, pl.ds(pl.multiple_of(z * PART, PART), PART), :])
 
         @pl.when(i == 3)
         def _():
@@ -928,15 +920,15 @@
             vm((2, 8 * PART, COLS), F32), vm((RING, 4 * PART, COLS), F32),
             vm((2, 8 * PART, COLS), BF), vm((UNITS, 8 * PART, COLS), BF),
             vm((RING, 4 * PART, COLS), BF), vm((UNITS, 4 * PART, COLS), BF),
-            vm((RING, 3, PART, COLS), BF), vm((UNITS, 3, PART, COLS), BF),
-            vm((RING, 3, PART, COLS), BF), vm((UNITS, 3, PART, COLS), BF),
-            vm((EARLY, 8 * PART, COLS), F32), vm((EARLY, 2, 3, PART, COLS), BF), vm((EARLY, 2, 3, PART, COLS), BF),
-            vm((EARLY, 2, 3, PART, COLS), BF), vm((EARLY, 2, 3, PART, COLS), BF),
-            vm((EARLY, PART, COLS), F32), vm((EARLY, PART, COLS), BF), vm((EARLY, PART, COLS), BF),
+            vm((RING, 3 * PART, COLS), BF), vm((UNITS, 3 * PART, COLS), BF),
+            vm((RING, 3 * PART, COLS), BF), vm((UNITS, 3 * PART, COLS), BF),
+            vm((EARLY, 8 * PART, COLS), F32), vm((EARLY, 6 * PART, COLS), BF), vm((EARLY, 6 * PART, COLS), BF),
+            vm((EARLY, 6 * PART, COLS), BF), vm((EARLY, 6 * PART, COLS), BF),
+            vm((EARLY, PART, COLS), BF), vm((EARLY, PART, COLS), BF),
             vm(sums, F32), vm(sums, F32), vm(sums, F32), vm((4,) + sums, F32),
             dma((7,)), dma((2,)), dma((2,)), dma((UNITS,)), dma((RING,)), dma((UNITS,)),
-            dma((RING, 3)), dma((UNITS, 3)), dma((RING, 3)), dma((UNITS, 3)),
-            dma((EARLY, 2, 3)), dma((EARLY, 2, 3)), dma((EARLY, 2, 3)), dma((EARLY, 2, 3)), dma((EARLY,)), dma((EARLY,)),
+            dma((RING,)), dma((UNITS,)), dma((RING,)), dma((UNITS,)),
+            dma((EARLY,)), dma((EARLY,)), dma((EARLY,)), dma((EARLY,)), dma((EARLY,)), dma((EARLY,)),
             dma((5,)), dma((5,)),
         ],
         compiler_params=pltpu.CompilerParams(collective_id=1, has_side_effects=True, vmem_limit_bytes=VMEM_BYTES),
@@ -944,12 +936,12 @@
     )(l, d, vec)
 
 
-def finish(result, dh, g_qkv, g_out, g_up, g_down, vec):
+def finish(result, dh, g_qkv, g_out, g_up, g_down, vec, hist, stats, shard):
     rows = result.shape[0]
-    pieces = 4
-
-    def body(result_ref, dh_ref, qkv_ref, out_ref, up_ref, down_ref, vec_ref,
-             result_to, dh_to, gains_to, shifts_to, qkv_to, out_to, out_bias_to, up_to, up_bias_to, down_to, down_bias_to, *scratch):
+    pieces = 1
+
+    def body(result_ref, dh_ref, qkv_ref, out_ref, up_ref, down_ref, vec_ref, hist_ref, stats_ref,
+             result_to, dh_to, gains_to, shifts_to, qkv_to, out_to, out_bias_to, up_to, up_bias_to, down_to, down_bias_to, hist_to, stats_to, *scratch):
         *bufs, into, outof = scratch
         copies = []
         for src, dst in ((dh_ref, dh_to), (result_ref, result_to)):
@@ -973,6 +965,8 @@
         for j in range(FF // D):
             up_bias_to[:, j * D : (j + 1) * D] = vec_ref[5 + j : 6 + j, :D]
         down_bias_to[...] = vec_ref[9:10, :D]
+        hist_to[...] = hist_ref[0, :shard]
+        stats_to[...] = stats_ref[0, :3]
         for save in saves:
             save.wait()
 
@@ -986,9 +980,10 @@
         out_shape=[
             shape(rows, D, dtype=BF), shape(rows, D), shape(2, D), shape(2, D), shape(PART, QKV), shape(PART, D),
             shape(D), shape(PART, FF), shape(FF), shape(4 * PART, D), shape(D),
+            jax.ShapeDtypeStruct((shard,), jnp.int32), jax.ShapeDtypeStruct((3,), F32),
         ],
-        in_specs=[outside] * 6 + [inside],
-        out_specs=[outside, outside, inside, inside, outside, outside, inside, outside, inside, outside, inside],
+        in_specs=[outside] * 6 + [inside] * 3,
+        out_specs=[outside, outside, inside, inside, outside, outside, inside, outside, inside, outside, inside, inside, inside],
         scratch_shapes=[
             pltpu.VMEM((pieces, rows // pieces, D), F32), pltpu.VMEM((pieces, rows // pieces, D), BF),
             pltpu.VMEM((PART, QKV), F32), pltpu.VMEM((PART, D), F32), pltpu.VMEM((PART, FF), F32),
@@ -997,7 +992,7 @@
         ],
         compiler_params=pltpu.CompilerParams(vmem_limit_bytes=VMEM_BYTES),
         name="place_outputs",
-    )(result, dh, g_qkv, g_out, g_up, g_down, vec)
+    )(result, dh, g_qkv, g_out, g_up, g_down, vec, hist, stats)
     return tuple(out)
 
 
@@ -1027,7 +1022,7 @@
     if small:
         result_bf, dh, l, d, vec = run_blocks(patches, targets, code_ids, codebook, weights)
         g_qkv, g_out, g_up, g_down, vec, hist, stats = reduce_weights(l, d, vec, vocab_all)
-        return finish(result_bf, dh, g_qkv, g_out, g_up, g_down, vec) + (hist[0, :vocab_local], stats[0, :3])
+        return finish(result_bf, dh, g_qkv, g_out, g_up, g_down, vec, hist, stats, vocab_local)
     else:
         shard_rows = lax.all_gather(codebook, "dp", axis=0, tiled=True)
         chosen = jnp.take(shard_rows, jnp.clip(code_ids, 0, vocab_all - 1), axis=0)

time: 224 us -> 216 us (0.964)
  Pallas kernels: 221 us -> 215 us
    pallas_call x1, Pallas kernels: 95.2 us -> 90.6 us  [reduce_weights(): pl.pallas_call(functools.partial(reduce_kernel, vocab), out_shape=[jax.Sh...]
where the time goes in v4:
time: 216 us
  Pallas kernels  215 us (100%)
    pallas_call x1, Pallas kernels, run_blocks(): pl.pallas_call(blocks_kernel, out_shape=[jax.ShapeDtypeStruct((rows, D),...  118 us
    pallas_call x1, Pallas kernels, reduce_weights(): pl.pallas_call(functools.partial(reduce_kernel, vocab), out_shape=[jax.Sh...  90.6 us
    pallas_call x1, Pallas kernels, finish(): pl.pallas_call(body, out_shape=[shape(rows, D, dtype=BF), shape(rows, D),...  6.18 us

profile of v4, /device:TPU:0, one launch (start us, length us, event | category | flops | bytes accessed | tf_op | source)
XLA Modules:
  0.0 216.1 jit_solution(1081970182705049397)
XLA Ops:
  0.6 118.5 %blocks.1 = (bf16[1024,768]{1,0:T(8,128)(2,1)}, f32[1024,768]{1,0:T(8,128)}, bf16[1024,5376]{1,0:T(8,128)(2,1)}, bf16[1024,6912]{1,0:T(8,128)(2,1)}, f32[16,1024]{1,0:T(8,128)}) custom-call(bf16[4,256,768]{2,1,0:T(8,128)(2,1)} %bitcast.12, bf16[4,256,768]{2,1,0:T(8,128)(2,1)} %bitcast.13, s32[1,1024]{1,0:T(1,128)} %bitcast.17, ...), custom_call_target="tpu_custom_call" | custom-call | tf_op jit(solution)/shard_map/blocks/pallas_call | solution.py:572
  119.1 90.6 %weight_grad_reduce.1 = (f32[48,2304]{1,0:T(8,128)}, f32[48,768]{1,0:T(8,128)}, f32[48,3072]{1,0:T(8,128)}, f32[192,768]{1,0:T(8,128)}, f32[16,1024]{1,0:T(8,128)}, /*index=5*/s32[1,256]{1,0:T(1,128)}, f32[8,128]{1,0:T(8,128)}) custom-call(bf16[1024,5376]{1,0:T(8,128)(2,1)} %get-tuple-element.27.l_ref, bf16[1024,6912]{1,0:T(8,128)(2,1)} %get-tuple-element.28.d_ref, ...), custom_call_target="tpu_custom_call" | custom-call | tf_op jit(solution)/shard_map/weight_grad_reduce/pallas_call | solution.py:905
  209.7 6.2 %place_outputs.1 = (bf16[1,1024,768]{2,1,0:T(8,128)(2,1)}, f32[1,1024,768]{2,1,0:T(8,128)}, f32[1,2,768]{2,1,0:T(2,128)}, f32[1,2,768]{2,1,0:T(2,128)}, f32[1,48...) custom-call(bf16[1024,768]{1,0:T(8,128)(2,1)} %get-tuple-element.25., ...), custom_call_target="tpu_custom_call" | custom-call | tf_op jit(solution)/shard_map/place_outputs/pallas_call | solution.py:978

commit v5 on v4

--- a/solution.py
+++ b/solution.py
@@ -26,7 +26,7 @@
 HEAD_SCALE = HD**-0.5
 MESH = pl.DeviceIdType.MESH
 BF, F32 = jnp.bfloat16, jnp.float32
-VMEM_BYTES = 60 << 20
+VMEM_BYTES, REDUCE_BYTES, PLACE_BYTES = 60 << 20, 48 << 20, 14 << 20
 
 
 def matmul_nn(left, right):
@@ -931,7 +931,7 @@
             dma((EARLY,)), dma((EARLY,)), dma((EARLY,)), dma((EARLY,)), dma((EARLY,)), dma((EARLY,)),
             dma((5,)), dma((5,)),
         ],
-        compiler_params=pltpu.CompilerParams(collective_id=1, has_side_effects=True, vmem_limit_bytes=VMEM_BYTES),
+        compiler_params=pltpu.CompilerParams(collective_id=1, has_side_effects=True, vmem_limit_bytes=REDUCE_BYTES),
         name="weight_grad_reduce",
     )(l, d, vec)
 
@@ -942,22 +942,15 @@
 
     def body(result_ref, dh_ref, qkv_ref, out_ref, up_ref, down_ref, vec_ref, hist_ref, stats_ref,
              result_to, dh_to, gains_to, shifts_to, qkv_to, out_to, out_bias_to, up_to, up_bias_to, down_to, down_bias_to, hist_to, stats_to, *scratch):
-        *bufs, into, outof = scratch
+        (outof,) = scratch
         copies = []
         for src, dst in ((dh_ref, dh_to), (result_ref, result_to)):
             for i in range(pieces):
                 part = pl.ds(i * rows // pieces, rows // pieces)
                 copies.append((src.at[part], dst.at[0, part]))
         copies += [(qkv_ref, qkv_to.at[0]), (out_ref, out_to.at[0]), (up_ref, up_to.at[0]), (down_ref, down_to.at[0])]
-        loads, saves = [], []
-        for i, (src, dst) in enumerate(copies):
-            buf = bufs[i // pieces].at[i % pieces] if i < 2 * pieces else bufs[i - 2 * pieces + 2]
-            loads.append(pltpu.make_async_copy(src, buf, into.at[i]))
-            saves.append(pltpu.make_async_copy(buf, dst, outof.at[i]))
-        for load in loads:
-            load.start()
-        for load, save in zip(loads, saves):
-            load.wait()
+        saves = [pltpu.make_async_copy(src, dst, outof.at[i]) for i, (src, dst) in enumerate(copies)]
+        for save in saves:
             save.start()
         gains_to[0] = vec_ref[0:2, :D]
         shifts_to[0] = vec_ref[2:4, :D]
@@ -985,12 +978,9 @@
         in_specs=[outside] * 6 + [inside] * 3,
         out_specs=[outside, outside, inside, inside, outside, outside, inside, outside, inside, outside, inside, inside, inside],
         scratch_shapes=[
-            pltpu.VMEM((pieces, rows // pieces, D), F32), pltpu.VMEM((pieces, rows // pieces, D), BF),
-            pltpu.VMEM((PART, QKV), F32), pltpu.VMEM((PART, D), F32), pltpu.VMEM((PART, FF), F32),
-            pltpu.VMEM((4 * PART, D), F32),
-            pltpu.SemaphoreType.DMA((2 * pieces + 4,)), pltpu.SemaphoreType.DMA((2 * pieces + 4,)),
+            pltpu.SemaphoreType.DMA((2 * pieces + 4,)),
         ],
-        compiler_params=pltpu.CompilerParams(vmem_limit_bytes=VMEM_BYTES),
+        compiler_params=pltpu.CompilerParams(vmem_limit_bytes=PLACE_BYTES),
         name="place_outputs",
     )(result, dh, g_qkv, g_out, g_up, g_down, vec, hist, stats)
     return tuple(out)

time: 216 us -> 212 us (0.981)
  Pallas kernels: 215 us -> 210 us
    pallas_call x1, Pallas kernels: 6.18 us -> 3.4 us  [finish(): pl.pallas_call(body, out_shape=[shape(rows, D, dtype=BF), shape(rows, D),...]
where the time goes in v5:
time: 212 us
  Pallas kernels  210 us (99%)
    pallas_call x1, Pallas kernels, run_blocks(): pl.pallas_call(blocks_kernel, out_shape=[jax.ShapeDtypeStruct((rows, D),...  119 us
    pallas_call x1, Pallas kernels, reduce_weights(): pl.pallas_call(functools.partial(reduce_kernel, vocab), out_shape=[jax.Sh...  88.6 us

profile of v5, /device:TPU:0, one launch (start us, length us, event | category | flops | bytes accessed | tf_op | source)
XLA Modules:
  0.0 212.2 jit_solution(4939670774273995930)
XLA Ops:
  0.6 118.5 %blocks.1 = (bf16[1024,768]{1,0:T(8,128)(2,1)}, f32[1024,768]{1,0:T(8,128)}, bf16[1024,5376]{1,0:T(8,128)(2,1)}, bf16[1024,6912]{1,0:T(8,128)(2,1)}, f32[16,1024]{1,0:T(8,128)}) custom-call(bf16[4,256,768]{2,1,0:T(8,128)(2,1)} %bitcast.12, bf16[4,256,768]{2,1,0:T(8,128)(2,1)} %bitcast.13, s32[1,1024]{1,0:T(1,128)} %bitcast.17, ...), custom_call_target="tpu_custom_call" | custom-call | tf_op jit(solution)/shard_map/blocks/pallas_call | solution.py:572
  119.2 0.0 copy-start.2
  119.2 0.8 copy-done.2
  120.0 0.0 copy-start
  120.0 0.0 copy-start.1
  120.0 88.6 %weight_grad_reduce.1 = (f32[48,2304]{1,0:T(8,128)S(1)}, f32[48,768]{1,0:T(8,128)S(1)}, f32[48,3072]{1,0:T(8,128)S(1)}, f32[192,768]{1,0:T(8,128)S(1)}, f32[16,1...) custom-call(bf16[1024,5376]{1,0:T(8,128)(2,1)} %get-tuple-element.27.l_ref, ...), custom_call_target="tpu_custom_call" | custom-call | tf_op jit(solution)/shard_map/weight_grad_reduce/pallas_call | solution.py:905
  208.6 0.0 copy-done
  208.6 0.0 copy-done.1
  208.6 3.4 %place_outputs.1 = (bf16[1,1024,768]{2,1,0:T(8,128)(2,1)}, f32[1,1024,768]{2,1,0:T(8,128)}, f32[1,2,768]{2,1,0:T(2,128)}, f32[1,2,768]{2,1,0:T(2,128)}, f32[1,48...) custom-call(bf16[1024,768]{1,0:T(8,128)(2,1)S(1)} %copy-done.1, ...), custom_call_target="tpu_custom_call" | custom-call | tf_op jit(solution)/shard_map/place_outputs/pallas_call | solution.py:971
Async XLA Ops:
  119.2 0.8 copy-start.2
  120.0 88.6 %copy-start = (f32[1024,768]{1,0:T(8,128)S(1)}, f32[1024,768]{1,0:T(8,128)}, u32[]{:S(2)}) copy-start(f32[1024,768]{1,0:T(8,128)} %get-tuple-element.26.dh_ref) | copy-start | bytes 9437188
  120.0 88.6 %copy-start.1 = (bf16[1024,768]{1,0:T(8,128)(2,1)S(1)}, bf16[1024,768]{1,0:T(8,128)(2,1)}, u32[]{:S(2)}) copy-start(bf16[1024,768]{1,0:T(8,128)(2,1)} %get-tuple-element.25.result_ref) | copy-start | bytes 4718596

commit v6 on v5

--- a/solution.py
+++ b/solution.py
@@ -431,36 +431,6 @@
     lax.fori_loop(1, 8, event, 0)
     pick_core(7)
 
-    for p in pieces:
-
-        @pl.when(z < 3)
-        def _():
-            send_z(0, dp, True, p).wait_send()
-
-        @pl.when(z > 0)
-        def _():
-            send_z(1, dp, False, p).wait_send()
-
-        send_y(0, 0, p).wait_send()
-
-        @pl.when(home)
-        def _():
-            for order in (1, 2, 3):
-                send_y(order, number_at(2 * order - 1), p).wait_send()
-            for e in (4, 5, 6, 7):
-                send_x(e - 3, number_at(e), p).wait_send()
-
-        @pl.when(home & jnp.logical_not(corner))
-        def _():
-            for e in (1, 3, 5):
-                pass_on(e, p).wait_send()
-
-        @pl.when(home & corner)
-        def _():
-            send_x(0, number_at(3), p).wait_send()
-
-        for e in range(8):
-            send_core(e, number_at(e), p).wait_send()
     for load in loads:
         load.wait()
 
@@ -557,6 +527,37 @@
     def _():
         for image in range(IMAGES):
             cross(image).wait_send()
+
+    for p in pieces:
+
+        @pl.when(z < 3)
+        def _():
+            send_z(0, dp, True, p).wait_send()
+
+        @pl.when(z > 0)
+        def _():
+            send_z(1, dp, False, p).wait_send()
+
+        send_y(0, 0, p).wait_send()
+
+        @pl.when(home)
+        def _():
+            for order in (1, 2, 3):
+                send_y(order, number_at(2 * order - 1), p).wait_send()
+            for e in (4, 5, 6, 7):
+                send_x(e - 3, number_at(e), p).wait_send()
+
+        @pl.when(home & jnp.logical_not(corner))
+        def _():
+            for e in (1, 3, 5):
+                pass_on(e, p).wait_send()
+
+        @pl.when(home & corner)
+        def _():
+            send_x(0, number_at(3), p).wait_send()
+
+        for e in range(8):
+            send_core(e, number_at(e), p).wait_send()
 
     trade.wait()
     vec_ref[V_LOSS : V_LOSS + 1, :D] = loss_buf[0:1, :]
@@ -609,11 +610,11 @@
 
 
 def reduce_kernel(
-    vocab, l_ref, d_ref, vec_ref, qkv_out, out_out, up_out, down_out, vec_out, hist_out, stats_out,
+    vocab, l_ref, d_ref, vec_from, qkv_out, out_out, up_out, down_out, vec_out, hist_out, stats_out,
     left, right, product, acc_y, acc_z, tx_c, rx_c, tx_y, rx_y, tx_up, rx_up, tx_dn, rx_dn,
-    acc_e, tx_eu, rx_eu, tx_ed, rx_ed, tx_l, rx_l, vec_tx, vec_c, vec_y, vec_z,
+    acc_e, tx_eu, rx_eu, tx_ed, rx_ed, tx_l, rx_l, vec_ref, vec_tx, vec_c, vec_y, vec_z,
     lsem, dsem, sc, rc, sy, ry, s_up, r_up, s_dn, r_dn,
-    s_eu, r_eu, s_ed, r_ed, s_l, r_l, sv, rv,
+    s_eu, r_eu, s_ed, r_ed, s_l, r_l, sv, rv, vec_sem,
 ):
     sec, dp = lax.axis_index("section"), lax.axis_index("dp")
     core, y, z = dp % 2, (dp // 2) % 2, dp // 4
@@ -628,8 +629,10 @@
         cols = pl.ds(pl.multiple_of(n * COLS, COLS), COLS)
         return pltpu.make_async_copy(d_ref.at[:, cols], right.at[n % 2], dsem.at[n % 2])
 
+    vec_load = pltpu.make_async_copy(vec_from, vec_ref, vec_sem)
     lefts[0].start()
     load_right(0).start()
+    vec_load.start()
 
     barrier = pltpu.get_barrier_semaphore()
     for target in [across, along_y] + along_z:
@@ -719,7 +722,6 @@
     vec_core = remote(vec_ref, vec_c, sv.at[0], rv.at[0], across)
     vec_along_y = remote(vec_tx, vec_y, sv.at[1], rv.at[1], along_y)
     vec_along_z = [remote(vec_z.at[z], vec_z.at[z], sv.at[2 + k], rv.at[2 + k], along_z[k]) for k in range(3)]
-    vec_core.start()
 
     def multiply(u):
         down = u >= FIRST_DOWN
@@ -859,7 +861,12 @@
             settle(PART, acc_z.at[u % RING], up_args(u), dn_args(u))
             put(u, acc_z[u % RING, pl.ds(pl.multiple_of(z * PART, PART), PART), :])
 
-        @pl.when(i == 3)
+        @pl.when(i == 1)
+        def _():
+            vec_load.wait()
+            vec_core.start()
+
+        @pl.when(i == 4)
         def _():
             vec_core.wait()
             vec_tx[...] = vec_ref[...] + vec_c[...]
@@ -913,7 +920,7 @@
             jax.ShapeDtypeStruct((1, V_COLS - D), jnp.int32),
             jax.ShapeDtypeStruct((8, 128), F32),
         ],
-        in_specs=[pl.BlockSpec(memory_space=pl.ANY)] * 2 + [pl.BlockSpec(memory_space=pltpu.VMEM)],
+        in_specs=[pl.BlockSpec(memory_space=pl.ANY)] * 3,
         out_specs=[pl.BlockSpec(memory_space=pltpu.VMEM)] * 7,
         scratch_shapes=[
             vm((7, rows, D), BF), vm((2, rows, COLS), BF), vm((4 * D, COLS), F32),
@@ -925,11 +932,11 @@
             vm((EARLY, 8 * PART, COLS), F32), vm((EARLY, 6 * PART, COLS), BF), vm((EARLY, 6 * PART, COLS), BF),
             vm((EARLY, 6 * PART, COLS), BF), vm((EARLY, 6 * PART, COLS), BF),
             vm((EARLY, PART, COLS), BF), vm((EARLY, PART, COLS), BF),
-            vm(sums, F32), vm(sums, F32), vm(sums, F32), vm((4,) + sums, F32),
+            vm(sums, F32), vm(sums, F32), vm(sums, F32), vm(sums, F32), vm((4,) + sums, F32),
             dma((7,)), dma((2,)), dma((2,)), dma((UNITS,)), dma((RING,)), dma((UNITS,)),
             dma((RING,)), dma((UNITS,)), dma((RING,)), dma((UNITS,)),
             dma((EARLY,)), dma((EARLY,)), dma((EARLY,)), dma((EARLY,)), dma((EARLY,)), dma((EARLY,)),
-            dma((5,)), dma((5,)),
+            dma((5,)), dma((5,)), dma(()),
         ],
         compiler_params=pltpu.CompilerParams(collective_id=1, has_side_effects=True, vmem_limit_bytes=REDUCE_BYTES),
         name="weight_grad_reduce",

time: 212 us -> 213 us (level)
  no operation moved by 1% of the time
where the time goes in v6:
time: 213 us
  Pallas kernels  211 us (99%)
    pallas_call x1, Pallas kernels, run_blocks(): pl.pallas_call(blocks_kernel, out_shape=[jax.ShapeDtypeStruct((rows, D),...  119 us
    pallas_call x1, Pallas kernels, reduce_weights(): pl.pallas_call(functools.partial(reduce_kernel, vocab), out_shape=[jax.Sh...  89.5 us

profile of v6, /device:TPU:0, one launch (start us, length us, event | category | flops | bytes accessed | tf_op | source)
XLA Modules:
  0.0 213.2 jit_solution(7602616503248960986)
XLA Ops:
  0.6 118.5 %blocks.1 = (bf16[1024,768]{1,0:T(8,128)(2,1)}, f32[1024,768]{1,0:T(8,128)}, bf16[1024,5376]{1,0:T(8,128)(2,1)}, bf16[1024,6912]{1,0:T(8,128)(2,1)}, f32[16,1024]{1,0:T(8,128)}) custom-call(bf16[4,256,768]{2,1,0:T(8,128)(2,1)} %bitcast.12, bf16[4,256,768]{2,1,0:T(8,128)(2,1)} %bitcast.13, s32[1,1024]{1,0:T(1,128)} %bitcast.17, ...), custom_call_target="tpu_custom_call" | custom-call | tf_op jit(solution)/shard_map/blocks/pallas_call | solution.py:573
  119.2 0.0 copy-start.2
  119.2 0.8 copy-done.2
  120.0 0.0 copy-start
  120.0 0.0 copy-start.1
  120.0 89.5 %weight_grad_reduce.1 = (f32[48,2304]{1,0:T(8,128)S(1)}, f32[48,768]{1,0:T(8,128)S(1)}, f32[48,3072]{1,0:T(8,128)S(1)}, f32[192,768]{1,0:T(8,128)S(1)}, f32[16,1...) custom-call(bf16[1024,5376]{1,0:T(8,128)(2,1)} %get-tuple-element.27.l_ref, ...), custom_call_target="tpu_custom_call" | custom-call | tf_op jit(solution)/shard_map/weight_grad_reduce/pallas_call | solution.py:912
  209.6 0.0 copy-done
  209.6 0.0 copy-done.1
  209.6 3.4 %place_outputs.1 = (bf16[1,1024,768]{2,1,0:T(8,128)(2,1)}, f32[1,1024,768]{2,1,0:T(8,128)}, f32[1,2,768]{2,1,0:T(2,128)}, f32[1,2,768]{2,1,0:T(2,128)}, f32[1,48...) custom-call(bf16[1024,768]{1,0:T(8,128)(2,1)S(1)} %copy-done.1, ...), custom_call_target="tpu_custom_call" | custom-call | tf_op jit(solution)/shard_map/place_outputs/pallas_call | solution.py:978
Async XLA Ops:
  119.2 0.8 copy-start.2
  120.0 89.5 %copy-start = (f32[1024,768]{1,0:T(8,128)S(1)}, f32[1024,768]{1,0:T(8,128)}, u32[]{:S(2)}) copy-start(f32[1024,768]{1,0:T(8,128)} %get-tuple-element.26.dh_ref) | copy-start | bytes 9437188
  120.0 89.6 %copy-start.1 = (bf16[1024,768]{1,0:T(8,128)(2,1)S(1)}, bf16[1024,768]{1,0:T(8,128)(2,1)}, u32[]{:S(2)}) copy-start(bf16[1024,768]{1,0:T(8,128)(2,1)} %get-tuple-element.25.result_ref) | copy-start | bytes 4718596
